TPU v7x, 128 devices: a whole 4x4x4 slice. The times are simulated.
128 devices in a mesh: db: 16 (over y, x), seq: 8 (over z, core).
Axes of the slice: x: 4, y: 4, z: 4, core: 2. Of those that a mesh axis runs over, the one named last changes fastest.
Arguments:
- self_query: bfloat16 [49152, 2048], P(('db', 'seq')), may hold values from -500 to 500
- self_key: bfloat16 [49152, 2048], P(('db', 'seq')), may hold values from -6 to 6
- self_value: bfloat16 [49152, 2048], P(('db', 'seq')), may hold values from -6 to 6
- cross_query: bfloat16 [49152, 2048], P(('db', 'seq')), may hold values from -700 to 700
- retrieval_shard: int32 [768, 2], P(('db', 'seq')), may hold values from 0 to 15, all different within a row; in each aligned block of 6 rows (0 to 5, 6 to 11, ...) at most 2 rows name the same one
- retrieval_row: int32 [768, 2], P(('db', 'seq')), may hold values from 0 to 31
- database: bfloat16 [512, 64, 896], P('db'), may hold values from -6 to 6
- ffn_in: bfloat16 [896, 3584], P(None, 'db'), may hold values from -0.1875 to 0.1875
- ffn_out: bfloat16 [3584, 896], P('db'), may hold values from -0.09375 to 0.09375
- cross_projection: bfloat16 [896, 4096], P(None, 'db'), may hold values from -0.1875 to 0.1875
Outputs:
- self_attended: bfloat16 [49152, 2048], P(('db', 'seq'))
- cross_attended: bfloat16 [49152, 2048], P(('db', 'seq'))
Inputs may be any that keep to these rules, and one draw needn't show every extreme that they name: `retrieval_shard`: each row names 2 different shards; among the rows of one device no shard is named more than 2 times, a bound that some block reaches.
All inputs are finite; a program needn't handle non-finite values.
Results may differ from a plain program's by a relative error of at most 0.04.
Values may be sent and summed in bfloat16 or wider, within the bound.
No kernel may reach another device: no remote copies, remote signals or barrier semaphores. Data moves between devices by JAX's collectives and lax.ppermute only.
A program may use at most 256 MiB of HBM per device.

v0:
```python
import math

import jax
import jax.numpy as jnp
from jax import lax
from jax.sharding import PartitionSpec as P

HEADS = 16
HEAD_DIM = 128
STRETCH = 64
NEIGH = 2
CAP = 2


def shifted(value, axis, steps):
    count = lax.axis_size(axis)
    leading, last = (max(0, -steps), min(count, count - steps))
    return lax.ppermute(value, axis, [(source, source + steps) for source in range(leading, last)])


def normalize(values):
    wide = values.astype(jnp.float32)
    return (wide * lax.rsqrt(jnp.mean(wide * wide, axis=-1, keepdims=True) + 1e-06)).astype(
        jnp.bfloat16
    )


def shards(
    self_query,
    self_key,
    self_value,
    cross_query,
    retrieval_shard,
    retrieval_row,
    database,
    ffn_in,
    ffn_out,
    cross_projection,
):
    width = HEADS * HEAD_DIM
    scale = 1.0 / math.sqrt(HEAD_DIM)
    rows = self_query.shape[0]
    stretches = rows // STRETCH
    shard_list = retrieval_shard.reshape(-1)
    row_list = retrieval_row.reshape(-1)
    requests = shard_list.shape[0]
    owners = lax.axis_size("db")
    order = jnp.arange(requests)
    earlier = (order[:, None] > order[None, :]) & (shard_list[:, None] == shard_list[None, :])
    rank = jnp.sum(earlier.astype(jnp.int32), axis=1)
    slot = shard_list * CAP + rank
    slots = jnp.arange(owners * CAP)
    hits = slots[:, None] == slot[None, :]
    wanted = (jnp.sum(jnp.where(hits, row_list[None, :] + 1, 0), axis=1) - 1).reshape(owners, CAP)
    asked = lax.all_to_all(wanted, "db", split_axis=0, concat_axis=0, tiled=True)
    found = jnp.take(database, jnp.maximum(asked, 0), axis=0)
    found = jnp.where((asked >= 0)[:, :, None, None], found, jnp.zeros_like(found))
    arrived = lax.all_to_all(found, "db", split_axis=0, concat_axis=0, tiled=True)
    arrived = arrived.reshape(owners * CAP, arrived.shape[2], arrived.shape[3])
    picked = jnp.take(arrived, slot, axis=0)
    neighbours = picked.reshape(-1, picked.shape[2])
    span = NEIGH * arrived.shape[1]
    normed_in = normalize(neighbours)
    expanded = jax.nn.gelu(
        jnp.dot(
            normed_in,
            lax.all_gather(ffn_in, "db", axis=1, tiled=True),
            preferred_element_type=jnp.float32,
        ),
        approximate=True,
    ).astype(jnp.bfloat16)
    mixed = jnp.dot(
        expanded,
        lax.all_gather(ffn_out, "db", axis=0, tiled=True),
        preferred_element_type=jnp.float32,
    )
    encoded = (neighbours.astype(jnp.float32) + mixed).astype(jnp.bfloat16)
    normed_out = normalize(encoded)
    own = jnp.dot(
        normed_out,
        lax.all_gather(cross_projection, "db", axis=1, tiled=True),
        preferred_element_type=jnp.float32,
    ).astype(jnp.bfloat16)
    previous = shifted(own[-span:], "seq", 1)
    projected = jnp.concatenate([previous, own], axis=0)
    projected = projected.reshape(stretches + 1, span, 2, HEADS, HEAD_DIM)
    cross_keys = projected[:, :, 0]
    cross_values = projected[:, :, 1]
    padded = jnp.concatenate(
        [
            jnp.zeros((1, width), jnp.bfloat16),
            cross_query,
            jnp.zeros((STRETCH - 1, width), jnp.bfloat16),
        ],
        axis=0,
    )
    grouped_query = padded.reshape(stretches + 1, STRETCH, HEADS, HEAD_DIM)
    scores = (
        jnp.einsum("gqhd,gkhd->ghqk", grouped_query, cross_keys, preferred_element_type=jnp.float32)
        * scale
    )
    probs = jnp.exp(scores - jnp.max(scores, axis=-1, keepdims=True))
    denominator = jnp.sum(probs, axis=-1)
    cross_out = jnp.einsum(
        "ghqk,gkhd->gqhd",
        probs.astype(jnp.bfloat16),
        cross_values,
        preferred_element_type=jnp.float32,
    )
    cross_out = cross_out / jnp.transpose(denominator, (0, 2, 1))[..., None]
    cross_attended = cross_out.reshape(-1, width)[1 : rows + 1].astype(jnp.bfloat16)
    position = lax.axis_index("seq") * rows + jnp.arange(rows)
    query = self_query.reshape(rows, HEADS, HEAD_DIM)
    best = jnp.full((HEADS, rows), -1e30, jnp.float32)
    keys = lax.all_gather(self_key, "seq", axis=0, tiled=True).reshape(-1, HEADS, HEAD_DIM)
    values = lax.all_gather(self_value, "seq", axis=0, tiled=True).reshape(-1, HEADS, HEAD_DIM)
    count = keys.shape[0]
    block_scores = (
        jnp.einsum("qhd,khd->hqk", query, keys, preferred_element_type=jnp.float32) * scale
    )
    allowed = jnp.arange(count)[None, :] <= position[:, None]
    block_scores = jnp.where(allowed[None], block_scores, -1e30)
    fresh = jnp.maximum(best, jnp.max(block_scores, axis=-1))
    block_probs = jnp.where(allowed[None], jnp.exp(block_scores - fresh[..., None]), 0.0)
    running = jnp.sum(block_probs, axis=-1)
    summed = jnp.einsum(
        "hqk,khd->hqd", block_probs.astype(jnp.bfloat16), values, preferred_element_type=jnp.float32
    )
    best, running, summed = (fresh, running, summed)
    self_out = summed / running[..., None]
    self_attended = jnp.transpose(self_out, (1, 0, 2)).reshape(rows, width).astype(jnp.bfloat16)
    return (self_attended, cross_attended)


def solution(mesh):
    in_specs = (
        P(("db", "seq"), None),
        P(("db", "seq"), None),
        P(("db", "seq"), None),
        P(("db", "seq"), None),
        P(("db", "seq"), None),
        P(("db", "seq"), None),
        P("db", None, None),
        P(None, "db"),
        P("db", None),
        P(None, "db"),
    )
    out_specs = (P(("db", "seq"), None), P(("db", "seq"), None))
    return jax.shard_map(shards, mesh=mesh, in_specs=in_specs, out_specs=out_specs, check_vma=False)
```

profile of v0, /device:TPU:1, one launch (start us, length us, event | category | flops | bytes accessed | tf_op | source)
XLA Modules:
  0.0 461.4 jit_solution(2357627016175675936)
XLA Ops:
  7.2 0.0 all-gather.12.cloned.1.call-start
  7.2 0.7 all-gather.12.cloned.1.call-update
  7.9 0.0 all-gather.10.cloned.1.call-start
  8.0 0.7 all-gather.10.cloned.1.call-update
  8.7 0.0 all-gather.14.cloned.1.call-start
  8.7 0.7 all-gather.14.cloned.1.call-update
  9.4 0.0 all-gather.6.cloned.1.call-start
  9.5 2.6 copy.74
  12.0 0.0 all-gather.6.cloned.1.call-update
  12.1 0.1 copy.79
  12.2 0.1 add.102
  12.3 0.1 copy.78
  12.4 0.1 reshape.195
  12.4 0.2 convert_reduce_fusion
  12.6 0.1 select_reduce_fusion
  12.7 0.7 sub.25
  13.4 7.6 %all-to-all-start = ((s32[16,1,2]{2,1,0:T(1,128)}), s32[16,1,2]{2,1,0:T(1,128)S(1)}, u32[]{:S(2)}, u32[]{:S(2)}) async-start(s32[16,1,2]{2,1,0:T(1,128)} %bitcast.5), calls=%async_computation | async-start | bytes 16384 | tf_op jit(solution)/shard_map/all_to_all | solution.py:55
  21.0 0.0 all-gather.8.cloned.1.call-start
  21.1 0.5 all-gather.8.cloned.1.call-update
  21.6 5.7 %all-to-all-done = s32[16,1,2]{2,1,0:T(1,128)S(1)} async-done(((s32[16,1,2]{2,1,0:T(1,128)}), s32[16,1,2]{2,1,0:T(1,128)S(1)}, u32[]{:S(2)}, u32[]{:S(2)}) %all-to-all-start) | async-done | bytes 160 | tf_op jit(solution)/shard_map/all_to_all | solution.py:55
  27.4 0.1 copy.81
  27.5 0.1 copy.85
  27.5 0.1 reshape.202
  27.6 0.1 copy.84
  27.7 0.1 copy.82
  27.8 5.0 %gather_fusion = bf16[32,64,896]{2,1,0:T(8,128)(2,1)} fusion(bf16[32,64,896]{2,1,0:T(8,128)(2,1)} %param.16, s32[1024]{0:T(1024)S(1)} %pad_clamp_fusion.1), kind=kCustom, calls=%fused_computation | custom fusion | bytes 7340160 | tf_op jit(solution)/shard_map/jit(_take)/gather | solution.py:56
  32.8 4.5 select_select_fusion
  37.3 4.7 %all-to-all-start.1 = ((bf16[16,2,64,896]{3,2,1,0:T(8,128)(2,1)}), bf16[16,2,64,896]{3,2,1,0:T(8,128)(2,1)}, u32[]{:S(2)}, u32[]{:S(2)}) async-start(bf16[16,2,64,896]{3,2,1,0:T(8,128)(2,1)} %select_select_fusion), calls=%async_computation.1 | async-start | bytes 7340032 | tf_op jit(solution)/shard_map/all_to_all | solution.py:58
  42.0 0.1 copy.86
  42.1 0.1 mul.85
  42.2 0.1 broadcast_in_dim.97
  42.3 0.1 broadcast_in_dim.98
  42.4 0.1 pad.4.clone
  42.5 64.8 %all-to-all-done.1 = bf16[16,2,64,896]{3,2,1,0:T(8,128)(2,1)} async-done(((bf16[16,2,64,896]{3,2,1,0:T(8,128)(2,1)}), bf16[16,2,64,896]{3,2,1,0:T(8,128)(2,1)}, u32[]{:S(2)}, u32[]{:S(2)}) %all-to-all-start.1) | async-done | bytes 3670048 | tf_op jit(solution)/shard_map/all_to_all | solution.py:58
  107.3 2.8 gather_fusion.1
  110.1 0.5 multiply_reduce_fusion.1
  110.6 0.1 rsqrt.20
  110.7 1.4 bitcast_select_fusion
  112.1 66.4 %all-gather.10.cloned.1.call-done = bf16[896,3584]{0,1:T(8,128)(2,1)} async-done(((bf16[896,224]{0,1:T(8,128)(2,1)}), bf16[896,3584]{0,1:T(8,128)(2,1)}) %all-gather.10.cloned.1.call-update) | async-done | bytes 6422544 | tf_op jit(solution)/shard_map/all_gather | solution.py:67
  178.4 17.1 %fusion.24 = (f32[768]{0:T(1024)S(1)}, bf16[768,896]{1,0:T(8,128)(2,1)S(1)}) fusion(bf16[3584,896]{1,0:T(8,128)(2,1)} %all-gather.12.cloned.1.call-done, bf16[768,896]{1,0:T(8,128)(2,1)} %bitcast_select_fusion, bf16[896,3584]{0,1:T(8,128)(2,1)} %all-gather.10.cloned.1.call-done, f32[768]{0:T(1024)S(1)} %rsqrt.20), kind=kOutput, calls=%fused_computation.41 | convolution fusion | flops 9895967744 | bytes 15603712 | tf_op jit(solution)/shard_map/dot_general | solution.py:72
  195.6 56.7 %all-gather.14.cloned.1.call-done = bf16[896,4096]{1,0:T(8,128)(2,1)} async-done(((bf16[896,256]{1,0:T(8,128)(2,1)}), bf16[896,4096]{1,0:T(8,128)(2,1)}) %all-gather.14.cloned.1.call-update) | async-done | bytes 7340048 | tf_op jit(solution)/shard_map/all_gather | solution.py:81
  252.3 10.5 %convolution_convert_fusion = bf16[768,4096]{1,0:T(8,128)(2,1)S(1)} fusion(bf16[896,4096]{1,0:T(8,128)(2,1)} %all-gather.14.cloned.1.call-done, bf16[768,896]{1,0:T(8,128)(2,1)S(1)} %get-tuple-element.21, f32[768]{0:T(1024)S(1)} %add_rsqrt_fusion.1), kind=kOutput, calls=%fused_computation.19 | convolution fusion | flops 5642354688 | bytes 15010816 | tf_op jit(solution)/shard_map/dot_general | solution.py:79
  262.9 2.9 copy-done.2
  265.8 1.0 slice.21
  266.8 4.6 collective-permute-start
  271.4 0.8 maximum_bitcast_fusion.1
  272.3 1.8 copy.96
  274.0 0.7 iota_compare_fusion
  274.7 31.2 %collective-permute-done = bf16[128,4096]{1,0:T(8,128)(2,1)} collective-permute-done((bf16[128,4096]{1,0:T(8,128)(2,1)}, bf16[128,4096]{1,0:T(8,128)(2,1)}, u32[]{:S(2)}, u32[]{:S(2)}) %collective-permute-start) | collective-permute-done | bytes 1048608 | tf_op jit(solution)/shard_map/ppermute | solution.py:18
  305.9 6.9 %maximum_bitcast_fusion = bf16[112,8,32,128]{3,1,2,0:T(8,128)(2,1)} fusion(bf16[768,4096]{1,0:T(8,128)(2,1)} %copy-done.2, bf16[128,4096]{1,0:T(8,128)(2,1)} %collective-permute-done), kind=kLoop, calls=%fused_computation.18 | loop fusion | flops 14680064 | bytes 14680064
  312.8 5.5 %copy.97 = bf16[112,8,32,128]{3,2,1,0:T(8,128)(2,1)S(1)} copy(bf16[112,8,32,128]{3,1,2,0:T(8,128)(2,1)} %maximum_bitcast_fusion) | data formatting | bytes 14680064
  318.4 3.1 fusion.52
  321.4 2.7 multiply_reduce_fusion
  324.2 2.4 fusion.20
  326.6 2.5 fusion.18
  329.1 1.2 copy.90
  330.3 0.5 copy.118
  330.8 1.5 slice.24
  332.4 32.7 %fusion = (f32[16,384]{1,0:T(8,128)S(1)}, f32[16,384,3072]{2,1,0:T(8,128)}) fusion(pred[384,3072]{1,0:T(8,128)(4,1)S(1)} %iota_compare_fusion, bf16[3072,16,128]{0,2,1:T(8,128)(2,1)} %bitcast.73, bf16[384,2048]{1,0:T(8,128)(2,1)S(1)} %copy-done), kind=kOutput, calls=%fused_computation.4 | convolution fusion | flops 4888455168 | bytes 90857472 | tf_op jit(solution)/shard_map/qhd,khd->hqk/dot_general | solution.py:119
  365.0 25.9 %fusion.1 = f32[16,384]{1,0:T(8,128)S(1)} fusion(f32[16,384,3072]{2,1,0:T(8,128)} %get-tuple-element.19, f32[16,384]{1,0:T(8,128)S(1)} %broadcast_maximum_fusion, pred[384,3072]{1,0:T(8,128)(4,1)S(1)} %iota_compare_fusion), kind=kLoop, calls=%fused_computation.5 | loop fusion | flops 94365696 | bytes 76726272 | tf_op jit(solution)/shard_map/reduce_sum | solution.py:125
  391.0 10.8 %all-gather.8.cloned.1.call-done = bf16[3072,2048]{1,0:T(8,128)(2,1)} async-done(((bf16[384,2048]{1,0:T(8,128)(2,1)}), bf16[3072,2048]{1,0:T(8,128)(2,1)}) %all-gather.8.cloned.1.call-update) | async-done | bytes 12582928 | tf_op jit(solution)/shard_map/all_gather | solution.py:116
  401.8 16.6 %copy.77 = bf16[3072,2048]{0,1:T(8,128)(2,1)} copy(bf16[3072,2048]{1,0:T(8,128)(2,1)} %all-gather.8.cloned.1.call-done) | data formatting | bytes 25165824 | tf_op jit(solution)/shard_map/all_gather | solution.py:116
  418.4 33.8 %fusion.19 = bf16[384,16,128]{0,2,1:T(8,128)(2,1)} fusion(bf16[3072,16,128]{0,2,1:T(8,128)(2,1)} %bitcast.75, f32[16,384,3072]{2,1,0:T(8,128)} %get-tuple-element.19, f32[16,384]{1,0:T(8,128)S(1)} %broadcast_maximum_fusion, pred[384,3072]{1,0:T(8,128)(4,1)S(1)} %iota_compare_fusion, f32[384,16]{0,1:T(8,128)S(1)} %bitcast.81), kind=kOutput, calls=%fused_computation.36 | convolution fusion | flops 4927782912 | bytes 90882048 | tf_op jit(solution)/shard_map/hqk,khd->hqd/dot_general | solution.py:126
  452.3 2.6 copy.91
  (32 shorter events, 0.1 us)
Async XLA Ops:
  7.2 325.2 %copy-start = (bf16[384,2048]{1,0:T(8,128)(2,1)S(1)}, bf16[384,2048]{1,0:T(8,128)(2,1)}, u32[]{:S(2)}) copy-start(bf16[384,2048]{1,0:T(8,128)(2,1)} %param.10) | copy-start | bytes 4718596
  7.2 4.9 %copy-start.7 = (s32[6,2]{0,1:T(2,128)S(1)}, s32[6,2]{0,1:T(2,128)}, u32[]{:S(2)}) copy-start(s32[6,2]{0,1:T(2,128)} %param.15) | copy-start | bytes 148
  7.2 5.1 %copy-start.6 = (s32[6,2]{0,1:T(2,128)S(1)}, s32[6,2]{0,1:T(2,128)}, u32[]{:S(2)}) copy-start(s32[6,2]{0,1:T(2,128)} %param.14) | copy-start | bytes 148
  7.2 104.9 %all-gather.12.cloned.1.call-start = ((), (), s32[]{:S(2)}) async-start(), calls=%async_computation.5 | async-start | bytes 6823936 | tf_op jit(solution)/shard_map/all_gather | solution.py:74
  7.9 170.5 %all-gather.10.cloned.1.call-start = ((), (), s32[]{:S(2)}) async-start(), calls=%async_computation.4 | async-start | bytes 6823936 | tf_op jit(solution)/shard_map/all_gather | solution.py:67
  8.7 243.6 %all-gather.14.cloned.1.call-start = ((), (), s32[]{:S(2)}) async-start(), calls=%async_computation.6 | async-start | bytes 7798784 | tf_op jit(solution)/shard_map/all_gather | solution.py:81
  9.4 322.9 %all-gather.6.cloned.1.call-start = ((), (), s32[]{:S(2)}) async-start(), calls=%async_computation.2 | async-start | bytes 14155776 | tf_op jit(solution)/shard_map/all_gather | solution.py:115
  13.4 13.9 %all-to-all-start = ((s32[16,1,2]{2,1,0:T(1,128)}), s32[16,1,2]{2,1,0:T(1,128)S(1)}, u32[]{:S(2)}, u32[]{:S(2)}) async-start(s32[16,1,2]{2,1,0:T(1,128)} %bitcast.5), calls=%async_computation | async-start | bytes 16384 | tf_op jit(solution)/shard_map/all_to_all | solution.py:55
  21.0 380.7 %all-gather.8.cloned.1.call-start = ((), (), s32[]{:S(2)}) async-start(), calls=%async_computation.3 | async-start | bytes 14155776 | tf_op jit(solution)/shard_map/all_gather | solution.py:116
  37.3 70.0 %all-to-all-start.1 = ((bf16[16,2,64,896]{3,2,1,0:T(8,128)(2,1)}), bf16[16,2,64,896]{3,2,1,0:T(8,128)(2,1)}, u32[]{:S(2)}, u32[]{:S(2)}) async-start(bf16[16,2,64,896]{3,2,1,0:T(8,128)(2,1)} %select_select_fusion), calls=%async_computation.1 | async-start | bytes 7340032 | tf_op jit(solution)/shard_map/all_to_all | solution.py:58
  252.3 19.1 %copy-start.5 = (bf16[384,2048]{1,0:T(8,128)(2,1)S(1)}, bf16[384,2048]{1,0:T(8,128)(2,1)}, u32[]{:S(2)}) copy-start(bf16[384,2048]{1,0:T(8,128)(2,1)} %param.13) | copy-start | bytes 4718596
  262.8 2.9 copy-start.2
  266.8 39.1 %collective-permute-start = (bf16[128,4096]{1,0:T(8,128)(2,1)}, bf16[128,4096]{1,0:T(8,128)(2,1)}, u32[]{:S(2)}, u32[]{:S(2)}) collective-permute-start(bf16[128,4096]{1,0:T(8,128)(2,1)} %slice.21), channel_id=1, source_target_pairs={{0,1},{1,2},{2,3},{3,4},{4,5},{5,6},{6,7},{8,9},{9,10},{10,11},{11... | collective-permute-start | bytes 3145736 | tf_op jit(solution)/shard_map/ppermute | solution.py:18
  318.4 3.1 copy-start.3
  324.2 2.4 copy-start.4
  418.4 36.4 %copy-start.1 = (bf16[384,2048]{1,0:T(8,128)(2,1)S(1)}, bf16[384,2048]{1,0:T(8,128)(2,1)}, u32[]{:S(2)}) copy-start(bf16[384,2048]{1,0:T(8,128)(2,1)} %param.10) | copy-start | bytes 4718596
Sparse Core Ops, SparseCore 0:
  10.2 101.3 all-gather.11
  113.7 64.7 all-gather.9
  180.5 71.7 all-gather.13
  254.4 73.4 all-gather.5
  329.4 72.2 all-gather.7
where the time goes:
time: 462 us; the launch traced here: 461 us
  waiting for transfers between devices  238 us (52%)
  matrix products  99.4 us (22%)
  local copies, waits for them, and re-layouts  49.1 us (11%)
  other arithmetic  43.5 us (9%)
  starting transfers between devices  17.1 us (4%)
  between operations  14 us (3%)
    all_gather x1, waiting for transfers between devices, shards(): lax.all_gather(ffn_in, 'db', axis=1, tiled=True)  66.4 us
    all_to_all x1, waiting for transfers between devices, shards(): lax.all_to_all(found, 'db', split_axis=0, concat_axis=0, tiled=True)  64.8 us
    all_gather x1, waiting for transfers between devices, shards(): lax.all_gather(cross_projection, 'db', axis=1, tiled=True)  56.7 us
    dot_general x1, matrix products, shards(): jnp.einsum('hqk,khd->hqd', block_probs.astype(jnp.bfloat16), values, pref...  33.8 us
    dot_general x1, matrix products, shards(): jnp.einsum('qhd,khd->hqk', query, keys, preferred_element_type=jnp.float32)  32.7 us
    ppermute x1, waiting for transfers between devices, shifted(): lax.ppermute(value, axis, [(source, source + steps) for source in range(l...  31.2 us
    reduce_sum x1, other arithmetic, shards(): running = jnp.sum(block_probs, axis=-1)  25.9 us
    dot_general x1, matrix products, shards(): jnp.dot(expanded, lax.all_gather(ffn_out, 'db', axis=0, tiled=True), pref...  17.1 us
  transfers between devices with their start and end apart: 8, of which 6 were waited for; matrix products, arithmetic and copies ran while one was open for 29% of the time, Pallas kernels for 0%

commit v1 on v0

v1 whole, which is shorter than its diff:
```python
import functools
import math

import jax
import jax.numpy as jnp
from jax import lax
from jax.experimental import pallas as pl
from jax.experimental.pallas import tpu as pltpu
from jax.sharding import PartitionSpec as P

HEADS = 16
HEAD_DIM = 128
STRETCH = 64
NEIGH = 2
CAP = 2
LOG2E = 1.4426950408889634
BF16 = jnp.bfloat16
F32 = jnp.float32
NT = (((1,), (1,)), ((), ()))
ANY = pl.BlockSpec(memory_space=pl.ANY)
VMEM = pl.BlockSpec(memory_space=pltpu.VMEM)
HOPS = ((0, 0), (2, 0), (2, 1), (1, 0), (3, 0), (1, 1), (3, 1), (0, 1))


def cost(flops, size, exps=0):
    return pl.CostEstimate(flops=int(flops), bytes_accessed=int(size), transcendentals=int(exps))


def params(mib=56, **more):
    return pltpu.CompilerParams(vmem_limit_bytes=mib << 20, **more)


def hop(value, chips, flip):
    count = lax.axis_size("seq")
    pairs = [(i, ((i + 2 * chips) % count) ^ flip) for i in range(count)]
    return lax.ppermute(value, "seq", pairs)


def run_copies(copies):
    for copy in copies:
        copy.start()
    for copy in copies:
        copy.wait()


def rms(wide):
    return wide * lax.rsqrt(jnp.mean(wide * wide, axis=-1, keepdims=True) + 1e-06)


def fetch_kernel(asked, database, found, sem):
    run_copies(
        [
            pltpu.make_async_copy(database.at[asked[i]], found.at[i], sem.at[i])
            for i in range(found.shape[0])
        ]
    )


def fetch(asked, database):
    slots = asked.shape[0]
    shape = (slots, *database.shape[1:])
    return pl.pallas_call(
        fetch_kernel,
        grid_spec=pltpu.PrefetchScalarGridSpec(
            num_scalar_prefetch=1,
            grid=(1,),
            in_specs=[ANY],
            out_specs=ANY,
            scratch_shapes=[pltpu.SemaphoreType.DMA((slots,))],
        ),
        out_shape=jax.ShapeDtypeStruct(shape, BF16),
        cost_estimate=cost(0, 4 * math.prod(shape)),
        compiler_params=params(),
        name="fetch",
    )(asked, database)


def ffn_blocks(xn, gathered, half):
    count = gathered.shape[0]
    w_in = jnp.concatenate([gathered[b, :half] for b in range(count)], axis=0)
    w_out = jnp.concatenate([gathered[b, half:] for b in range(count)], axis=0)
    hidden = lax.dot_general(xn, w_in, NT, preferred_element_type=F32)
    hidden = jax.nn.gelu(hidden, approximate=True).astype(BF16)
    return jnp.dot(hidden, w_out, preferred_element_type=F32)


def ffn_first_kernel(half, slot, arrived, gathered, total, normed, x, sem):
    tokens = arrived.shape[1]

    @pl.when(pl.program_id(0) == 0)
    def _():
        run_copies(
            [
                pltpu.make_async_copy(
                    arrived.at[slot[i]], x.at[i * tokens : (i + 1) * tokens], sem.at[i]
                )
                for i in range(x.shape[0] // tokens)
            ]
        )
        wide = x[...].astype(F32)
        normed[...] = rms(wide).astype(BF16)
        total[...] = wide

    total[...] += ffn_blocks(normed[...], gathered, half)


def ffn_second_kernel(half, normed, before, gathered, out, total):
    @pl.when(pl.program_id(0) == 0)
    def _():
        total[...] = before[...]

    total[...] += ffn_blocks(normed[...], gathered, half)

    @pl.when(pl.program_id(0) == pl.num_programs(0) - 1)
    def _():
        encoded = total[...].astype(BF16).astype(F32)
        out[...] = rms(encoded).astype(BF16)


def ffn_first(slot, arrived, gathered, half):
    requests = slot.shape[0]
    rows, width = requests * arrived.shape[1], arrived.shape[2]
    owners = gathered.shape[0]
    step = 4
    whole = lambda i, s: (0, 0)
    return pl.pallas_call(
        functools.partial(ffn_first_kernel, half),
        grid_spec=pltpu.PrefetchScalarGridSpec(
            num_scalar_prefetch=1,
            grid=(owners // step,),
            in_specs=[ANY, pl.BlockSpec((step, 2 * half, width), lambda i, s: (i, 0, 0))],
            out_specs=[pl.BlockSpec((rows, width), whole), pl.BlockSpec((rows, width), whole)],
            scratch_shapes=[pltpu.VMEM((rows, width), BF16), pltpu.SemaphoreType.DMA((requests,))],
        ),
        out_shape=[
            jax.ShapeDtypeStruct((rows, width), F32),
            jax.ShapeDtypeStruct((rows, width), BF16),
        ],
        cost_estimate=cost(4 * rows * width * owners * half, 16e6, rows * owners * half),
        compiler_params=params(),
        name="ffn_first",
    )(slot, arrived, gathered)


def ffn_second(normed, before, gathered, half):
    rows, width = normed.shape
    owners = gathered.shape[0]
    step = 4
    whole = pl.BlockSpec((rows, width), lambda i: (0, 0))
    return pl.pallas_call(
        functools.partial(ffn_second_kernel, half),
        grid=(owners // step,),
        in_specs=[whole, whole, pl.BlockSpec((step, 2 * half, width), lambda i: (i, 0, 0))],
        out_specs=whole,
        out_shape=jax.ShapeDtypeStruct((rows, width), BF16),
        scratch_shapes=[pltpu.VMEM((rows, width), F32)],
        cost_estimate=cost(4 * rows * width * owners * half, 16e6, rows * owners * half),
        compiler_params=params(),
        name="ffn_second",
    )(normed, before, gathered)


def attend(query, keys, values, allowed, scale):
    scores = lax.dot_general(query, keys, NT, preferred_element_type=F32)
    if allowed is not None:
        scores = jnp.where(allowed, scores, -jnp.inf)
    probs = jnp.exp2((scores - jnp.max(scores, axis=-1, keepdims=True)) * scale)
    total = jnp.sum(probs, axis=-1, keepdims=True)
    return jnp.dot(probs.astype(BF16), values, preferred_element_type=F32) / total


def cross_kernel(first, scale, core, normed, mine, other, query, ahead, out, sent, weights, sem):
    step = pl.program_id(0)
    groups = weights.shape[0]
    width = weights.shape[2]
    d = HEAD_DIM
    own = pl.multiple_of(core[0] * d, d)
    rest = pl.multiple_of((1 - core[0]) * d, d)

    def copies(j):
        found = []
        for part in range(2):
            for t, (source, place) in enumerate(((mine, own), (other, rest))):
                found.append(
                    pltpu.make_async_copy(
                        source.at[part * groups + j, first:, :],
                        weights.at[j, pl.ds(part * 2 * d + place, d), :],
                        sem.at[j, 2 * part + t],
                    )
                )
        return found

    @pl.when(step == 0)
    def _():
        for j in range(groups):
            for copy in copies(j):
                copy.start()

    for copy in copies(step):
        copy.wait()
    pairs = lax.dot_general(normed[...], weights[step], NT, preferred_element_type=F32).astype(BF16)
    span = NEIGH * STRETCH
    stretches = normed.shape[0] // span
    at_row = lax.broadcasted_iota(jnp.int32, (STRETCH, 2 * span), 0)
    at_key = lax.broadcasted_iota(jnp.int32, (STRETCH, 2 * span), 1)
    allowed = (at_row == STRETCH - 1) == (at_key >= span)
    for t in range(2):
        lanes = slice(t * d, (t + 1) * d)
        keys = pairs[:, t * d : (t + 1) * d]
        values = pairs[:, (2 + t) * d : (3 + t) * d]
        for b in range(stretches):
            rows = slice(b * STRETCH, (b + 1) * STRETCH)
            low, high = max(b - 1, 0) * span, (b + 1) * span
            out[rows, lanes] = attend(
                query[rows, lanes], keys[low:high], values[low:high], allowed if b else None, scale
            ).astype(BF16)
        sent[:, lanes] = attend(
            ahead[:, lanes], keys[-span:], values[-span:], None, scale
        ).astype(BF16)


def cross(core, normed, mine, other, query, ahead, half):
    rows, width = query.shape
    first = 2 * half
    groups = mine.shape[0] // 2
    d = HEAD_DIM
    column = lambda j, c: (0, j)
    deep = normed.shape[1]
    return pl.pallas_call(
        functools.partial(cross_kernel, first, LOG2E / math.sqrt(d)),
        grid_spec=pltpu.PrefetchScalarGridSpec(
            num_scalar_prefetch=1,
            grid=(groups,),
            in_specs=[
                pl.BlockSpec(normed.shape, lambda j, c: (0, 0)),
                ANY,
                ANY,
                pl.BlockSpec((rows, 2 * d), column),
                pl.BlockSpec((STRETCH, 2 * d), column),
            ],
            out_specs=[
                pl.BlockSpec((rows, 2 * d), column),
                pl.BlockSpec((STRETCH, 2 * d), column),
            ],
            scratch_shapes=[
                pltpu.VMEM((groups, 4 * d, deep), BF16),
                pltpu.SemaphoreType.DMA((groups, 4)),
            ],
        ),
        out_shape=[
            jax.ShapeDtypeStruct(query.shape, BF16),
            jax.ShapeDtypeStruct(ahead.shape, BF16),
        ],
        cost_estimate=cost(2 * normed.shape[0] * deep * 4 * d * groups * 2, 12e6, rows * 256 * 16),
        compiler_params=params(),
        name="cross",
    )(core, normed, mine, other, query, ahead)


def place_of(chip, core, hop_of, chips):
    return lax.rem(chip + hop_of[0], chips), jnp.bitwise_xor(core, hop_of[1])


def pack_kernel(where, query, key, value, *rest):
    parts, sem = rest[:-1], rest[-1]
    block = parts[0].shape[2]
    copies = []
    for n, part in enumerate(parts):
        columns = pl.ds(pl.multiple_of(where[n] * block, block), block)
        for a, source in enumerate((query, key, value)):
            copies.append(
                pltpu.make_async_copy(source.at[:, columns], part.at[a], sem.at[n, a])
            )
    run_copies(copies)


def pack(where, query, key, value):
    rows, width = query.shape
    count = len(HOPS)
    shape = (3, rows, width // count)
    return pl.pallas_call(
        pack_kernel,
        grid_spec=pltpu.PrefetchScalarGridSpec(
            num_scalar_prefetch=1,
            grid=(1,),
            in_specs=[ANY] * 3,
            out_specs=[ANY] * count,
            scratch_shapes=[pltpu.SemaphoreType.DMA((count, 3))],
        ),
        out_shape=[jax.ShapeDtypeStruct(shape, BF16)] * count,
        cost_estimate=cost(0, 12 * rows * width),
        compiler_params=params(),
        name="pack",
    )(where, query, key, value)


def self_kernel(scale, source, *refs):
    count = len(HOPS)
    parts, outs = refs[:count], refs[count : 2 * count]
    query, key, value, result = refs[2 * count :]
    rows = parts[0].shape[1]
    d = HEAD_DIM
    for n in range(count):
        place = pl.ds(pl.multiple_of(source[n] * rows, rows), rows)
        query[place, :] = parts[n][0]
        key[place, :] = parts[n][1]
        value[place, :d] = parts[n][2]
    value[:, d:] = jnp.ones((count * rows, d), BF16)
    at_row = lax.broadcasted_iota(jnp.int32, (rows, rows), 0)
    at_key = lax.broadcasted_iota(jnp.int32, (rows, rows), 1)
    allowed = at_key <= at_row
    for i in range(count):
        low, high = i * rows, (i + 1) * rows
        block = query[low:high, :]
        scores = lax.dot_general(block, key[low:high, :], NT, preferred_element_type=F32)
        scores = jnp.where(allowed, scores, -jnp.inf)
        if i:
            left = lax.dot_general(block, key[:low, :], NT, preferred_element_type=F32)
            scores = jnp.concatenate([left, scores], axis=1)
        best = jnp.max(scores, axis=-1, keepdims=True)
        probs = jnp.exp2((scores - best) * scale).astype(BF16)
        summed = jnp.dot(probs, value[:high, :], preferred_element_type=F32)
        result[low:high, :] = (summed[:, :d] / summed[:, d:]).astype(BF16)
    for n in range(count):
        place = pl.ds(pl.multiple_of(source[n] * rows, rows), rows)
        outs[n][...] = result[place, :]


def self_attention(source, parts):
    count = len(HOPS)
    _, rows, width = parts[0].shape
    d = HEAD_DIM
    length = count * rows
    return pl.pallas_call(
        functools.partial(self_kernel, LOG2E / math.sqrt(d)),
        grid_spec=pltpu.PrefetchScalarGridSpec(
            num_scalar_prefetch=1,
            grid=(width // d,),
            in_specs=[pl.BlockSpec((3, rows, d), lambda h, s: (0, 0, h))] * count,
            out_specs=[pl.BlockSpec((rows, d), lambda h, s: (0, h))] * count,
            scratch_shapes=[
                pltpu.VMEM((length, d), BF16),
                pltpu.VMEM((length, d), BF16),
                pltpu.VMEM((length, 2 * d), BF16),
                pltpu.VMEM((length, d), BF16),
            ],
        ),
        out_shape=[jax.ShapeDtypeStruct((rows, width), BF16)] * count,
        cost_estimate=cost(3 * length * length * d * 2, 8e6, length * length),
        compiler_params=params(),
        name="causal",
    )(source, *parts)


def unpack_kernel(where, *refs):
    parts, out, sem = refs[:-2], refs[-2], refs[-1]
    block = parts[0].shape[1]
    run_copies(
        [
            pltpu.make_async_copy(
                part, out.at[:, pl.ds(pl.multiple_of(where[n] * block, block), block)], sem.at[n]
            )
            for n, part in enumerate(parts)
        ]
    )


def unpack(where, parts):
    rows, block = parts[0].shape
    count = len(parts)
    return pl.pallas_call(
        unpack_kernel,
        grid_spec=pltpu.PrefetchScalarGridSpec(
            num_scalar_prefetch=1,
            grid=(1,),
            in_specs=[ANY] * count,
            out_specs=ANY,
            scratch_shapes=[pltpu.SemaphoreType.DMA((count,))],
        ),
        out_shape=jax.ShapeDtypeStruct((rows, block * count), BF16),
        cost_estimate=cost(0, 4 * rows * block * count),
        compiler_params=params(),
        name="unpack",
    )(where, *parts)


def requests_of(retrieval_shard, retrieval_row):
    shard_list = retrieval_shard.reshape(-1)
    row_list = retrieval_row.reshape(-1)
    owners = lax.axis_size("db")
    order = jnp.arange(shard_list.shape[0])
    earlier = (order[:, None] > order[None, :]) & (shard_list[:, None] == shard_list[None, :])
    rank = jnp.sum(earlier.astype(jnp.int32), axis=1)
    slot = shard_list * CAP + rank
    hits = jnp.arange(owners * CAP)[:, None] == slot[None, :]
    wanted = jnp.sum(jnp.where(hits, row_list[None, :], 0), axis=1).reshape(owners, CAP)
    asked = lax.all_to_all(wanted, "db", split_axis=0, concat_axis=0, tiled=True)
    return slot, asked.reshape(-1)


def shards(
    self_query,
    self_key,
    self_value,
    cross_query,
    retrieval_shard,
    retrieval_row,
    database,
    ffn_in,
    ffn_out,
    cross_projection,
):
    owners = lax.axis_size("db")
    count = lax.axis_size("seq")
    chips = count // 2
    place = lax.axis_index("seq")
    chip, core = place // 2, place % 2
    half = ffn_out.shape[0] // 2
    deep = ffn_out.shape[1]
    width = self_query.shape[1]

    part = jnp.concatenate(
        [
            lax.dynamic_slice_in_dim(ffn_in.T, core * half, half, 0),
            lax.dynamic_slice_in_dim(ffn_out, core * half, half, 0),
            lax.dynamic_slice_in_dim(cross_projection.T, core * HEAD_DIM, HEAD_DIM, 0),
        ],
        axis=0,
    )
    mine = lax.all_gather(part, "db", axis=0, tiled=True).reshape(owners, -1, deep)
    other = hop(mine, 0, 1)

    slot, asked = requests_of(retrieval_shard, retrieval_row)
    asked = jnp.clip(asked, 0, database.shape[0] - 1)
    found = fetch(asked, database)
    arrived = lax.all_to_all(found, "db", split_axis=0, concat_axis=0, tiled=True)

    ahead = lax.ppermute(cross_query[:STRETCH], "seq", [(i, i - 1) for i in range(1, count)])

    target = jnp.stack([((core ^ f) * chips + (chip + k) % chips) for k, f in HOPS])
    source = jnp.stack([((chip - k) % chips * 2 + (core ^ f)) for k, f in HOPS])
    parts = pack(target.astype(jnp.int32), self_query, self_key, self_value)
    parts = [parts[0]] + [hop(p, k, f) for p, (k, f) in zip(parts[1:], HOPS[1:])]
    done = self_attention(source.astype(jnp.int32), parts)
    back = [done[0]] + [hop(p, chips - k, f) for p, (k, f) in zip(done[1:], HOPS[1:])]
    self_attended = unpack(target.astype(jnp.int32), back)

    total, normed_in = ffn_first(slot, arrived, mine, half)
    normed_out = ffn_second(normed_in, total, other, half)
    own, sent = cross(
        core.reshape(1).astype(jnp.int32), normed_out, mine, other, cross_query, ahead, half
    )
    before = lax.ppermute(sent, "seq", [(i, i + 1) for i in range(count - 1)])
    last = jnp.arange(STRETCH)[:, None] == STRETCH - 1
    head = jnp.where(last, own[:STRETCH], before)
    cross_attended = lax.dynamic_update_slice(own, head, (0, 0))
    return (self_attended, cross_attended)


def solution(mesh):
    in_specs = (
        P(("db", "seq"), None),
        P(("db", "seq"), None),
        P(("db", "seq"), None),
        P(("db", "seq"), None),
        P(("db", "seq"), None),
        P(("db", "seq"), None),
        P("db", None, None),
        P(None, "db"),
        P("db", None),
        P(None, "db"),
    )
    out_specs = (P(("db", "seq"), None), P(("db", "seq"), None))
    return jax.shard_map(shards, mesh=mesh, in_specs=in_specs, out_specs=out_specs, check_vma=False)
```

time: 462 us -> 588 us (1.27)
  Pallas kernels: 0 us -> 391 us
  waiting for transfers between devices: 238 us -> 126 us
  matrix products: 99.4 us -> 0 us
  local copies, waits for them, and re-layouts: 49.1 us -> 7.04 us
  other arithmetic: 43.5 us -> 2.98 us
  starting transfers between devices: 17.1 us -> 34.4 us
  blocking collectives: 0 us -> 11.2 us
    pallas_call x0 -> x7, Pallas kernels: none -> 391 us  [the longest x1 145 us: pack(): pl.pallas_call(pack_kernel, grid_spec=pltpu.PrefetchScalarGridSpec(num_sc...]
    dot_general x6 -> x0, matrix products: 99.4 us -> none  [the longest x1 33.8 us: shards(): jnp.einsum('hqk,khd->hqd', block_probs.astype(jnp.bfloat16), values, pref...]
    all_to_all x1, waiting for transfers between devices: 64.8 us -> 0.01 us  [shards(): lax.all_to_all(found, 'db', split_axis=0, concat_axis=0, tiled=True)]
    all_gather x5 -> x1, waiting for transfers between devices: 134 us -> 81.8 us  [shards(): lax.all_gather(part, 'db', axis=0, tiled=True).reshape(owners, -1, deep)]
    reduce_sum x5 -> x2, other arithmetic: 29.1 us -> 0.27 us  [the longest x1 0.18 us: requests_of(): rank = jnp.sum(earlier.astype(jnp.int32), axis=1)]
    ppermute x1 -> x17, starting transfers between devices: 4.6 us -> 29.9 us  [the longest x15 25.7 us: hop(): return lax.ppermute(value, 'seq', pairs)]
    all_gather x1 -> x0, local copies, waits for them, and re-layouts: 16.6 us -> none  [shards(): lax.all_gather(self_value, 'seq', axis=0, tiled=True)]
    unnamed x22 -> x41, local copies, waits for them, and re-layouts: 16 us -> 2.09 us
  transfers between devices with their start and end apart: 8 -> 19, of which waited for: 6 -> 8; matrix products, arithmetic and copies ran while one was open for 29% -> 1% of each run, Pallas kernels for 0% -> 67%
where the time goes in v1:
time: 588 us
  Pallas kernels  391 us (66%)
  waiting for transfers between devices  126 us (21%)
  starting transfers between devices  34.4 us (6%)
  between operations  14.4 us (2%)
  blocking collectives  11.2 us (2%)
  local copies, waits for them, and re-layouts  7.04 us (1%)
    pallas_call x1, Pallas kernels, pack(): pl.pallas_call(pack_kernel, grid_spec=pltpu.PrefetchScalarGridSpec(num_sc...  145 us
    pallas_call x1, Pallas kernels, fetch(): pl.pallas_call(fetch_kernel, grid_spec=pltpu.PrefetchScalarGridSpec(num_s...  113 us
    all_gather x1, waiting for transfers between devices, shards(): lax.all_gather(part, 'db', axis=0, tiled=True).reshape(owners, -1, deep)  81.8 us
    pallas_call x1, Pallas kernels, unpack(): pl.pallas_call(unpack_kernel, grid_spec=pltpu.PrefetchScalarGridSpec(num_...  49.5 us
    ppermute x15, waiting for transfers between devices, hop(): return lax.ppermute(value, 'seq', pairs)  44.6 us
    pallas_call x1, Pallas kernels, cross(): pl.pallas_call(functools.partial(cross_kernel, first, LOG2E / math.sqrt(d...  36.6 us
    ppermute x15, starting transfers between devices, hop(): return lax.ppermute(value, 'seq', pairs)  25.7 us
    pallas_call x1, Pallas kernels, self_attention(): pl.pallas_call(functools.partial(self_kernel, LOG2E / math.sqrt(d)), grid...  20.5 us
  transfers between devices with their start and end apart: 19, of which 8 were waited for; matrix products, arithmetic and copies ran while one was open for 1% of the time, Pallas kernels for 67%

profile of v1, /device:TPU:1, one launch (start us, length us, event | category | flops | bytes accessed | tf_op | source)
XLA Modules:
  0.0 587.6 jit_solution(18185369672332273731)
XLA Ops:
  7.2 0.0 copy-start
  7.2 0.0 all-gather.2.cloned.1.call-start
  7.2 0.9 copy-done
  8.2 0.0 copy-start.8
  8.2 0.0 copy-start.9
  8.2 0.2 copy.30
  8.4 0.9 constant_dynamic-slice_fusion.1
  9.4 1.0 dynamic-slice_bitcast_fusion
  10.3 0.9 pad_maximum_fusion
  11.2 0.0 all-gather.2.cloned.1.call-update
  11.2 81.8 %all-gather.2.cloned.1.call-done = bf16[5632,896]{1,0:T(8,128)(2,1)} async-done(((bf16[352,896]{1,0:T(8,128)(2,1)}), bf16[5632,896]{1,0:T(8,128)(2,1)}) %all-gather.2.cloned.1.call-update) | async-done | bytes 10092560 | tf_op jit(solution)/shard_map/all_gather | solution.py:430
  93.1 0.7 collective-permute-start.14
  93.7 0.1 copy.26
  93.8 0.1 reshape.39
  93.9 0.1 copy.27
  94.0 0.1 broadcast_in_dim.27
  94.1 0.2 convert_reduce_fusion
  94.3 0.1 select_reduce_fusion
  94.4 0.1 all_to_all.9
  94.5 11.2 %all_to_all.14 = s32[16,1,2]{2,1,0:T(1,128)S(1)} all-to-all(s32[16,1,2]{2,1,0:T(1,128)S(1)} %bitcast.23), channel_id=1, replica_groups=mesh['db'=16,'seq'=8] {'db'}, dimensions={0} | all-to-all | bytes 256 | tf_op jit(solution)/shard_map/all_to_all | solution.py:397
  105.7 0.6 min.12.asked
  106.3 113.2 %fetch.1 = bf16[32,64,896]{2,1,0:T(8,128)(2,1)} custom-call(s32[32]{0:T(128)} %min.12.asked, bf16[32,64,896]{2,1,0:T(8,128)(2,1)} %database.1), custom_call_target="tpu_custom_call" | custom-call | bytes 7340032 | tf_op jit(solution)/shard_map/fetch/pallas_call | solution.py:62
  219.5 4.5 all-to-all-start.1
  224.2 0.6 stack.62.where
  224.8 144.9 %pack.1 = (bf16[3,384,256]{2,1,0:T(8,128)(2,1)}, bf16[3,384,256]{2,1,0:T(8,128)(2,1)}, bf16[3,384,256]{2,1,0:T(8,128)(2,1)}, bf16[3,384,256]{2,1,0:T(8,128)(2,1)...) custom-call(s32[8]{0:T(128)} %stack.62.where, ...), custom_call_target="tpu_custom_call" | custom-call | bytes 9437184 | tf_op jit(solution)/shard_map/pack/pallas_call | solution.py:281
  369.7 2.9 collective-permute-start
  372.7 1.7 collective-permute-start.1
  374.4 1.3 collective-permute-start.2
  375.6 1.4 collective-permute-start.3
  377.0 7.9 %collective-permute-done.refs_1_ = bf16[3,384,256]{2,1,0:T(8,128)(2,1)S(1)} collective-permute-done((bf16[3,384,256]{2,1,0:T(8,128)(2,1)}, bf16[3,384,256]{2,1,0:T(8,128)(2,1)S(1)}, u32[]{:S(2)}, u32[]{:S(2)}) %collective-permute-start) | collective-permute-done | bytes 589856 | tf_op jit(solution)/shard_map/ppermute | solution.py:36
  384.9 5.5 collective-permute-start.4
  390.5 10.7 %collective-permute-done.1.refs_2_ = bf16[3,384,256]{2,1,0:T(8,128)(2,1)S(1)} collective-permute-done((bf16[3,384,256]{2,1,0:T(8,128)(2,1)}, bf16[3,384,256]{2,1,0:T(8,128)(2,1)S(1)}, u32[]{:S(2)}, u32[]{:S(2)}) %collective-permute-start.1) | collective-permute-done | bytes 589856 | tf_op jit(solution)/shard_map/ppermute | solution.py:36
  401.2 0.6 collective-permute-start.5
  401.8 10.3 %collective-permute-done.2.refs_3_ = bf16[3,384,256]{2,1,0:T(8,128)(2,1)S(1)} collective-permute-done((bf16[3,384,256]{2,1,0:T(8,128)(2,1)}, bf16[3,384,256]{2,1,0:T(8,128)(2,1)S(1)}, u32[]{:S(2)}, u32[]{:S(2)}) %collective-permute-start.2) | collective-permute-done | bytes 589856 | tf_op jit(solution)/shard_map/ppermute | solution.py:36
  412.1 1.7 collective-permute-start.6
  413.8 1.0 slice.6
  414.8 0.6 stack.71.source
  415.4 2.2 collective-permute-start.15
  417.6 7.2 %collective-permute-done.4.refs_5_ = bf16[3,384,256]{2,1,0:T(8,128)(2,1)} collective-permute-done((bf16[3,384,256]{2,1,0:T(8,128)(2,1)}, bf16[3,384,256]{2,1,0:T(8,128)(2,1)}, u32[]{:S(2)}, u32[]{:S(2)}) %collective-permute-start.4) | collective-permute-done | bytes 589856 | tf_op jit(solution)/shard_map/ppermute | solution.py:36
  424.8 0.1 collective-permute-done.5.refs_6_
  424.9 0.0 collective-permute-done.6.refs_7_
  424.9 20.5 %causal.1 = (bf16[384,256]{1,0:T(8,128)(2,1)}, bf16[384,256]{1,0:T(8,128)(2,1)}, bf16[384,256]{1,0:T(8,128)(2,1)}, bf16[384,256]{1,0:T(8,128)(2,1)}, bf16[384,25...) custom-call(s32[8]{0:T(128)} %stack.71.source, ...), custom_call_target="tpu_custom_call" | custom-call | flops 7247757312 | bytes 8000000 | tf_op jit(solution)/shard_map/causal/pallas_call | solution.py:334
  445.4 2.9 collective-permute-start.7
  448.3 0.7 collective-permute-start.8
  449.0 2.6 collective-permute-start.9
  451.6 13.8 %ffn_first.1 = (f32[768,896]{1,0:T(8,128)}, bf16[768,896]{1,0:T(8,128)(2,1)}) custom-call(s32[12]{0:T(128)} %copy-done.18, bf16[32,64,896]{2,1,0:T(8,128)(2,1)} %all-to-all-done.1.arrived, bf16[16,352,896]{2,1,0:T(8,128)(2,1)} %bitcast.25), custom_call_target="tpu_custom_call" | custom-call | flops 4932501504 | bytes 16000000 | tf_op jit(solution)/shard_map/ffn_first/pallas_call | solution.py:126
  465.5 12.5 %ffn_second.1.normed = bf16[768,896]{1,0:T(8,128)(2,1)} custom-call(bf16[768,896]{1,0:T(8,128)(2,1)} %get-tuple-element.38.normed, f32[768,896]{1,0:T(8,128)} %get-tuple-element.39.before, bf16[16,352,896]{2,1,0:T(8,128)(2,1)} %collective-permute-done.14.gathered.other), custom_call_target="tpu_custom_call" | custom-call | flops 4932501504 | bytes 16000000 | tf_op jit(solution)/shard_map/ffn_second/pallas_call | solution.py:150
  478.0 36.6 %cross.1 = (bf16[384,2048]{1,0:T(8,128)(2,1)}, bf16[64,2048]{1,0:T(8,128)(2,1)}) custom-call(s32[1]{0:T(128)} %bitcast.16.core, bf16[768,896]{1,0:T(8,128)(2,1)} %ffn_second.1.normed, bf16[16,352,896]{2,1,0:T(8,128)(2,1)} %bitcast.26, bf16[16,352,896]{2,1,0:T(8,128)(2,1)} %collective-permute-done.14.gathered.other, bf16[384,2048]{1,0:T(8,128)(2,1)} %query.3, ...), custom_call_target="tpu_custom_call" | custom-call | flops 11274289152 | bytes 12000000 | tf_op jit(solution)/shard_map/cross/pallas_call | solution.py:229
  514.6 1.9 collective-permute-start.16
  516.5 0.3 collective-permute-start.10
  516.8 0.0 collective-permute-done.7.refs_1_
  516.8 3.2 collective-permute-start.11
  520.0 0.0 collective-permute-done.8.refs_2_
  520.0 0.1 collective-permute-start.12
  520.2 0.1 collective-permute-start.13
  520.3 6.1 %collective-permute-done.10.refs_4_ = bf16[384,256]{1,0:T(8,128)(2,1)S(1)} collective-permute-done((bf16[384,256]{1,0:T(8,128)(2,1)S(1)}, bf16[384,256]{1,0:T(8,128)(2,1)S(1)}, u32[]{:S(2)}, u32[]{:S(2)}) %collective-permute-start.10) | collective-permute-done | bytes 196640 | tf_op jit(solution)/shard_map/ppermute | solution.py:36
  526.4 0.0 collective-permute-done.11.refs_5_
  526.4 2.3 collective-permute-done.12.refs_6_
  528.7 0.0 collective-permute-done.13.refs_7_
  528.7 0.6 copy-done.6
  529.3 0.1 copy-done.7
  529.4 49.5 %unpack.1 = bf16[384,2048]{1,0:T(8,128)(2,1)} custom-call(s32[8]{0:T(128)} %stack.62.where, bf16[384,256]{1,0:T(8,128)(2,1)} %get-tuple-element.30.refs_0_, bf16[384,256]{1,0:T(8,128)(2,1)} %copy-done.1, bf16[384,256]{1,0:T(8,128)(2,1)} %copy-done.2, bf16[384,256]{1,0:T(8,128)(2,1)} %copy-done.3, bf16[384,256]{1,0:T(8,128)(2,1)} %copy-done.4, ...), custom_call_target="tpu_custom_call" | custom-call | bytes 3145728 | tf_op jit(solution)/shard_map/unpack/pallas_call | solution.py:371
  578.9 0.0 collective-permute-done.16
  578.9 1.8 select_dynamic-update-slice_fusion
  (41 shorter events, 0.1 us)
Async XLA Ops:
  7.2 1.0 copy-start
  7.2 85.9 %all-gather.2.cloned.1.call-start = ((), (), s32[]{:S(2)}) async-start(), calls=%async_computation.2 | async-start | bytes 10723328 | tf_op jit(solution)/shard_map/all_gather | solution.py:430
  8.2 85.5 %copy-start.8 = (s32[6,2]{0,1:T(2,128)S(1)}, s32[6,2]{0,1:T(2,128)}, u32[]{:S(2)}) copy-start(s32[6,2]{0,1:T(2,128)} %param.14) | copy-start | bytes 148
  8.2 85.7 %copy-start.9 = (s32[6,2]{0,1:T(2,128)S(1)}, s32[6,2]{0,1:T(2,128)}, u32[]{:S(2)}) copy-start(s32[6,2]{0,1:T(2,128)} %param.15) | copy-start | bytes 148
  93.1 372.4 %collective-permute-start.14 = (bf16[16,352,896]{2,1,0:T(8,128)(2,1)}, bf16[16,352,896]{2,1,0:T(8,128)(2,1)}, u32[]{:S(2)}, u32[]{:S(2)}) collective-permute-start(bf16[16,352,896]{2,1,0:T(8,128)(2,1)} %bitcast.24), channel_id=1, source_target_pairs={{0,1},{1,0},{2,3},{3,2},{4,5},{5,4},{6,7},{7,6},{8,9},{9,8},{10,11... | collective-permute-start | bytes 30277640 | tf_op jit(solution)/shard_map/ppermute | solution.py:36
  94.3 125.2 %copy-start.18 = (s32[12]{0:T(128)}, s32[12]{0:T(128)S(1)}, u32[]{:S(2)}) copy-start(s32[12]{0:T(128)S(1)} %multiply_add_fusion.slot) | copy-start | bytes 148
  219.5 232.1 %all-to-all-start.1 = ((bf16[32,64,896]{2,1,0:T(8,128)(2,1)}), bf16[32,64,896]{2,1,0:T(8,128)(2,1)}, u32[]{:S(2)}, u32[]{:S(2)}) async-start(bf16[32,64,896]{2,1,0:T(8,128)(2,1)} %fetch.1), calls=%async_computation.1 | async-start | bytes 7340032 | tf_op jit(solution)/shard_map/all_to_all | solution.py:436
  369.7 15.2 %collective-permute-start = (bf16[3,384,256]{2,1,0:T(8,128)(2,1)}, bf16[3,384,256]{2,1,0:T(8,128)(2,1)S(1)}, u32[]{:S(2)}, u32[]{:S(2)}) collective-permute-start(bf16[3,384,256]{2,1,0:T(8,128)(2,1)} %get-tuple-element.23), channel_id=1, source_target_pairs={{0,4},{1,5},{2,6},{3,7},{4,0},{5,1},{6,2},{7,3},{8,12},{9,13},{10,... | collective-permute-start | bytes 1769480 | tf_op jit(solution)/shard_map/ppermute | solution.py:36
  372.7 28.5 %collective-permute-start.1 = (bf16[3,384,256]{2,1,0:T(8,128)(2,1)}, bf16[3,384,256]{2,1,0:T(8,128)(2,1)S(1)}, u32[]{:S(2)}, u32[]{:S(2)}) collective-permute-start(bf16[3,384,256]{2,1,0:T(8,128)(2,1)} %get-tuple-element.24), channel_id=1, source_target_pairs={{0,5},{1,4},{2,7},{3,6},{4,1},{5,0},{6,3},{7,2},{8,13},{9,12},{10,... | collective-permute-start | bytes 1769480 | tf_op jit(solution)/shard_map/ppermute | solution.py:36
  374.4 37.7 %collective-permute-start.2 = (bf16[3,384,256]{2,1,0:T(8,128)(2,1)}, bf16[3,384,256]{2,1,0:T(8,128)(2,1)S(1)}, u32[]{:S(2)}, u32[]{:S(2)}) collective-permute-start(bf16[3,384,256]{2,1,0:T(8,128)(2,1)} %get-tuple-element.25), channel_id=1, source_target_pairs={{0,2},{1,3},{2,4},{3,5},{4,6},{5,7},{6,0},{7,1},{8,10},{9,11},{10,... | collective-permute-start | bytes 1769480 | tf_op jit(solution)/shard_map/ppermute | solution.py:36
  375.6 39.7 %collective-permute-start.3 = (bf16[3,384,256]{2,1,0:T(8,128)(2,1)}, bf16[3,384,256]{2,1,0:T(8,128)(2,1)S(1)}, u32[]{:S(2)}, u32[]{:S(2)}) collective-permute-start(bf16[3,384,256]{2,1,0:T(8,128)(2,1)} %get-tuple-element.26), channel_id=1, source_target_pairs={{0,6},{1,7},{2,0},{3,1},{4,2},{5,3},{6,4},{7,5},{8,14},{9,15},{10,... | collective-permute-start | bytes 1769480 | tf_op jit(solution)/shard_map/ppermute | solution.py:36
  384.9 40.0 %copy-start.10 = (bf16[3,384,256]{2,1,0:T(8,128)(2,1)}, bf16[3,384,256]{2,1,0:T(8,128)(2,1)S(1)}, u32[]{:S(2)}) copy-start(bf16[3,384,256]{2,1,0:T(8,128)(2,1)S(1)} %collective-permute-done.refs_1_) | copy-start | bytes 1769476
  384.9 39.9 %collective-permute-start.4 = (bf16[3,384,256]{2,1,0:T(8,128)(2,1)}, bf16[3,384,256]{2,1,0:T(8,128)(2,1)}, u32[]{:S(2)}, u32[]{:S(2)}) collective-permute-start(bf16[3,384,256]{2,1,0:T(8,128)(2,1)} %get-tuple-element.27), channel_id=1, source_target_pairs={{0,3},{1,2},{2,5},{3,4},{4,7},{5,6},{6,1},{7,0},{8,11},{9,10},{10,... | collective-permute-start | bytes 1769480 | tf_op jit(solution)/shard_map/ppermute | solution.py:36
  401.2 23.7 %copy-start.11 = (bf16[3,384,256]{2,1,0:T(8,128)(2,1)}, bf16[3,384,256]{2,1,0:T(8,128)(2,1)S(1)}, u32[]{:S(2)}) copy-start(bf16[3,384,256]{2,1,0:T(8,128)(2,1)S(1)} %collective-permute-done.1.refs_2_) | copy-start | bytes 1769476
  401.2 23.7 %collective-permute-start.5 = (bf16[3,384,256]{2,1,0:T(8,128)(2,1)}, bf16[3,384,256]{2,1,0:T(8,128)(2,1)}, u32[]{:S(2)}, u32[]{:S(2)}) collective-permute-start(bf16[3,384,256]{2,1,0:T(8,128)(2,1)} %get-tuple-element.28), channel_id=1, source_target_pairs={{0,7},{1,6},{2,1},{3,0},{4,3},{5,2},{6,5},{7,4},{8,15},{9,14},{10,... | collective-permute-start | bytes 1769480 | tf_op jit(solution)/shard_map/ppermute | solution.py:36
  412.1 12.8 %copy-start.12 = (bf16[3,384,256]{2,1,0:T(8,128)(2,1)}, bf16[3,384,256]{2,1,0:T(8,128)(2,1)S(1)}, u32[]{:S(2)}) copy-start(bf16[3,384,256]{2,1,0:T(8,128)(2,1)S(1)} %collective-permute-done.2.refs_3_) | copy-start | bytes 1769476
  412.1 12.8 %collective-permute-start.6 = (bf16[3,384,256]{2,1,0:T(8,128)(2,1)}, bf16[3,384,256]{2,1,0:T(8,128)(2,1)}, u32[]{:S(2)}, u32[]{:S(2)}) collective-permute-start(bf16[3,384,256]{2,1,0:T(8,128)(2,1)} %get-tuple-element.29), channel_id=1, source_target_pairs={{0,1},{1,0},{2,3},{3,2},{4,5},{5,4},{6,7},{7,6},{8,9},{9,8},{10,11... | collective-permute-start | bytes 1769480 | tf_op jit(solution)/shard_map/ppermute | solution.py:36
  415.4 9.5 %copy-start.13 = (bf16[3,384,256]{2,1,0:T(8,128)(2,1)}, bf16[3,384,256]{2,1,0:T(8,128)(2,1)S(1)}, u32[]{:S(2)}) copy-start(bf16[3,384,256]{2,1,0:T(8,128)(2,1)S(1)} %collective-permute-done.3.refs_4_) | copy-start | bytes 1769476
  415.4 62.6 %collective-permute-start.15 = (bf16[64,2048]{1,0:T(8,128)(2,1)S(1)}, bf16[64,2048]{1,0:T(8,128)(2,1)}, u32[]{:S(2)}, u32[]{:S(2)}) collective-permute-start(bf16[64,2048]{1,0:T(8,128)(2,1)S(1)} %slice.6), channel_id=1, source_target_pairs={{1,0},{2,1},{3,2},{4,3},{5,4},{6,5},{7,6},{9,8},{10,9},{11,10},{12... | collective-permute-start | bytes 786440 | tf_op jit(solution)/shard_map/ppermute | solution.py:438
  445.4 71.4 %collective-permute-start.7 = (bf16[384,256]{1,0:T(8,128)(2,1)}, bf16[384,256]{1,0:T(8,128)(2,1)S(1)}, u32[]{:S(2)}, u32[]{:S(2)}) collective-permute-start(bf16[384,256]{1,0:T(8,128)(2,1)} %get-tuple-element.31), channel_id=1, source_target_pairs={{0,4},{1,5},{2,6},{3,7},{4,0},{5,1},{6,2},{7,3},{8,12},{9,13},{10,... | collective-permute-start | bytes 589832 | tf_op jit(solution)/shard_map/ppermute | solution.py:36
  448.3 71.7 %collective-permute-start.8 = (bf16[384,256]{1,0:T(8,128)(2,1)}, bf16[384,256]{1,0:T(8,128)(2,1)S(1)}, u32[]{:S(2)}, u32[]{:S(2)}) collective-permute-start(bf16[384,256]{1,0:T(8,128)(2,1)} %get-tuple-element.32), channel_id=1, source_target_pairs={{0,5},{1,4},{2,7},{3,6},{4,1},{5,0},{6,3},{7,2},{8,13},{9,12},{10,... | collective-permute-start | bytes 589832 | tf_op jit(solution)/shard_map/ppermute | solution.py:36
  449.0 71.1 %collective-permute-start.9 = (bf16[384,256]{1,0:T(8,128)(2,1)}, bf16[384,256]{1,0:T(8,128)(2,1)S(1)}, u32[]{:S(2)}, u32[]{:S(2)}) collective-permute-start(bf16[384,256]{1,0:T(8,128)(2,1)} %get-tuple-element.33), channel_id=1, source_target_pairs={{0,6},{1,7},{2,0},{3,1},{4,2},{5,3},{6,4},{7,5},{8,14},{9,15},{10,... | collective-permute-start | bytes 589832 | tf_op jit(solution)/shard_map/ppermute | solution.py:36
  477.9 38.6 %copy-start.17 = (bf16[384,256]{1,0:T(8,128)(2,1)S(1)}, bf16[384,256]{1,0:T(8,128)(2,1)}, u32[]{:S(2)}) copy-start(bf16[384,256]{1,0:T(8,128)(2,1)} %get-tuple-element.34) | copy-start | bytes 589828
  477.9 38.9 %copy-start.16 = (bf16[384,256]{1,0:T(8,128)(2,1)S(1)}, bf16[384,256]{1,0:T(8,128)(2,1)}, u32[]{:S(2)}) copy-start(bf16[384,256]{1,0:T(8,128)(2,1)} %get-tuple-element.35) | copy-start | bytes 589828
  477.9 42.1 %copy-start.15 = (bf16[384,256]{1,0:T(8,128)(2,1)S(1)}, bf16[384,256]{1,0:T(8,128)(2,1)}, u32[]{:S(2)}) copy-start(bf16[384,256]{1,0:T(8,128)(2,1)} %get-tuple-element.36) | copy-start | bytes 589828
  477.9 42.2 %copy-start.14 = (bf16[384,256]{1,0:T(8,128)(2,1)S(1)}, bf16[384,256]{1,0:T(8,128)(2,1)}, u32[]{:S(2)}) copy-start(bf16[384,256]{1,0:T(8,128)(2,1)} %get-tuple-element.37) | copy-start | bytes 589828
  514.6 64.3 %collective-permute-start.16 = (bf16[64,2048]{1,0:T(8,128)(2,1)}, bf16[64,2048]{1,0:T(8,128)(2,1)S(1)}, u32[]{:S(2)}, u32[]{:S(2)}) collective-permute-start(bf16[64,2048]{1,0:T(8,128)(2,1)} %get-tuple-element.41), channel_id=1, source_target_pairs={{0,1},{1,2},{2,3},{3,4},{4,5},{5,6},{6,7},{8,9},{9,10},{10,11},{11... | collective-permute-start | bytes 786440 | tf_op jit(solution)/shard_map/ppermute | solution.py:453
  516.5 9.8 %collective-permute-start.10 = (bf16[384,256]{1,0:T(8,128)(2,1)S(1)}, bf16[384,256]{1,0:T(8,128)(2,1)S(1)}, u32[]{:S(2)}, u32[]{:S(2)}) collective-permute-start(bf16[384,256]{1,0:T(8,128)(2,1)S(1)} %copy-done.17), channel_id=1, source_target_pairs={{0,2},{1,3},{2,4},{3,5},{4,6},{5,7},{6,0},{7,1},{8,10},{9,11},{10,... | collective-permute-start | bytes 589832 | tf_op jit(solution)/shard_map/ppermute | solution.py:36
  516.8 11.9 %copy-start.1 = (bf16[384,256]{1,0:T(8,128)(2,1)}, bf16[384,256]{1,0:T(8,128)(2,1)S(1)}, u32[]{:S(2)}) copy-start(bf16[384,256]{1,0:T(8,128)(2,1)S(1)} %collective-permute-done.7.refs_1_) | copy-start | bytes 589828
  516.8 9.5 %collective-permute-start.11 = (bf16[384,256]{1,0:T(8,128)(2,1)S(1)}, bf16[384,256]{1,0:T(8,128)(2,1)S(1)}, u32[]{:S(2)}, u32[]{:S(2)}) collective-permute-start(bf16[384,256]{1,0:T(8,128)(2,1)S(1)} %copy-done.16), channel_id=1, source_target_pairs={{0,7},{1,6},{2,1},{3,0},{4,3},{5,2},{6,5},{7,4},{8,15},{9,14},{10,... | collective-permute-start | bytes 589832 | tf_op jit(solution)/shard_map/ppermute | solution.py:36
  520.0 8.6 %copy-start.2 = (bf16[384,256]{1,0:T(8,128)(2,1)}, bf16[384,256]{1,0:T(8,128)(2,1)S(1)}, u32[]{:S(2)}) copy-start(bf16[384,256]{1,0:T(8,128)(2,1)S(1)} %collective-permute-done.8.refs_2_) | copy-start | bytes 589828
  520.0 8.6 %collective-permute-start.12 = (bf16[384,256]{1,0:T(8,128)(2,1)S(1)}, bf16[384,256]{1,0:T(8,128)(2,1)S(1)}, u32[]{:S(2)}, u32[]{:S(2)}) collective-permute-start(bf16[384,256]{1,0:T(8,128)(2,1)S(1)} %copy-done.15), channel_id=1, source_target_pairs={{0,3},{1,2},{2,5},{3,4},{4,7},{5,6},{6,1},{7,0},{8,11},{9,10},{10,... | collective-permute-start | bytes 589832 | tf_op jit(solution)/shard_map/ppermute | solution.py:36
  520.1 8.6 %copy-start.3 = (bf16[384,256]{1,0:T(8,128)(2,1)}, bf16[384,256]{1,0:T(8,128)(2,1)S(1)}, u32[]{:S(2)}) copy-start(bf16[384,256]{1,0:T(8,128)(2,1)S(1)} %collective-permute-done.9.refs_3_) | copy-start | bytes 589828
  520.2 8.5 %collective-permute-start.13 = (bf16[384,256]{1,0:T(8,128)(2,1)S(1)}, bf16[384,256]{1,0:T(8,128)(2,1)S(1)}, u32[]{:S(2)}, u32[]{:S(2)}) collective-permute-start(bf16[384,256]{1,0:T(8,128)(2,1)S(1)} %copy-done.14), channel_id=1, source_target_pairs={{0,1},{1,0},{2,3},{3,2},{4,5},{5,4},{6,7},{7,6},{8,9},{9,8},{10,11... | collective-permute-start | bytes 589832 | tf_op jit(solution)/shard_map/ppermute | solution.py:36
  526.4 2.3 copy-start.4
  526.4 2.3 copy-start.5
  528.7 0.7 copy-start.6
  528.7 0.8 copy-start.7
Sparse Core Ops, SparseCore 0:
  11.3 81.6 all-gather.1

commit v2 on v0

v2 whole, which is shorter than its diff:
```python
import functools
import math

import jax
import jax.numpy as jnp
from jax import lax
from jax.experimental import pallas as pl
from jax.experimental.pallas import tpu as pltpu
from jax.sharding import PartitionSpec as P

HEADS = 16
HEAD_DIM = 128
STRETCH = 64
NEIGH = 2
CAP = 2
LOG2E = 1.4426950408889634
BF16 = jnp.bfloat16
F32 = jnp.float32
NT = (((1,), (1,)), ((), ()))
ANY = pl.BlockSpec(memory_space=pl.ANY)
VMEM = pl.BlockSpec(memory_space=pltpu.VMEM)
HOPS = ((0, 0), (2, 0), (2, 1), (1, 0), (3, 0), (1, 1), (3, 1), (0, 1))


def cost(flops, size, exps=0):
    return pl.CostEstimate(flops=int(flops), bytes_accessed=int(size), transcendentals=int(exps))


def params(mib=56, **more):
    return pltpu.CompilerParams(vmem_limit_bytes=mib << 20, **more)


def hop(value, chips, flip):
    count = lax.axis_size("seq")
    pairs = [(i, ((i + 2 * chips) % count) ^ flip) for i in range(count)]
    return lax.ppermute(value, "seq", pairs)


def run_copies(copies):
    for copy in copies:
        copy.start()
    for copy in copies:
        copy.wait()


def rms(wide):
    return wide * lax.rsqrt(jnp.mean(wide * wide, axis=-1, keepdims=True) + 1e-06)


def relay(reads, writes):
    for copy in reads:
        copy.start()
    for read, write in zip(reads, writes):
        read.wait()
        write.start()
    for copy in writes:
        copy.wait()


def fetch_kernel(asked, database, found, held, sem):
    last = database.shape[0] - 1
    count = found.shape[0]
    relay(
        [
            pltpu.make_async_copy(
                database.at[jnp.clip(asked[i], 0, last)], held.at[i], sem.at[0, i]
            )
            for i in range(count)
        ],
        [pltpu.make_async_copy(held.at[i], found.at[i], sem.at[1, i]) for i in range(count)],
    )


def fetch(asked, database):
    slots = asked.shape[0]
    shape = (slots, *database.shape[1:])
    return pl.pallas_call(
        fetch_kernel,
        grid_spec=pltpu.PrefetchScalarGridSpec(
            num_scalar_prefetch=1,
            grid=(1,),
            in_specs=[ANY],
            out_specs=ANY,
            scratch_shapes=[pltpu.VMEM(shape, BF16), pltpu.SemaphoreType.DMA((2, slots))],
        ),
        out_shape=jax.ShapeDtypeStruct(shape, BF16),
        cost_estimate=cost(0, 4 * math.prod(shape)),
        compiler_params=params(),
        name="fetch",
    )(asked, database)


def rows_of(gathered, target, first, sems, owner):
    size = target.shape[0] // gathered.shape[0]
    return pltpu.make_async_copy(
        gathered.at[owner, first : first + size, :],
        target.at[owner * size : (owner + 1) * size, :],
        sems.at[owner],
    )


def encode_kernel(
    first, slot, arrived, gathered, out, x, normed, w_in, w_out, hidden, x_sem, in_sem, out_sem
):
    tokens = arrived.shape[1]
    owners = gathered.shape[0]
    size = w_in.shape[0] // owners
    picks = [
        pltpu.make_async_copy(
            arrived.at[slot[i]], x.at[i * tokens : (i + 1) * tokens, :], x_sem.at[i]
        )
        for i in range(x.shape[0] // tokens)
    ]
    ins = [rows_of(gathered, w_in, first, in_sem, b) for b in range(owners)]
    outs = [rows_of(gathered, w_out, first + size, out_sem, b) for b in range(owners)]
    for copy in picks + ins + outs:
        copy.start()
    for copy in picks + ins + outs:
        copy.wait()
    normed[...] = rms(x[...].astype(F32)).astype(BF16)
    step = 512
    blocks = w_in.shape[0] // step

    def expand(j):
        rows = w_in[j * step : (j + 1) * step, :]
        return lax.dot_general(normed[...], rows, NT, preferred_element_type=F32)

    now = expand(0)
    for j in range(blocks):
        later = expand(j + 1) if j + 1 < blocks else None
        hidden[:, j * step : (j + 1) * step] = jax.nn.gelu(now, approximate=True).astype(BF16)
        now = later
    mixed = jnp.dot(hidden[...], w_out[...], preferred_element_type=F32)
    encoded = (x[...].astype(F32) + mixed).astype(BF16).astype(F32)
    out[...] = rms(encoded).astype(BF16)


def encode(slot, arrived, gathered, first, size):
    requests = slot.shape[0]
    rows, deep = requests * arrived.shape[1], arrived.shape[2]
    owners = gathered.shape[0]
    return pl.pallas_call(
        functools.partial(encode_kernel, first),
        grid_spec=pltpu.PrefetchScalarGridSpec(
            num_scalar_prefetch=1,
            grid=(1,),
            in_specs=[ANY, ANY],
            out_specs=pl.BlockSpec((rows, deep), lambda i, s: (0, 0)),
            scratch_shapes=[
                pltpu.VMEM((rows, deep), BF16),
                pltpu.VMEM((rows, deep), BF16),
                pltpu.VMEM((owners * size, deep), BF16),
                pltpu.VMEM((owners * size, deep), BF16),
                pltpu.VMEM((rows, owners * size), BF16),
                pltpu.SemaphoreType.DMA((requests,)),
                pltpu.SemaphoreType.DMA((owners,)),
                pltpu.SemaphoreType.DMA((owners,)),
            ],
        ),
        out_shape=jax.ShapeDtypeStruct((rows, deep), BF16),
        cost_estimate=cost(4 * rows * deep * owners * size, 16e6, rows * owners * size),
        compiler_params=params(),
        name="encode",
    )(slot, arrived, gathered)


def attend(queries, keys, values, allowed, scale):
    scores = [
        jnp.where(allowed, lax.dot_general(q, k, NT, preferred_element_type=F32), -jnp.inf)
        for q, k in zip(queries, keys)
    ]
    scores = jnp.concatenate(scores, axis=0)
    probs = jnp.exp2((scores - jnp.max(scores, axis=-1, keepdims=True)) * scale)
    total = jnp.sum(probs, axis=-1, keepdims=True)
    probs = probs.astype(BF16)
    rows = queries[0].shape[0]
    summed = [
        jnp.dot(probs[n * rows : (n + 1) * rows], v, preferred_element_type=F32)
        for n, v in enumerate(values)
    ]
    return jnp.concatenate(summed, axis=0) / total


def cross_kernel(scale, normed, gathered, query, out, sent, weights, sem):
    d = HEAD_DIM
    span = NEIGH * STRETCH
    groups = gathered.shape[0] // 2
    copies = [
        [
            pltpu.make_async_copy(
                gathered.at[part * groups + j, : 2 * d, :],
                weights.at[j, part * 2 * d : (part + 1) * 2 * d, :],
                sem.at[j, part],
            )
            for part in range(2)
        ]
        for j in range(groups)
    ]
    for pair in copies:
        for copy in pair:
            copy.start()
    for pair in copies:
        for copy in pair:
            copy.wait()
    at_row = lax.broadcasted_iota(jnp.int32, (2 * STRETCH, 2 * span), 0)
    at_key = lax.broadcasted_iota(jnp.int32, (2 * STRETCH, 2 * span), 1)
    allowed = (at_row >= STRETCH) == (at_key >= span)
    blocks = range(normed.shape[0] // (2 * span))

    def project(j):
        return lax.dot_general(
            normed[...], weights[j], NT, preferred_element_type=F32
        ).astype(BF16)

    pairs = project(0)
    for j in range(groups):
        later = project(j + 1) if j + 1 < groups else None
        for t in range(2):
            lanes = slice((2 * j + t) * d, (2 * j + t + 1) * d)
            result = attend(
                [query[2 * b * STRETCH : 2 * (b + 1) * STRETCH, lanes] for b in blocks],
                [pairs[2 * b * span : 2 * (b + 1) * span, t * d : (t + 1) * d] for b in blocks],
                [pairs[2 * b * span : 2 * (b + 1) * span, (2 + t) * d : (3 + t) * d] for b in blocks],
                allowed,
                scale,
            )
            result = pltpu.roll(result, STRETCH - 1, 0)
            out[:, lanes] = result.astype(BF16)
            sent[:, lanes] = result[:STRETCH].astype(BF16)
        pairs = later


def cross(normed, gathered, query):
    rows, width = query.shape
    d = HEAD_DIM
    deep = normed.shape[1]
    groups = gathered.shape[0] // 2
    return pl.pallas_call(
        functools.partial(cross_kernel, LOG2E / math.sqrt(d)),
        in_specs=[VMEM, ANY, VMEM],
        out_specs=[VMEM, VMEM],
        out_shape=[
            jax.ShapeDtypeStruct(query.shape, BF16),
            jax.ShapeDtypeStruct((STRETCH, width), BF16),
        ],
        scratch_shapes=[
            pltpu.VMEM((groups, 4 * d, deep), BF16),
            pltpu.SemaphoreType.DMA((groups, 2)),
        ],
        cost_estimate=cost(4 * normed.shape[0] * deep * width, 12e6, 2 * rows * width),
        compiler_params=params(),
        name="cross",
    )(normed, gathered, query)


def mend_kernel(own, before, out):
    last = lax.broadcasted_iota(jnp.int32, own.shape, 0) == STRETCH - 1
    out[...] = jnp.where(last, own[...].astype(F32), before[...].astype(F32)).astype(BF16)


def mend(own, before):
    block = pl.BlockSpec(before.shape, lambda i: (0, 0))
    return pl.pallas_call(
        mend_kernel,
        grid=(1,),
        in_specs=[block, block],
        out_specs=block,
        out_shape=jax.ShapeDtypeStruct(own.shape, BF16),
        input_output_aliases={0: 0},
        cost_estimate=cost(0, 6 * math.prod(before.shape)),
        compiler_params=params(),
        name="mend",
    )(own, before)


def partners(chips):
    place = lax.axis_index("seq")
    chip, core = lax.div(place, 2), lax.rem(place, 2)
    reached, reaching = [], []
    for k, f in HOPS:
        side = 1 - core if f else core
        reached.append(side * chips + lax.rem(chip + k, chips))
        reaching.append(lax.rem(chip + chips - k, chips) * 2 + side)
    return reached, reaching


def pack_kernel(chips, query, key, value, *rest):
    count = len(HOPS)
    parts, held, sem = rest[:count], rest[count], rest[count + 1]
    block = parts[0].shape[2]
    reached, _ = partners(chips)
    reads, writes = [], []
    for n in (*range(1, count), 0):
        columns = pl.ds(pl.multiple_of(reached[n] * block, block), block)
        for a, source in enumerate((query, key, value)):
            reads.append(
                pltpu.make_async_copy(source.at[:, columns], held.at[n, a], sem.at[0, n, a])
            )
            writes.append(pltpu.make_async_copy(held.at[n, a], parts[n].at[a], sem.at[1, n, a]))
    relay(reads, writes)


def pack(chips, query, key, value):
    rows, width = query.shape
    count = len(HOPS)
    shape = (3, rows, width // count)
    return pl.pallas_call(
        functools.partial(pack_kernel, chips),
        in_specs=[ANY] * 3,
        out_specs=[ANY] * count,
        scratch_shapes=[pltpu.VMEM((count, *shape), BF16), pltpu.SemaphoreType.DMA((2, count, 3))],
        out_shape=[jax.ShapeDtypeStruct(shape, BF16)] * count,
        cost_estimate=cost(0, 12 * rows * width),
        compiler_params=params(),
        name="pack",
    )(query, key, value)


def self_kernel(chips, scale, *refs):
    count = len(HOPS)
    _, source = partners(chips)
    parts, outs = refs[:count], refs[count : 2 * count]
    query, key, value, result = refs[2 * count :]
    rows = parts[0].shape[1]
    d = HEAD_DIM
    for n in range(count):
        place = pl.ds(pl.multiple_of(source[n] * rows, rows), rows)
        query[place, :] = parts[n][0]
        key[place, :] = parts[n][1]
        value[place, :d] = parts[n][2]
    value[:, d:] = jnp.ones((count * rows, d), BF16)
    at_row = lax.broadcasted_iota(jnp.int32, (rows, rows), 0)
    at_key = lax.broadcasted_iota(jnp.int32, (rows, rows), 1)
    allowed = at_key <= at_row
    for i in range(count):
        low, high = i * rows, (i + 1) * rows
        block = query[low:high, :]
        scores = lax.dot_general(block, key[low:high, :], NT, preferred_element_type=F32)
        scores = jnp.where(allowed, scores, -jnp.inf)
        if i:
            left = lax.dot_general(block, key[:low, :], NT, preferred_element_type=F32)
            scores = jnp.concatenate([left, scores], axis=1)
        best = jnp.max(scores, axis=-1, keepdims=True)
        probs = jnp.exp2((scores - best) * scale).astype(BF16)
        summed = jnp.dot(probs, value[:high, :], preferred_element_type=F32)
        result[low:high, :] = (summed[:, :d] / summed[:, d:]).astype(BF16)
    for n in range(count):
        place = pl.ds(pl.multiple_of(source[n] * rows, rows), rows)
        outs[n][...] = result[place, :]


def self_attention(chips, parts):
    count = len(HOPS)
    _, rows, width = parts[0].shape
    d = HEAD_DIM
    length = count * rows
    return pl.pallas_call(
        functools.partial(self_kernel, chips, LOG2E / math.sqrt(d)),
        grid=(width // d,),
        in_specs=[pl.BlockSpec((3, rows, d), lambda h: (0, 0, h))] * count,
        out_specs=[pl.BlockSpec((rows, d), lambda h: (0, h))] * count,
        scratch_shapes=[
            pltpu.VMEM((length, d), BF16),
            pltpu.VMEM((length, d), BF16),
            pltpu.VMEM((length, 2 * d), BF16),
            pltpu.VMEM((length, d), BF16),
        ],
        out_shape=[jax.ShapeDtypeStruct((rows, width), BF16)] * count,
        cost_estimate=cost(3 * length * length * d * 2, 8e6, length * length),
        compiler_params=params(),
        name="causal",
    )(*parts)


def unpack_kernel(chips, *refs):
    parts, out = refs[:-1], refs[-1]
    block = parts[0].shape[1]
    reached, _ = partners(chips)
    for n, part in enumerate(parts):
        out[:, pl.ds(pl.multiple_of(reached[n] * block, block), block)] = part[...]


def unpack(chips, parts):
    rows, block = parts[0].shape
    count = len(parts)
    return pl.pallas_call(
        functools.partial(unpack_kernel, chips),
        in_specs=[VMEM] * count,
        out_specs=VMEM,
        out_shape=jax.ShapeDtypeStruct((rows, block * count), BF16),
        cost_estimate=cost(0, 4 * rows * block * count),
        compiler_params=params(),
        name="unpack",
    )(*parts)


def requests_of(retrieval_shard, retrieval_row):
    shard_list = retrieval_shard.reshape(-1)
    row_list = retrieval_row.reshape(-1)
    owners = lax.axis_size("db")
    order = jnp.arange(shard_list.shape[0])
    earlier = (order[:, None] > order[None, :]) & (shard_list[:, None] == shard_list[None, :])
    rank = jnp.sum(earlier.astype(jnp.int32), axis=1)
    slot = shard_list * CAP + rank
    hits = jnp.arange(owners * CAP)[:, None] == slot[None, :]
    wanted = jnp.sum(jnp.where(hits, row_list[None, :], 0), axis=1).reshape(owners, CAP)
    return slot, wanted


def shards(
    self_query,
    self_key,
    self_value,
    cross_query,
    retrieval_shard,
    retrieval_row,
    database,
    ffn_in,
    ffn_out,
    cross_projection,
):
    owners = lax.axis_size("db")
    count = lax.axis_size("seq")
    chips = count // 2
    size, deep = ffn_out.shape
    together = lax.optimization_barrier

    weights = jnp.concatenate([cross_projection.T, ffn_in.T, ffn_out], axis=0)
    share = weights.shape[0] // count
    part = lax.dynamic_slice_in_dim(weights, lax.axis_index("seq") * share, share, 0)
    gathered = lax.all_gather(part, ("db", "seq"), axis=0, tiled=True).reshape(owners, -1, deep)

    slot, wanted = requests_of(retrieval_shard, retrieval_row)
    asked = lax.all_to_all(wanted, "db", split_axis=0, concat_axis=0, tiled=True)
    self_query, self_key, self_value, _ = together((self_query, self_key, self_value, wanted))
    parts = pack(chips, self_query, self_key, self_value)
    asked, *parts = together((asked, *parts))
    parts = [parts[0]] + [hop(p, k, f) for p, (k, f) in zip(parts[1:], HOPS[1:])]

    found = fetch(asked.reshape(-1), database)
    arrived = lax.all_to_all(found, "db", split_axis=0, concat_axis=0, tiled=True)
    ahead = lax.ppermute(cross_query[:STRETCH], "seq", [(i, i - 1) for i in range(1, count)])

    done = self_attention(chips, parts)
    back = [done[0]] + [hop(p, chips - k, f) for p, (k, f) in zip(done[1:], HOPS[1:])]

    shifted = jnp.concatenate([cross_query[STRETCH - 1 :], ahead[: STRETCH - 1]], axis=0)
    gathered, shifted, arrived, *back = together((gathered, shifted, arrived, *back))
    normed = encode(slot, arrived, gathered, cross_projection.shape[1], size)
    own, sent = cross(normed, gathered, shifted)
    before = lax.ppermute(sent, "seq", [(i, i + 1) for i in range(count - 1)])
    own, *back = together((own, *back))
    self_attended = unpack(chips, back)
    cross_attended = mend(own, before)
    return (self_attended, cross_attended)


def solution(mesh):
    in_specs = (
        P(("db", "seq"), None),
        P(("db", "seq"), None),
        P(("db", "seq"), None),
        P(("db", "seq"), None),
        P(("db", "seq"), None),
        P(("db", "seq"), None),
        P("db", None, None),
        P(None, "db"),
        P("db", None),
        P(None, "db"),
    )
    out_specs = (P(("db", "seq"), None), P(("db", "seq"), None))
    return jax.shard_map(shards, mesh=mesh, in_specs=in_specs, out_specs=out_specs, check_vma=False)
```

time: 462 us -> 201 us (0.44)
  waiting for transfers between devices: 238 us -> 55.9 us
  matrix products: 99.4 us -> 0 us
  Pallas kernels: 0 us -> 72.8 us
  local copies, waits for them, and re-layouts: 49.1 us -> 5.02 us
  other arithmetic: 43.5 us -> 2.46 us
  starting transfers between devices: 17.1 us -> 50.4 us
    all_gather x5 -> x1, waiting for transfers between devices: 134 us -> 0.01 us  [shards(): lax.all_gather(part, ('db', 'seq'), axis=0, tiled=True)]
    dot_general x6 -> x0, matrix products: 99.4 us -> none  [the longest x1 33.8 us: shards(): jnp.einsum('hqk,khd->hqd', block_probs.astype(jnp.bfloat16), values, pref...]
    pallas_call x0 -> x7, Pallas kernels: none -> 72.8 us  [the longest x1 19.8 us: self_attention(): pl.pallas_call(functools.partial(self_kernel, chips, LOG2E / math.sqrt(d)...]
    all_to_all x1, waiting for transfers between devices: 64.8 us -> 0.01 us  [shards(): lax.all_to_all(found, 'db', split_axis=0, concat_axis=0, tiled=True)]
    ppermute x1 -> x16, starting transfers between devices: 4.6 us -> 37.4 us  [the longest x14 30.6 us: hop(): return lax.ppermute(value, 'seq', pairs)]
    reduce_sum x5 -> x2, other arithmetic: 29.1 us -> 0.27 us  [the longest x1 0.18 us: requests_of(): rank = jnp.sum(earlier.astype(jnp.int32), axis=1)]
    ppermute x1 -> x16, waiting for transfers between devices: 31.2 us -> 54.4 us  [the longest x14 53.7 us: hop(): return lax.ppermute(value, 'seq', pairs)]
    all_gather x1 -> x0, local copies, waits for them, and re-layouts: 16.6 us -> none  [shards(): lax.all_gather(self_value, 'seq', axis=0, tiled=True)]
  transfers between devices with their start and end apart: 8 -> 19, of which waited for: 6 -> 11; matrix products, arithmetic and copies ran while one was open for 29% -> 2% of each run, Pallas kernels for 0% -> 17%
where the time goes in v2:
time: 201 us
  Pallas kernels  72.8 us (36%)
  waiting for transfers between devices  55.9 us (28%)
  starting transfers between devices  50.4 us (25%)
  between operations  14.4 us (7%)
  local copies, waits for them, and re-layouts  5.02 us (2%)
  other arithmetic  2.46 us (1%)
    ppermute x14, waiting for transfers between devices, hop(): return lax.ppermute(value, 'seq', pairs)  53.7 us
    ppermute x14, starting transfers between devices, hop(): return lax.ppermute(value, 'seq', pairs)  30.6 us
    pallas_call x1, Pallas kernels, self_attention(): pl.pallas_call(functools.partial(self_kernel, chips, LOG2E / math.sqrt(d)...  19.8 us
    pallas_call x1, Pallas kernels, encode(): pl.pallas_call(functools.partial(encode_kernel, first), grid_spec=pltpu.P...  19.4 us
    pallas_call x1, Pallas kernels, cross(): pl.pallas_call(functools.partial(cross_kernel, LOG2E / math.sqrt(d)), in_...  17.9 us
    all_to_all x1, starting transfers between devices, shards(): lax.all_to_all(wanted, 'db', split_axis=0, concat_axis=0, tiled=True)  7.58 us
    pallas_call x1, Pallas kernels, fetch(): pl.pallas_call(fetch_kernel, grid_spec=pltpu.PrefetchScalarGridSpec(num_s...  6.3 us
    all_to_all x1, starting transfers between devices, shards(): lax.all_to_all(found, 'db', split_axis=0, concat_axis=0, tiled=True)  5.42 us
  transfers between devices with their start and end apart: 19, of which 11 were waited for; matrix products, arithmetic and copies ran while one was open for 2% of the time, Pallas kernels for 17%

profile of v2, /device:TPU:1, one launch (start us, length us, event | category | flops | bytes accessed | tf_op | source)
XLA Modules:
  0.0 201.0 jit_solution(11669862397635286664)
XLA Ops:
  7.2 0.0 copy-start.9
  7.2 0.0 all-gather.2.cloned.1.call-start
  7.2 1.3 copy.34
  8.5 0.8 fusion.1
  9.3 0.0 all-gather.2.cloned.1.call-update
  9.3 0.1 copy.33
  9.4 0.1 reshape.28
  9.5 0.1 copy.35
  9.6 0.1 broadcast_in_dim.18
  9.7 0.2 convert_reduce_fusion
  9.9 0.1 select_reduce_fusion
  10.0 0.7 all_to_all.11
  10.7 7.6 %all-to-all-start = ((s32[16,1,2]{2,1,0:T(1,128)}), s32[16,1,2]{2,1,0:T(1,128)S(1)}, u32[]{:S(2)}, u32[]{:S(2)}) async-start(s32[16,1,2]{2,1,0:T(1,128)} %bitcast.3), calls=%async_computation | async-start | bytes 16384 | tf_op jit(solution)/shard_map/all_to_all | solution.py:434
  18.3 4.8 %pack.1 = (bf16[3,384,256]{2,1,0:T(8,128)(2,1)}, bf16[3,384,256]{2,1,0:T(8,128)(2,1)}, bf16[3,384,256]{2,1,0:T(8,128)(2,1)}, bf16[3,384,256]{2,1,0:T(8,128)(2,1)...) custom-call(bf16[384,2048]{1,0:T(8,128)(2,1)} %query, ...), custom_call_target="tpu_custom_call" | custom-call | bytes 9437184 | tf_op jit(solution)/shard_map/pack/pallas_call | solution.py:307
  23.1 1.4 all-to-all-done
  24.5 0.1 copy.37
  24.6 0.1 copy.38
  24.7 0.6 reshape.30.asked
  25.3 6.3 %fetch.1 = bf16[32,64,896]{2,1,0:T(8,128)(2,1)} custom-call(s32[32]{0:T(128)} %reshape.30.asked, bf16[32,64,896]{2,1,0:T(8,128)(2,1)} %database.1), custom_call_target="tpu_custom_call" | custom-call | bytes 7340032 | tf_op jit(solution)/shard_map/fetch/pallas_call | solution.py:77
  31.7 0.0 copy-start
  31.7 5.4 %all-to-all-start.1 = ((bf16[32,64,896]{2,1,0:T(8,128)(2,1)}), bf16[32,64,896]{2,1,0:T(8,128)(2,1)}, u32[]{:S(2)}, u32[]{:S(2)}) async-start(bf16[32,64,896]{2,1,0:T(8,128)(2,1)} %fetch.1), calls=%async_computation.1 | async-start | bytes 7340032 | tf_op jit(solution)/shard_map/all_to_all | solution.py:441
  37.1 4.6 %collective-permute-start.1 = (bf16[3,384,256]{2,1,0:T(8,128)(2,1)}, bf16[3,384,256]{2,1,0:T(8,128)(2,1)S(1)}, u32[]{:S(2)}, u32[]{:S(2)}) collective-permute-start(bf16[3,384,256]{2,1,0:T(8,128)(2,1)} %get-tuple-element.65), channel_id=1, source_target_pairs={{0,4},{1,5},{2,6},{3,7},{4,0},{5,1},{6,2},{7,3},{8,12},{9,13},{10,... | collective-permute-start | bytes 1769480 | tf_op jit(solution)/shard_map/ppermute | solution.py:36
  41.7 1.8 collective-permute-start.2
  43.5 0.8 collective-permute-start.3
  44.2 2.4 %collective-permute-start.4 = (bf16[3,384,256]{2,1,0:T(8,128)(2,1)}, bf16[3,384,256]{2,1,0:T(8,128)(2,1)S(1)}, u32[]{:S(2)}, u32[]{:S(2)}) collective-permute-start(bf16[3,384,256]{2,1,0:T(8,128)(2,1)} %get-tuple-element.68), channel_id=1, source_target_pairs={{0,6},{1,7},{2,0},{3,1},{4,2},{5,3},{6,4},{7,5},{8,14},{9,15},{10,... | collective-permute-start | bytes 1769480 | tf_op jit(solution)/shard_map/ppermute | solution.py:36
  46.7 0.0 collective-permute-start.5
  46.7 9.4 %collective-permute-done.1.refs_1_ = bf16[3,384,256]{2,1,0:T(8,128)(2,1)S(1)} collective-permute-done((bf16[3,384,256]{2,1,0:T(8,128)(2,1)}, bf16[3,384,256]{2,1,0:T(8,128)(2,1)S(1)}, u32[]{:S(2)}, u32[]{:S(2)}) %collective-permute-start.1) | collective-permute-done | bytes 589856 | tf_op jit(solution)/shard_map/ppermute | solution.py:36
  56.1 8.7 %collective-permute-start.6 = (bf16[3,384,256]{2,1,0:T(8,128)(2,1)S(1)}, bf16[3,384,256]{2,1,0:T(8,128)(2,1)S(1)}, u32[]{:S(2)}, u32[]{:S(2)}) collective-permute-start(bf16[3,384,256]{2,1,0:T(8,128)(2,1)S(1)} %copy-done.12), channel_id=1, source_target_pairs={{0,7},{1,6},{2,1},{3,0},{4,3},{5,2},{6,5},{7,4},{8,15},{9,14},{10,... | collective-permute-start | bytes 1769480 | tf_op jit(solution)/shard_map/ppermute | solution.py:36
  64.8 9.1 %collective-permute-done.2.refs_2_ = bf16[3,384,256]{2,1,0:T(8,128)(2,1)S(1)} collective-permute-done((bf16[3,384,256]{2,1,0:T(8,128)(2,1)}, bf16[3,384,256]{2,1,0:T(8,128)(2,1)S(1)}, u32[]{:S(2)}, u32[]{:S(2)}) %collective-permute-start.2) | collective-permute-done | bytes 589856 | tf_op jit(solution)/shard_map/ppermute | solution.py:36
  73.9 1.0 collective-permute-start.7
  75.0 12.8 %collective-permute-done.3.refs_3_ = bf16[3,384,256]{2,1,0:T(8,128)(2,1)S(1)} collective-permute-done((bf16[3,384,256]{2,1,0:T(8,128)(2,1)}, bf16[3,384,256]{2,1,0:T(8,128)(2,1)S(1)}, u32[]{:S(2)}, u32[]{:S(2)}) %collective-permute-start.3) | collective-permute-done | bytes 589856 | tf_op jit(solution)/shard_map/ppermute | solution.py:36
  87.8 4.2 %collective-permute-start = (bf16[64,2048]{1,0:T(8,128)(2,1)S(1)}, bf16[64,2048]{1,0:T(8,128)(2,1)S(1)}, u32[]{:S(2)}, u32[]{:S(2)}) collective-permute-start(bf16[64,2048]{1,0:T(8,128)(2,1)S(1)} %slice.10), channel_id=1, source_target_pairs={{1,0},{2,1},{3,2},{4,3},{5,4},{6,5},{7,6},{9,8},{10,9},{11,10},{12... | collective-permute-start | bytes 786440 | tf_op jit(solution)/shard_map/ppermute | solution.py:442
  91.9 0.0 collective-permute-done.4.refs_4_
  92.0 8.4 %collective-permute-done.5.refs_5_ = bf16[3,384,256]{2,1,0:T(8,128)(2,1)S(1)} collective-permute-done((bf16[3,384,256]{2,1,0:T(8,128)(2,1)S(1)}, bf16[3,384,256]{2,1,0:T(8,128)(2,1)S(1)}, u32[]{:S(2)}, u32[]{:S(2)}) %collective-permute-start.5) | collective-permute-done | bytes 589856 | tf_op jit(solution)/shard_map/ppermute | solution.py:36
  100.4 0.5 collective-permute-done.6.refs_6_
  100.9 0.0 collective-permute-done.7.refs_7_
  101.0 0.3 copy-done.18
  101.2 0.5 copy-done.19
  101.8 19.8 %causal.1 = (bf16[384,256]{1,0:T(8,128)(2,1)}, bf16[384,256]{1,0:T(8,128)(2,1)}, bf16[384,256]{1,0:T(8,128)(2,1)}, bf16[384,256]{1,0:T(8,128)(2,1)}, bf16[384,25...) custom-call(bf16[3,384,256]{2,1,0:T(8,128)(2,1)} %get-tuple-element.64.refs_0_, ...), custom_call_target="tpu_custom_call" | custom-call | flops 7247757312 | bytes 8000000 | tf_op jit(solution)/shard_map/causal/pallas_call | solution.py:357
  121.6 2.8 %collective-permute-start.10 = (bf16[384,256]{1,0:T(8,128)(2,1)}, bf16[384,256]{1,0:T(8,128)(2,1)S(1)}, u32[]{:S(2)}, u32[]{:S(2)}) collective-permute-start(bf16[384,256]{1,0:T(8,128)(2,1)} %get-tuple-element.75), channel_id=1, source_target_pairs={{0,6},{1,7},{2,0},{3,1},{4,2},{5,3},{6,4},{7,5},{8,14},{9,15},{10,... | collective-permute-start | bytes 589832 | tf_op jit(solution)/shard_map/ppermute | solution.py:36
  124.4 0.0 collective-permute-start.11
  124.4 0.3 slice.9
  124.8 3.5 %collective-permute-start.12 = (bf16[384,256]{1,0:T(8,128)(2,1)S(1)}, bf16[384,256]{1,0:T(8,128)(2,1)S(1)}, u32[]{:S(2)}, u32[]{:S(2)}) collective-permute-start(bf16[384,256]{1,0:T(8,128)(2,1)S(1)} %copy-done.24), channel_id=1, source_target_pairs={{0,7},{1,6},{2,1},{3,0},{4,3},{5,2},{6,5},{7,4},{8,15},{9,14},{10,... | collective-permute-start | bytes 589832 | tf_op jit(solution)/shard_map/ppermute | solution.py:36
  128.3 0.0 collective-permute-start.13
  128.3 0.0 collective-permute-done
  128.3 0.1 collective-permute-start.14
  128.4 4.5 %collective-permute-done.10.refs_3_ = bf16[384,256]{1,0:T(8,128)(2,1)S(1)} collective-permute-done((bf16[384,256]{1,0:T(8,128)(2,1)}, bf16[384,256]{1,0:T(8,128)(2,1)S(1)}, u32[]{:S(2)}, u32[]{:S(2)}) %collective-permute-start.10) | collective-permute-done | bytes 196640 | tf_op jit(solution)/shard_map/ppermute | solution.py:36
  132.8 3.1 %collective-permute-start.8 = (bf16[384,256]{1,0:T(8,128)(2,1)S(1)}, bf16[384,256]{1,0:T(8,128)(2,1)S(1)}, u32[]{:S(2)}, u32[]{:S(2)}) collective-permute-start(bf16[384,256]{1,0:T(8,128)(2,1)S(1)} %copy-done.21), channel_id=1, source_target_pairs={{0,4},{1,5},{2,6},{3,7},{4,0},{5,1},{6,2},{7,3},{8,12},{9,13},{10,... | collective-permute-start | bytes 589832 | tf_op jit(solution)/shard_map/ppermute | solution.py:36
  136.0 0.0 collective-permute-done.11.refs_4_
  136.0 1.8 collective-permute-start.9
  137.8 1.4 pad_maximum_fusion.query
  139.1 0.7 collective-permute-done.12.refs_5_
  139.9 0.0 collective-permute-done.13.refs_6_
  139.9 0.0 collective-permute-done.14.refs_7_
  139.9 3.9 %collective-permute-done.8.refs_1_ = bf16[384,256]{1,0:T(8,128)(2,1)S(1)} collective-permute-done((bf16[384,256]{1,0:T(8,128)(2,1)S(1)}, bf16[384,256]{1,0:T(8,128)(2,1)S(1)}, u32[]{:S(2)}, u32[]{:S(2)}) %collective-permute-start.8) | collective-permute-done | bytes 196640 | tf_op jit(solution)/shard_map/ppermute | solution.py:36
  143.8 4.3 %collective-permute-done.9.refs_2_ = bf16[384,256]{1,0:T(8,128)(2,1)S(1)} collective-permute-done((bf16[384,256]{1,0:T(8,128)(2,1)S(1)}, bf16[384,256]{1,0:T(8,128)(2,1)S(1)}, u32[]{:S(2)}, u32[]{:S(2)}) %collective-permute-start.9) | collective-permute-done | bytes 196640 | tf_op jit(solution)/shard_map/ppermute | solution.py:36
  148.1 0.0 all-to-all-done.1.arrived
  148.1 19.4 %encode.1.normed = bf16[768,896]{1,0:T(8,128)(2,1)} custom-call(s32[12]{0:T(128)} %copy-done.25, bf16[32,64,896]{2,1,0:T(8,128)(2,1)} %all-to-all-done.1.arrived, bf16[16,704,896]{2,1,0:T(8,128)(2,1)} %bitcast.6), custom_call_target="tpu_custom_call" | custom-call | flops 9865003008 | bytes 16000000 | tf_op jit(solution)/shard_map/encode/pallas_call | solution.py:142
  167.5 17.9 %cross.1 = (bf16[384,2048]{1,0:T(8,128)(2,1)}, bf16[64,2048]{1,0:T(8,128)(2,1)}) custom-call(bf16[768,896]{1,0:T(8,128)(2,1)} %encode.1.normed, bf16[16,704,896]{2,1,0:T(8,128)(2,1)} %bitcast.7, bf16[384,2048]{1,0:T(8,128)(2,1)} %pad_maximum_fusion.query), custom_call_target="tpu_custom_call" | custom-call | flops 5637144576 | bytes 12000000 | tf_op jit(solution)/shard_map/cross/pallas_call | solution.py:238
  185.5 2.6 %collective-permute-start.15 = (bf16[64,2048]{1,0:T(8,128)(2,1)}, bf16[64,2048]{1,0:T(8,128)(2,1)S(1)}, u32[]{:S(2)}, u32[]{:S(2)}) collective-permute-start(bf16[64,2048]{1,0:T(8,128)(2,1)} %get-tuple-element.101), channel_id=1, source_target_pairs={{0,1},{1,2},{2,3},{3,4},{4,5},{5,6},{6,7},{8,9},{9,10},{10,11},{11... | collective-permute-start | bytes 786440 | tf_op jit(solution)/shard_map/ppermute | solution.py:451
  188.1 2.8 %unpack.1 = bf16[384,2048]{1,0:T(8,128)(2,1)} custom-call(bf16[384,256]{1,0:T(8,128)(2,1)} %get-tuple-element.92.refs_0_, bf16[384,256]{1,0:T(8,128)(2,1)} %copy-done.7, bf16[384,256]{1,0:T(8,128)(2,1)} %copy-done.8, bf16[384,256]{1,0:T(8,128)(2,1)} %copy-done.2, bf16[384,256]{1,0:T(8,128)(2,1)} %copy-done.3, bf16[384,256]{1,0:T(8,128)(2,1)} %copy-done.4, ...), custom_call_target="tpu_custom_call" | custom-call | bytes 3145728 | tf_op jit(solution)/shard_map/unpack/pallas_call | solution.py:386
  190.9 0.8 collective-permute-done.15.before
  191.7 0.7 copy-done.1
  192.4 1.8 mend.1
  (50 shorter events, 0.1 us)
Async XLA Ops:
  7.2 2.2 %copy-start.9 = (s32[6,2]{0,1:T(2,128)S(1)}, s32[6,2]{0,1:T(2,128)}, u32[]{:S(2)}) copy-start(s32[6,2]{0,1:T(2,128)} %param.14) | copy-start | bytes 148
  7.2 2.3 %copy-start.10 = (s32[6,2]{0,1:T(2,128)S(1)}, s32[6,2]{0,1:T(2,128)}, u32[]{:S(2)}) copy-start(s32[6,2]{0,1:T(2,128)} %param.15) | copy-start | bytes 148
  7.2 140.9 %all-gather.2.cloned.1.call-start = ((), (), s32[]{:S(2)}) async-start(), calls=%async_computation.2 | async-start | bytes 20342784 | tf_op jit(solution)/shard_map/all_gather | solution.py:431
  9.9 13.2 %copy-start.25 = (s32[12]{0:T(128)}, s32[12]{0:T(128)S(1)}, u32[]{:S(2)}) copy-start(s32[12]{0:T(128)S(1)} %multiply_add_fusion.slot) | copy-start | bytes 148
  10.7 13.8 %all-to-all-start = ((s32[16,1,2]{2,1,0:T(1,128)}), s32[16,1,2]{2,1,0:T(1,128)S(1)}, u32[]{:S(2)}, u32[]{:S(2)}) async-start(s32[16,1,2]{2,1,0:T(1,128)} %bitcast.3), calls=%async_computation | async-start | bytes 16384 | tf_op jit(solution)/shard_map/all_to_all | solution.py:434
  31.6 15.0 %copy-start.13 = (bf16[3,384,256]{2,1,0:T(8,128)(2,1)S(1)}, bf16[3,384,256]{2,1,0:T(8,128)(2,1)}, u32[]{:S(2)}) copy-start(bf16[3,384,256]{2,1,0:T(8,128)(2,1)} %get-tuple-element.69) | copy-start | bytes 1769476
  31.6 24.4 %copy-start.12 = (bf16[3,384,256]{2,1,0:T(8,128)(2,1)S(1)}, bf16[3,384,256]{2,1,0:T(8,128)(2,1)}, u32[]{:S(2)}) copy-start(bf16[3,384,256]{2,1,0:T(8,128)(2,1)} %get-tuple-element.70) | copy-start | bytes 1769476
  31.6 42.3 %copy-start.11 = (bf16[3,384,256]{2,1,0:T(8,128)(2,1)S(1)}, bf16[3,384,256]{2,1,0:T(8,128)(2,1)}, u32[]{:S(2)}) copy-start(bf16[3,384,256]{2,1,0:T(8,128)(2,1)} %get-tuple-element.71) | copy-start | bytes 1769476
  31.7 43.3 %copy-start = (bf16[384,2048]{1,0:T(8,128)(2,1)S(1)}, bf16[384,2048]{1,0:T(8,128)(2,1)}, u32[]{:S(2)}) copy-start(bf16[384,2048]{1,0:T(8,128)(2,1)} %param.13) | copy-start | bytes 4718596
  31.7 116.4 %all-to-all-start.1 = ((bf16[32,64,896]{2,1,0:T(8,128)(2,1)}), bf16[32,64,896]{2,1,0:T(8,128)(2,1)}, u32[]{:S(2)}, u32[]{:S(2)}) async-start(bf16[32,64,896]{2,1,0:T(8,128)(2,1)} %fetch.1), calls=%async_computation.1 | async-start | bytes 7340032 | tf_op jit(solution)/shard_map/all_to_all | solution.py:441
  37.1 19.0 %collective-permute-start.1 = (bf16[3,384,256]{2,1,0:T(8,128)(2,1)}, bf16[3,384,256]{2,1,0:T(8,128)(2,1)S(1)}, u32[]{:S(2)}, u32[]{:S(2)}) collective-permute-start(bf16[3,384,256]{2,1,0:T(8,128)(2,1)} %get-tuple-element.65), channel_id=1, source_target_pairs={{0,4},{1,5},{2,6},{3,7},{4,0},{5,1},{6,2},{7,3},{8,12},{9,13},{10,... | collective-permute-start | bytes 1769480 | tf_op jit(solution)/shard_map/ppermute | solution.py:36
  41.7 32.3 %collective-permute-start.2 = (bf16[3,384,256]{2,1,0:T(8,128)(2,1)}, bf16[3,384,256]{2,1,0:T(8,128)(2,1)S(1)}, u32[]{:S(2)}, u32[]{:S(2)}) collective-permute-start(bf16[3,384,256]{2,1,0:T(8,128)(2,1)} %get-tuple-element.66), channel_id=1, source_target_pairs={{0,5},{1,4},{2,7},{3,6},{4,1},{5,0},{6,3},{7,2},{8,13},{9,12},{10,... | collective-permute-start | bytes 1769480 | tf_op jit(solution)/shard_map/ppermute | solution.py:36
  43.5 44.3 %collective-permute-start.3 = (bf16[3,384,256]{2,1,0:T(8,128)(2,1)}, bf16[3,384,256]{2,1,0:T(8,128)(2,1)S(1)}, u32[]{:S(2)}, u32[]{:S(2)}) collective-permute-start(bf16[3,384,256]{2,1,0:T(8,128)(2,1)} %get-tuple-element.67), channel_id=1, source_target_pairs={{0,2},{1,3},{2,4},{3,5},{4,6},{5,7},{6,0},{7,1},{8,10},{9,11},{10,... | collective-permute-start | bytes 1769480 | tf_op jit(solution)/shard_map/ppermute | solution.py:36
  44.2 47.7 %collective-permute-start.4 = (bf16[3,384,256]{2,1,0:T(8,128)(2,1)}, bf16[3,384,256]{2,1,0:T(8,128)(2,1)S(1)}, u32[]{:S(2)}, u32[]{:S(2)}) collective-permute-start(bf16[3,384,256]{2,1,0:T(8,128)(2,1)} %get-tuple-element.68), channel_id=1, source_target_pairs={{0,6},{1,7},{2,0},{3,1},{4,2},{5,3},{6,4},{7,5},{8,14},{9,15},{10,... | collective-permute-start | bytes 1769480 | tf_op jit(solution)/shard_map/ppermute | solution.py:36
  46.7 53.7 %collective-permute-start.5 = (bf16[3,384,256]{2,1,0:T(8,128)(2,1)S(1)}, bf16[3,384,256]{2,1,0:T(8,128)(2,1)S(1)}, u32[]{:S(2)}, u32[]{:S(2)}) collective-permute-start(bf16[3,384,256]{2,1,0:T(8,128)(2,1)S(1)} %copy-done.13), channel_id=1, source_target_pairs={{0,3},{1,2},{2,5},{3,4},{4,7},{5,6},{6,1},{7,0},{8,11},{9,10},{10,... | collective-permute-start | bytes 1769480 | tf_op jit(solution)/shard_map/ppermute | solution.py:36
  56.1 44.9 %copy-start.14 = (bf16[3,384,256]{2,1,0:T(8,128)(2,1)}, bf16[3,384,256]{2,1,0:T(8,128)(2,1)S(1)}, u32[]{:S(2)}) copy-start(bf16[3,384,256]{2,1,0:T(8,128)(2,1)S(1)} %collective-permute-done.1.refs_1_) | copy-start | bytes 1769476
  56.1 44.9 %collective-permute-start.6 = (bf16[3,384,256]{2,1,0:T(8,128)(2,1)S(1)}, bf16[3,384,256]{2,1,0:T(8,128)(2,1)S(1)}, u32[]{:S(2)}, u32[]{:S(2)}) collective-permute-start(bf16[3,384,256]{2,1,0:T(8,128)(2,1)S(1)} %copy-done.12), channel_id=1, source_target_pairs={{0,7},{1,6},{2,1},{3,0},{4,3},{5,2},{6,5},{7,4},{8,15},{9,14},{10,... | collective-permute-start | bytes 1769480 | tf_op jit(solution)/shard_map/ppermute | solution.py:36
  73.9 27.0 %copy-start.15 = (bf16[3,384,256]{2,1,0:T(8,128)(2,1)}, bf16[3,384,256]{2,1,0:T(8,128)(2,1)S(1)}, u32[]{:S(2)}) copy-start(bf16[3,384,256]{2,1,0:T(8,128)(2,1)S(1)} %collective-permute-done.2.refs_2_) | copy-start | bytes 1769476
  73.9 27.0 %collective-permute-start.7 = (bf16[3,384,256]{2,1,0:T(8,128)(2,1)S(1)}, bf16[3,384,256]{2,1,0:T(8,128)(2,1)}, u32[]{:S(2)}, u32[]{:S(2)}) collective-permute-start(bf16[3,384,256]{2,1,0:T(8,128)(2,1)S(1)} %copy-done.11), channel_id=1, source_target_pairs={{0,1},{1,0},{2,3},{3,2},{4,5},{5,4},{6,7},{7,6},{8,9},{9,8},{10,11... | collective-permute-start | bytes 1769480 | tf_op jit(solution)/shard_map/ppermute | solution.py:36
  87.8 13.2 %copy-start.16 = (bf16[3,384,256]{2,1,0:T(8,128)(2,1)}, bf16[3,384,256]{2,1,0:T(8,128)(2,1)S(1)}, u32[]{:S(2)}) copy-start(bf16[3,384,256]{2,1,0:T(8,128)(2,1)S(1)} %collective-permute-done.3.refs_3_) | copy-start | bytes 1769476
  87.8 40.5 %collective-permute-start = (bf16[64,2048]{1,0:T(8,128)(2,1)S(1)}, bf16[64,2048]{1,0:T(8,128)(2,1)S(1)}, u32[]{:S(2)}, u32[]{:S(2)}) collective-permute-start(bf16[64,2048]{1,0:T(8,128)(2,1)S(1)} %slice.10), channel_id=1, source_target_pairs={{1,0},{2,1},{3,2},{4,3},{5,4},{6,5},{7,6},{9,8},{10,9},{11,10},{12... | collective-permute-start | bytes 786440 | tf_op jit(solution)/shard_map/ppermute | solution.py:442
  91.9 9.0 %copy-start.17 = (bf16[3,384,256]{2,1,0:T(8,128)(2,1)}, bf16[3,384,256]{2,1,0:T(8,128)(2,1)S(1)}, u32[]{:S(2)}) copy-start(bf16[3,384,256]{2,1,0:T(8,128)(2,1)S(1)} %collective-permute-done.4.refs_4_) | copy-start | bytes 1769476
  100.4 0.8 copy-start.18
  100.9 0.8 copy-start.19
  121.6 3.2 %copy-start.24 = (bf16[384,256]{1,0:T(8,128)(2,1)S(1)}, bf16[384,256]{1,0:T(8,128)(2,1)}, u32[]{:S(2)}) copy-start(bf16[384,256]{1,0:T(8,128)(2,1)} %get-tuple-element.77) | copy-start | bytes 589828
  121.6 6.7 %copy-start.23 = (bf16[384,256]{1,0:T(8,128)(2,1)S(1)}, bf16[384,256]{1,0:T(8,128)(2,1)}, u32[]{:S(2)}) copy-start(bf16[384,256]{1,0:T(8,128)(2,1)} %get-tuple-element.78) | copy-start | bytes 589828
  121.6 6.7 %copy-start.22 = (bf16[384,256]{1,0:T(8,128)(2,1)S(1)}, bf16[384,256]{1,0:T(8,128)(2,1)}, u32[]{:S(2)}) copy-start(bf16[384,256]{1,0:T(8,128)(2,1)} %get-tuple-element.79) | copy-start | bytes 589828
  121.6 11.2 %copy-start.21 = (bf16[384,256]{1,0:T(8,128)(2,1)S(1)}, bf16[384,256]{1,0:T(8,128)(2,1)}, u32[]{:S(2)}) copy-start(bf16[384,256]{1,0:T(8,128)(2,1)} %get-tuple-element.73) | copy-start | bytes 589828
  121.6 14.4 %copy-start.20 = (bf16[384,256]{1,0:T(8,128)(2,1)S(1)}, bf16[384,256]{1,0:T(8,128)(2,1)}, u32[]{:S(2)}) copy-start(bf16[384,256]{1,0:T(8,128)(2,1)} %get-tuple-element.74) | copy-start | bytes 589828
  121.6 11.2 %collective-permute-start.10 = (bf16[384,256]{1,0:T(8,128)(2,1)}, bf16[384,256]{1,0:T(8,128)(2,1)S(1)}, u32[]{:S(2)}, u32[]{:S(2)}) collective-permute-start(bf16[384,256]{1,0:T(8,128)(2,1)} %get-tuple-element.75), channel_id=1, source_target_pairs={{0,6},{1,7},{2,0},{3,1},{4,2},{5,3},{6,4},{7,5},{8,14},{9,15},{10,... | collective-permute-start | bytes 589832 | tf_op jit(solution)/shard_map/ppermute | solution.py:36
  124.4 11.6 %collective-permute-start.11 = (bf16[384,256]{1,0:T(8,128)(2,1)}, bf16[384,256]{1,0:T(8,128)(2,1)S(1)}, u32[]{:S(2)}, u32[]{:S(2)}) collective-permute-start(bf16[384,256]{1,0:T(8,128)(2,1)} %get-tuple-element.76), channel_id=1, source_target_pairs={{0,2},{1,3},{2,4},{3,5},{4,6},{5,7},{6,0},{7,1},{8,10},{9,11},{10,... | collective-permute-start | bytes 589832 | tf_op jit(solution)/shard_map/ppermute | solution.py:36
  124.8 15.1 %collective-permute-start.12 = (bf16[384,256]{1,0:T(8,128)(2,1)S(1)}, bf16[384,256]{1,0:T(8,128)(2,1)S(1)}, u32[]{:S(2)}, u32[]{:S(2)}) collective-permute-start(bf16[384,256]{1,0:T(8,128)(2,1)S(1)} %copy-done.24), channel_id=1, source_target_pairs={{0,7},{1,6},{2,1},{3,0},{4,3},{5,2},{6,5},{7,4},{8,15},{9,14},{10,... | collective-permute-start | bytes 589832 | tf_op jit(solution)/shard_map/ppermute | solution.py:36
  128.3 11.6 %collective-permute-start.13 = (bf16[384,256]{1,0:T(8,128)(2,1)S(1)}, bf16[384,256]{1,0:T(8,128)(2,1)S(1)}, u32[]{:S(2)}, u32[]{:S(2)}) collective-permute-start(bf16[384,256]{1,0:T(8,128)(2,1)S(1)} %copy-done.23), channel_id=1, source_target_pairs={{0,3},{1,2},{2,5},{3,4},{4,7},{5,6},{6,1},{7,0},{8,11},{9,10},{10,... | collective-permute-start | bytes 589832 | tf_op jit(solution)/shard_map/ppermute | solution.py:36
  128.3 11.6 %collective-permute-start.14 = (bf16[384,256]{1,0:T(8,128)(2,1)S(1)}, bf16[384,256]{1,0:T(8,128)(2,1)S(1)}, u32[]{:S(2)}, u32[]{:S(2)}) collective-permute-start(bf16[384,256]{1,0:T(8,128)(2,1)S(1)} %copy-done.22), channel_id=1, source_target_pairs={{0,1},{1,0},{2,3},{3,2},{4,5},{5,4},{6,7},{7,6},{8,9},{9,8},{10,11... | collective-permute-start | bytes 589832 | tf_op jit(solution)/shard_map/ppermute | solution.py:36
  132.8 6.3 %copy-start.2 = (bf16[384,256]{1,0:T(8,128)(2,1)}, bf16[384,256]{1,0:T(8,128)(2,1)S(1)}, u32[]{:S(2)}) copy-start(bf16[384,256]{1,0:T(8,128)(2,1)S(1)} %collective-permute-done.10.refs_3_) | copy-start | bytes 589828
  132.8 11.0 %collective-permute-start.8 = (bf16[384,256]{1,0:T(8,128)(2,1)S(1)}, bf16[384,256]{1,0:T(8,128)(2,1)S(1)}, u32[]{:S(2)}, u32[]{:S(2)}) collective-permute-start(bf16[384,256]{1,0:T(8,128)(2,1)S(1)} %copy-done.21), channel_id=1, source_target_pairs={{0,4},{1,5},{2,6},{3,7},{4,0},{5,1},{6,2},{7,3},{8,12},{9,13},{10,... | collective-permute-start | bytes 589832 | tf_op jit(solution)/shard_map/ppermute | solution.py:36
  136.0 3.1 %copy-start.3 = (bf16[384,256]{1,0:T(8,128)(2,1)}, bf16[384,256]{1,0:T(8,128)(2,1)S(1)}, u32[]{:S(2)}) copy-start(bf16[384,256]{1,0:T(8,128)(2,1)S(1)} %collective-permute-done.11.refs_4_) | copy-start | bytes 589828
  136.0 12.1 %collective-permute-start.9 = (bf16[384,256]{1,0:T(8,128)(2,1)S(1)}, bf16[384,256]{1,0:T(8,128)(2,1)S(1)}, u32[]{:S(2)}, u32[]{:S(2)}) collective-permute-start(bf16[384,256]{1,0:T(8,128)(2,1)S(1)} %copy-done.20), channel_id=1, source_target_pairs={{0,5},{1,4},{2,7},{3,6},{4,1},{5,0},{6,3},{7,2},{8,13},{9,12},{10,... | collective-permute-start | bytes 589832 | tf_op jit(solution)/shard_map/ppermute | solution.py:36
  139.9 27.6 %copy-start.4 = (bf16[384,256]{1,0:T(8,128)(2,1)}, bf16[384,256]{1,0:T(8,128)(2,1)S(1)}, u32[]{:S(2)}) copy-start(bf16[384,256]{1,0:T(8,128)(2,1)S(1)} %collective-permute-done.12.refs_5_) | copy-start | bytes 589828
  139.9 27.6 %copy-start.5 = (bf16[384,256]{1,0:T(8,128)(2,1)}, bf16[384,256]{1,0:T(8,128)(2,1)S(1)}, u32[]{:S(2)}) copy-start(bf16[384,256]{1,0:T(8,128)(2,1)S(1)} %collective-permute-done.13.refs_6_) | copy-start | bytes 589828
  139.9 27.6 %copy-start.6 = (bf16[384,256]{1,0:T(8,128)(2,1)}, bf16[384,256]{1,0:T(8,128)(2,1)S(1)}, u32[]{:S(2)}) copy-start(bf16[384,256]{1,0:T(8,128)(2,1)S(1)} %collective-permute-done.14.refs_7_) | copy-start | bytes 589828
  143.8 23.7 %copy-start.7 = (bf16[384,256]{1,0:T(8,128)(2,1)}, bf16[384,256]{1,0:T(8,128)(2,1)S(1)}, u32[]{:S(2)}) copy-start(bf16[384,256]{1,0:T(8,128)(2,1)S(1)} %collective-permute-done.8.refs_1_) | copy-start | bytes 589828
  148.1 19.4 %copy-start.8 = (bf16[384,256]{1,0:T(8,128)(2,1)}, bf16[384,256]{1,0:T(8,128)(2,1)S(1)}, u32[]{:S(2)}) copy-start(bf16[384,256]{1,0:T(8,128)(2,1)S(1)} %collective-permute-done.9.refs_2_) | copy-start | bytes 589828
  185.5 6.2 %collective-permute-start.15 = (bf16[64,2048]{1,0:T(8,128)(2,1)}, bf16[64,2048]{1,0:T(8,128)(2,1)S(1)}, u32[]{:S(2)}, u32[]{:S(2)}) collective-permute-start(bf16[64,2048]{1,0:T(8,128)(2,1)} %get-tuple-element.101), channel_id=1, source_target_pairs={{0,1},{1,2},{2,3},{3,4},{4,5},{5,6},{6,7},{8,9},{9,10},{10,11},{11... | collective-permute-start | bytes 786440 | tf_op jit(solution)/shard_map/ppermute | solution.py:451
  191.7 0.7 copy-start.1
Sparse Core Ops, SparseCore 0:
  11.1 129.2 all-gather.1

commit v3 on v2

v3 whole, which is shorter than its diff:
```python
import functools
import math

import jax
import jax.numpy as jnp
from jax import lax
from jax.experimental import pallas as pl
from jax.experimental.pallas import tpu as pltpu
from jax.sharding import PartitionSpec as P

HEADS = 16
HEAD_DIM = 128
STRETCH = 64
NEIGH = 2
CAP = 2
LOG2E = 1.4426950408889634
BF16 = jnp.bfloat16
F32 = jnp.float32
NT = (((1,), (1,)), ((), ()))
ANY = pl.BlockSpec(memory_space=pl.ANY)
VMEM = pl.BlockSpec(memory_space=pltpu.VMEM)
HOPS = (0, 2, 1, 3)


def cost(flops, size, exps=0):
    return pl.CostEstimate(flops=int(flops), bytes_accessed=int(size), transcendentals=int(exps))


def params(mib=56, **more):
    return pltpu.CompilerParams(vmem_limit_bytes=mib << 20, **more)


def hop(value, chips, flip):
    count = lax.axis_size("seq")
    pairs = [(i, ((i + 2 * chips) % count) ^ flip) for i in range(count)]
    return lax.ppermute(value, "seq", pairs)


def run_copies(copies):
    for copy in copies:
        copy.start()
    for copy in copies:
        copy.wait()


def rms(wide):
    return wide * lax.rsqrt(jnp.mean(wide * wide, axis=-1, keepdims=True) + 1e-06)


def relay(reads, writes):
    for copy in reads:
        copy.start()
    for read, write in zip(reads, writes):
        read.wait()
        write.start()
    for copy in writes:
        copy.wait()


def fetch_kernel(asked, database, found, held, sem):
    last = database.shape[0] - 1
    count = found.shape[0]
    relay(
        [
            pltpu.make_async_copy(
                database.at[jnp.clip(asked[i], 0, last)], held.at[i], sem.at[0, i]
            )
            for i in range(count)
        ],
        [pltpu.make_async_copy(held.at[i], found.at[i], sem.at[1, i]) for i in range(count)],
    )


def fetch(asked, database):
    slots = asked.shape[0]
    shape = (slots, *database.shape[1:])
    return pl.pallas_call(
        fetch_kernel,
        grid_spec=pltpu.PrefetchScalarGridSpec(
            num_scalar_prefetch=1,
            grid=(1,),
            in_specs=[ANY],
            out_specs=ANY,
            scratch_shapes=[pltpu.VMEM(shape, BF16), pltpu.SemaphoreType.DMA((2, slots))],
        ),
        out_shape=jax.ShapeDtypeStruct(shape, BF16),
        cost_estimate=cost(0, 4 * math.prod(shape)),
        compiler_params=params(),
        name="fetch",
    )(asked, database)


def half_kernel(half, ffn_in, ffn_out, projection, out):
    core = lax.rem(lax.axis_index("seq"), 2)
    rows = pl.ds(pl.multiple_of(core * half, 16), half)
    out[:half, :] = ffn_in[rows, :]
    out[half : 2 * half, :] = ffn_out[rows, :]
    columns = pl.ds(pl.multiple_of(core * HEAD_DIM, HEAD_DIM), HEAD_DIM)
    out[2 * half :, :] = jnp.transpose(projection[:, columns])


def half_of(ffn_in, ffn_out, projection):
    rows, deep = ffn_out.shape
    return pl.pallas_call(
        functools.partial(half_kernel, rows // 2),
        in_specs=[VMEM] * 3,
        out_specs=VMEM,
        out_shape=jax.ShapeDtypeStruct((rows + HEAD_DIM, deep), BF16),
        cost_estimate=cost(0, 4 * rows * deep),
        compiler_params=params(),
        name="half",
    )(ffn_in.T, ffn_out, projection)


def rows_of(gathered, target, first, size, place, sem):
    return [
        pltpu.make_async_copy(
            gathered.at[b, first : first + size, :], target.at[pl.ds(place(b), size), :], sem.at[b]
        )
        for b in range(gathered.shape[0])
    ]


def feed_forward(normed, w_in, w_out, hidden):
    step = 256
    for j in range(w_in.shape[0] // step):
        rows = slice(j * step, (j + 1) * step)
        wide = lax.dot_general(normed[...], w_in[rows, :], NT, preferred_element_type=F32)
        hidden[:, rows] = jax.nn.gelu(wide, approximate=True).astype(BF16)
    return jnp.dot(hidden[...], w_out[...], preferred_element_type=F32)


def encode_kernel(slot, arrived, gathered, total, normed, x, w_in, w_out, hidden, x_sem, sem):
    tokens = arrived.shape[1]
    half = w_in.shape[0] // gathered.shape[0]
    copies = [
        pltpu.make_async_copy(
            arrived.at[slot[i]], x.at[i * tokens : (i + 1) * tokens, :], x_sem.at[i]
        )
        for i in range(x.shape[0] // tokens)
    ]
    copies += rows_of(gathered, w_in, 0, half, lambda b: b * half, sem.at[0])
    copies += rows_of(gathered, w_out, half, half, lambda b: b * half, sem.at[1])
    run_copies(copies)
    normed[...] = rms(x[...].astype(F32)).astype(BF16)
    total[...] = x[...].astype(F32) + feed_forward(normed, w_in, w_out, hidden)


def encode(slot, arrived, gathered, half):
    requests = slot.shape[0]
    rows, deep = requests * arrived.shape[1], arrived.shape[2]
    owners = gathered.shape[0]
    whole = pl.BlockSpec((rows, deep), lambda i, s: (0, 0))
    return pl.pallas_call(
        encode_kernel,
        grid_spec=pltpu.PrefetchScalarGridSpec(
            num_scalar_prefetch=1,
            grid=(1,),
            in_specs=[ANY, ANY],
            out_specs=[whole, whole],
            scratch_shapes=[
                pltpu.VMEM((rows, deep), BF16),
                pltpu.VMEM((owners * half, deep), BF16),
                pltpu.VMEM((owners * half, deep), BF16),
                pltpu.VMEM((rows, owners * half), BF16),
                pltpu.SemaphoreType.DMA((requests,)),
                pltpu.SemaphoreType.DMA((2, owners)),
            ],
        ),
        out_shape=[
            jax.ShapeDtypeStruct((rows, deep), F32),
            jax.ShapeDtypeStruct((rows, deep), BF16),
        ],
        cost_estimate=cost(5e9, 12e6, 2e6),
        compiler_params=params(),
        name="encode",
    )(slot, arrived, gathered)


def attend(queries, keys, values, allowed, scale):
    scores = [
        jnp.where(allowed, lax.dot_general(q, k, NT, preferred_element_type=F32), -jnp.inf)
        for q, k in zip(queries, keys)
    ]
    scores = jnp.concatenate(scores, axis=0)
    probs = jnp.exp2((scores - jnp.max(scores, axis=-1, keepdims=True)) * scale)
    total = jnp.sum(probs, axis=-1, keepdims=True)
    probs = probs.astype(BF16)
    rows = queries[0].shape[0]
    summed = [
        jnp.dot(probs[n * rows : (n + 1) * rows], v, preferred_element_type=F32)
        for n, v in enumerate(values)
    ]
    return jnp.concatenate(summed, axis=0) / total


def cross_kernel(
    scale, half, before, normed_in, mine, other, query, out, sent, normed, w_in, w_out, hidden, w_pair, pairs, sem
):
    d = HEAD_DIM
    core = lax.rem(lax.axis_index("seq"), 2)
    own = lambda b: pl.multiple_of((2 * b + core) * d, d)
    rest = lambda b: pl.multiple_of((2 * b + 1 - core) * d, d)
    copies = rows_of(other, w_in, 0, half, lambda b: b * half, sem.at[0])
    copies += rows_of(other, w_out, half, half, lambda b: b * half, sem.at[1])
    projections = rows_of(mine, w_pair, 2 * half, d, own, sem.at[2])
    projections += rows_of(other, w_pair, 2 * half, d, rest, sem.at[3])
    for copy in copies + projections:
        copy.start()

    for copy in copies:
        copy.wait()
    mixed = feed_forward(normed_in, w_in, w_out, hidden)
    encoded = (before[...] + mixed).astype(BF16).astype(F32)
    for copy in projections:
        copy.wait()
    normed[...] = rms(encoded).astype(BF16)
    step = 512

    for j in range(w_pair.shape[0] // step):
        rows = slice(j * step, (j + 1) * step)
        wide = lax.dot_general(normed[...], w_pair[rows, :], NT, preferred_element_type=F32)
        pairs[:, rows] = wide.astype(BF16)

    span = NEIGH * STRETCH
    width = query.shape[1]
    at_row = lax.broadcasted_iota(jnp.int32, (2 * STRETCH, 2 * span), 0)
    at_key = lax.broadcasted_iota(jnp.int32, (2 * STRETCH, 2 * span), 1)
    allowed = (at_row >= STRETCH) == (at_key >= span)
    blocks = normed.shape[0] // (2 * span)
    together = 4
    for h in range(0, width // d, together):
        heads = [(t, b) for t in range(h, h + together) for b in range(blocks)]
        result = attend(
            [query[2 * b * STRETCH : 2 * (b + 1) * STRETCH, t * d : (t + 1) * d] for t, b in heads],
            [pairs[2 * b * span : 2 * (b + 1) * span, t * d : (t + 1) * d] for t, b in heads],
            [
                pairs[2 * b * span : 2 * (b + 1) * span, width + t * d : width + (t + 1) * d]
                for t, b in heads
            ],
            allowed,
            scale,
        )
        rows = query.shape[0]
        for n in range(together):
            lanes = slice((h + n) * d, (h + n + 1) * d)
            moved = pltpu.roll(result[n * rows : (n + 1) * rows], STRETCH - 1, 0)
            out[:, lanes] = moved.astype(BF16)
            sent[:, lanes] = moved[:STRETCH].astype(BF16)


def cross(before, normed_in, mine, other, query, half):
    rows, width = query.shape
    d = HEAD_DIM
    owners, _, deep = mine.shape
    tokens = before.shape[0]
    return pl.pallas_call(
        functools.partial(cross_kernel, LOG2E / math.sqrt(d), half),
        in_specs=[VMEM, VMEM, ANY, ANY, VMEM],
        out_specs=[VMEM, VMEM],
        scratch_shapes=[
            pltpu.VMEM((tokens, deep), BF16),
            pltpu.VMEM((owners * half, deep), BF16),
            pltpu.VMEM((owners * half, deep), BF16),
            pltpu.VMEM((tokens, owners * half), BF16),
            pltpu.VMEM((2 * width, deep), BF16),
            pltpu.VMEM((tokens, 2 * width), BF16),
            pltpu.SemaphoreType.DMA((4, owners)),
        ],
        out_shape=[
            jax.ShapeDtypeStruct(query.shape, BF16),
            jax.ShapeDtypeStruct((STRETCH, width), BF16),
        ],
        cost_estimate=cost(12e9, 20e6, 4e6),
        compiler_params=params(60),
        name="cross",
    )(before, normed_in, mine, other, query)


def mend_kernel(own, before, out):
    last = lax.broadcasted_iota(jnp.int32, own.shape, 0) == STRETCH - 1
    out[...] = jnp.where(last, own[...].astype(F32), before[...].astype(F32)).astype(BF16)


def mend(own, before):
    block = pl.BlockSpec(before.shape, lambda i: (0, 0))
    return pl.pallas_call(
        mend_kernel,
        grid=(1,),
        in_specs=[block, block],
        out_specs=block,
        out_shape=jax.ShapeDtypeStruct(own.shape, BF16),
        input_output_aliases={0: 0},
        cost_estimate=cost(0, 6 * math.prod(before.shape)),
        compiler_params=params(),
        name="mend",
    )(own, before)


def partners(chips):
    place = lax.axis_index("seq")
    chip, core = lax.div(place, 2), lax.rem(place, 2)
    sides = (core, 1 - core)
    reached = [[side * chips + lax.rem(chip + k, chips) for side in sides] for k in HOPS]
    reaching = [[lax.rem(chip + chips - k, chips) * 2 + side for side in sides] for k in HOPS]
    return reached, reaching


def pack_kernel(chips, query, key, value, *rest):
    count = len(HOPS)
    parts, held, sem = rest[:count], rest[count], rest[count + 1]
    block = parts[0].shape[3]
    reached, _ = partners(chips)
    reads, writes = [], []
    for n in (*range(1, count), 0):
        for f in range(2):
            columns = pl.ds(pl.multiple_of(reached[n][f] * block, block), block)
            for a, source in enumerate((query, key, value)):
                place = held.at[n, f, a]
                reads.append(
                    pltpu.make_async_copy(source.at[:, columns], place, sem.at[0, n, f, a])
                )
                writes.append(
                    pltpu.make_async_copy(place, parts[n].at[f, a], sem.at[1, n, f, a])
                )
    relay(reads, writes)


def pack(chips, query, key, value):
    rows, width = query.shape
    count = len(HOPS)
    shape = (2, 3, rows, width // (2 * count))
    return pl.pallas_call(
        functools.partial(pack_kernel, chips),
        in_specs=[ANY] * 3,
        out_specs=[ANY] * count,
        scratch_shapes=[pltpu.VMEM((count, *shape), BF16), pltpu.SemaphoreType.DMA((2, count, 2, 3))],
        out_shape=[jax.ShapeDtypeStruct(shape, BF16)] * count,
        cost_estimate=cost(0, 12 * rows * width),
        compiler_params=params(),
        name="pack",
    )(query, key, value)


def self_kernel(chips, scale, *refs):
    hops = len(HOPS)
    count = 2 * hops
    parts, outs = refs[:count], refs[count : count + hops]
    query, key, value, result = refs[count + hops :]
    _, source = partners(chips)
    rows = parts[0].shape[2]
    d = HEAD_DIM
    places = [
        [pl.ds(pl.multiple_of(source[n][f] * rows, rows), rows) for f in range(2)]
        for n in range(hops)
    ]
    for n in range(hops):
        for f in range(2):
            part, place = parts[f * hops + n], places[n][f]
            query[place, :] = part[0, 0]
            key[place, :] = part[0, 1]
            value[place, :d] = part[0, 2]
    value[:, d:] = jnp.ones((count * rows, d), BF16)
    at_row = lax.broadcasted_iota(jnp.int32, (rows, rows), 0)
    at_key = lax.broadcasted_iota(jnp.int32, (rows, rows), 1)
    allowed = at_key <= at_row
    for i in range(count):
        low, high = i * rows, (i + 1) * rows
        block = query[low:high, :]
        scores = lax.dot_general(block, key[low:high, :], NT, preferred_element_type=F32)
        scores = jnp.where(allowed, scores, -jnp.inf)
        if i:
            left = lax.dot_general(block, key[:low, :], NT, preferred_element_type=F32)
            scores = jnp.concatenate([left, scores], axis=1)
        best = jnp.max(scores, axis=-1, keepdims=True)
        probs = jnp.exp2((scores - best) * scale).astype(BF16)
        summed = jnp.dot(probs, value[:high, :], preferred_element_type=F32)
        result[low:high, :] = (summed[:, :d] / summed[:, d:]).astype(BF16)
    for n in range(hops):
        for f in range(2):
            outs[n][f] = result[places[n][f], :]


def self_attention(chips, same, flipped):
    hops = len(HOPS)
    _, _, rows, width = same[0].shape
    d = HEAD_DIM
    length = 2 * hops * rows
    at = lambda f: pl.BlockSpec((1, 3, rows, d), lambda h: (f, 0, 0, h))
    return pl.pallas_call(
        functools.partial(self_kernel, chips, LOG2E / math.sqrt(d)),
        grid=(width // d,),
        in_specs=[at(0)] * hops + [at(1)] * hops,
        out_specs=[pl.BlockSpec((2, rows, d), lambda h: (0, 0, h))] * hops,
        scratch_shapes=[
            pltpu.VMEM((length, d), BF16),
            pltpu.VMEM((length, d), BF16),
            pltpu.VMEM((length, 2 * d), BF16),
            pltpu.VMEM((length, d), BF16),
        ],
        out_shape=[jax.ShapeDtypeStruct((2, rows, width), BF16)] * hops,
        cost_estimate=cost(7e9, 8e6, length * length),
        compiler_params=params(),
        name="causal",
    )(*same, *flipped)


def unpack_kernel(chips, *refs):
    hops = len(HOPS)
    parts, out = refs[:-1], refs[-1]
    block = parts[0].shape[2]
    reached, _ = partners(chips)
    for n in range(hops):
        for f in range(2):
            columns = pl.ds(pl.multiple_of(reached[n][f] * block, block), block)
            out[:, columns] = parts[f * hops + n][0]


def unpack(chips, same, flipped):
    hops = len(HOPS)
    _, rows, block = same[0].shape
    at = lambda f: pl.BlockSpec((1, rows, block), lambda i: (f, 0, 0))
    shape = (rows, 2 * hops * block)
    return pl.pallas_call(
        functools.partial(unpack_kernel, chips),
        grid=(1,),
        in_specs=[at(0)] * hops + [at(1)] * hops,
        out_specs=pl.BlockSpec(shape, lambda i: (0, 0)),
        out_shape=jax.ShapeDtypeStruct(shape, BF16),
        cost_estimate=cost(0, 4 * math.prod(shape)),
        compiler_params=params(),
        name="unpack",
    )(*same, *flipped)


def requests_of(retrieval_shard, retrieval_row):
    shard_list = retrieval_shard.reshape(-1)
    row_list = retrieval_row.reshape(-1)
    owners = lax.axis_size("db")
    order = jnp.arange(shard_list.shape[0])
    earlier = (order[:, None] > order[None, :]) & (shard_list[:, None] == shard_list[None, :])
    rank = jnp.sum(earlier.astype(jnp.int32), axis=1)
    slot = shard_list * CAP + rank
    hits = jnp.arange(owners * CAP)[:, None] == slot[None, :]
    wanted = jnp.sum(jnp.where(hits, row_list[None, :], 0), axis=1).reshape(owners, CAP)
    return slot, wanted


def shards(
    self_query,
    self_key,
    self_value,
    cross_query,
    retrieval_shard,
    retrieval_row,
    database,
    ffn_in,
    ffn_out,
    cross_projection,
):
    owners = lax.axis_size("db")
    count = lax.axis_size("seq")
    chips = count // 2
    half, deep = ffn_out.shape[0] // 2, ffn_out.shape[1]
    together = lax.optimization_barrier

    part = half_of(ffn_in, ffn_out, cross_projection)
    mine = lax.all_gather(part, "db", axis=0, tiled=True).reshape(owners, -1, deep)

    slot, wanted = requests_of(retrieval_shard, retrieval_row)
    asked = lax.all_to_all(wanted, "db", split_axis=0, concat_axis=0, tiled=True)
    self_query, self_key, self_value, _ = together((self_query, self_key, self_value, wanted))
    parts = pack(chips, self_query, self_key, self_value)
    same = [parts[0]] + [hop(p, k, 0) for p, k in zip(parts[1:], HOPS[1:])]

    found = fetch(asked.reshape(-1), database)
    *same, _ = together((*same, found))
    flipped = [hop(p, 0, 1) for p in same]
    arrived = lax.all_to_all(found, "db", split_axis=0, concat_axis=0, tiled=True)
    ahead = lax.ppermute(cross_query[:STRETCH], "seq", [(i, i - 1) for i in range(1, count)])

    done = self_attention(chips, same, flipped)
    same = [done[0]] + [hop(p, chips - k, 0) for p, k in zip(done[1:], HOPS[1:])]
    flipped = [hop(p, 0, 1) for p in same]
    self_attended = unpack(chips, same, flipped)

    shifted = jnp.concatenate([cross_query[STRETCH - 1 :], ahead[: STRETCH - 1]], axis=0)
    mine, shifted, arrived, _ = together((mine, shifted, arrived, self_attended))
    other = hop(mine, 0, 1)
    total, normed = encode(slot, arrived, mine, half)
    own, sent = cross(total, normed, mine, other, shifted, half)
    before = lax.ppermute(sent, "seq", [(i, i + 1) for i in range(count - 1)])
    cross_attended = mend(own, before)
    return (self_attended, cross_attended)


def solution(mesh):
    in_specs = (
        P(("db", "seq"), None),
        P(("db", "seq"), None),
        P(("db", "seq"), None),
        P(("db", "seq"), None),
        P(("db", "seq"), None),
        P(("db", "seq"), None),
        P("db", None, None),
        P(None, "db"),
        P("db", None),
        P(None, "db"),
    )
    out_specs = (P(("db", "seq"), None), P(("db", "seq"), None))
    return jax.shard_map(shards, mesh=mesh, in_specs=in_specs, out_specs=out_specs, check_vma=False)
```

time: 201 us -> 189 us (0.940); the launches traced: 201 us -> 187 us
  starting transfers between devices: 50.4 us -> 27.4 us
  blocking collectives: 0 us -> 13 us
  waiting for transfers between devices: 55.9 us -> 50.8 us
    ppermute x14 -> x15, starting transfers between devices: 30.6 us -> 16.2 us  [hop(): return lax.ppermute(value, 'seq', pairs)]
    all_to_all x0 -> x1, blocking collectives: none -> 13 us  [shards(): lax.all_to_all(wanted, 'db', split_axis=0, concat_axis=0, tiled=True)]
    ppermute x14 -> x15, waiting for transfers between devices: 53.7 us -> 44.7 us  [hop(): return lax.ppermute(value, 'seq', pairs)]
    all_to_all x1 -> x0, starting transfers between devices: 7.58 us -> none  [shards(): lax.all_to_all(wanted, 'db', split_axis=0, concat_axis=0, tiled=True)]
    ppermute x1, waiting for transfers between devices: 0.78 us -> 3.61 us  [shards(): before = lax.ppermute(sent, 'seq', [(i, i + 1) for i in range(count - 1)])]
    ppermute x1, waiting for transfers between devices: 0.01 us -> 2.09 us  [shards(): lax.ppermute(cross_query[:STRETCH], 'seq', [(i, i - 1) for i in range(1,...]
    pallas_call x3 -> x4, Pallas kernels: 40.2 us -> 40.1 us  [the longest x1 22.9 us: cross(): pl.pallas_call(functools.partial(cross_kernel, LOG2E / math.sqrt(d), half...]
  transfers between devices with their start and end apart: 19 -> 19, of which waited for: 11 -> 10; matrix products, arithmetic and copies ran while one was open for 2% -> 2% of each run, Pallas kernels for 17% -> 25%
where the time goes in v3:
time: 189 us; the launch traced here: 187 us
  Pallas kernels  73.6 us (39%)
  waiting for transfers between devices  50.8 us (27%)
  starting transfers between devices  27.4 us (14%)
  between operations  14.3 us (8%)
  blocking collectives  13 us (7%)
  local copies, waits for them, and re-layouts  5.47 us (3%)
  other arithmetic  2.14 us (1%)
    ppermute x15, waiting for transfers between devices, hop(): return lax.ppermute(value, 'seq', pairs)  44.7 us
    pallas_call x1, Pallas kernels, cross(): pl.pallas_call(functools.partial(cross_kernel, LOG2E / math.sqrt(d), half...  22.9 us
    pallas_call x1, Pallas kernels, self_attention(): pl.pallas_call(functools.partial(self_kernel, chips, LOG2E / math.sqrt(d)...  19.8 us
    ppermute x15, starting transfers between devices, hop(): return lax.ppermute(value, 'seq', pairs)  16.2 us
    all_to_all x1, blocking collectives, shards(): lax.all_to_all(wanted, 'db', split_axis=0, concat_axis=0, tiled=True)  13 us
    pallas_call x1, Pallas kernels, encode(): pl.pallas_call(encode_kernel, grid_spec=pltpu.PrefetchScalarGridSpec(num_...  12.1 us
    pallas_call x1, Pallas kernels, fetch(): pl.pallas_call(fetch_kernel, grid_spec=pltpu.PrefetchScalarGridSpec(num_s...  7.09 us
    pallas_call x1, Pallas kernels, pack(): pl.pallas_call(functools.partial(pack_kernel, chips), in_specs=[ANY] * 3,...  4.8 us
  transfers between devices with their start and end apart: 19, of which 10 were waited for; matrix products, arithmetic and copies ran while one was open for 2% of the time, Pallas kernels for 25%

profile of v3, /device:TPU:1, one launch (start us, length us, event | category | flops | bytes accessed | tf_op | source)
XLA Modules:
  0.0 186.6 jit_solution(2795897335393712465)
XLA Ops:
  7.2 0.0 all-gather.2.cloned.1.call-start
  7.2 2.3 %half.1 = bf16[352,896]{1,0:T(8,128)(2,1)} custom-call(bf16[224,896]{1,0:T(8,128)(2,1)} %bitcast.4, bf16[224,896]{1,0:T(8,128)(2,1)} %ffn_out.1, bf16[896,256]{1,0:T(8,128)(2,1)} %projection.1), custom_call_target="tpu_custom_call" | custom-call | bytes 802816 | tf_op jit(solution)/shard_map/half/pallas_call | solution.py:104
  9.5 0.0 all-gather.2.cloned.1.call-update
  9.5 0.0 copy-start.9
  9.6 0.0 copy-start.10
  9.6 4.8 %pack.1 = (bf16[2,3,384,256]{3,2,1,0:T(8,128)(2,1)}, bf16[2,3,384,256]{3,2,1,0:T(8,128)(2,1)}, bf16[2,3,384,256]{3,2,1,0:T(8,128)(2,1)}, bf16[2,3,384,256]{3,2,1,0:T(8,128)(2,1)}) custom-call(bf16[384,2048]{1,0:T(8,128)(2,1)} %query, bf16[384,2048]{1,0:T(8,128)(2,1)} %key, bf16[384,2048]{1,0:T(8,128)(2,1)} %value), custom_call_target="tpu_custom_call" | custom-call | bytes 9437184 | tf_op jit(solution)/shard_map/pack/pallas_call | solution.py:333
  14.4 4.5 %collective-permute-start = (bf16[2,3,384,256]{3,2,1,0:T(8,128)(2,1)}, bf16[2,3,384,256]{3,2,1,0:T(8,128)(2,1)S(1)}, u32[]{:S(2)}, u32[]{:S(2)}) collective-permute-start(bf16[2,3,384,256]{3,2,1,0:T(8,128)(2,1)} %get-tuple-element.28), channel_id=1, source_target_pairs={{0,4},{1,5},{2,6},{3,7},{4,0},{5,1},{6,2},{7,3},{8,12},{9,13},{10,... | collective-permute-start | bytes 3538952 | tf_op jit(solution)/shard_map/ppermute | solution.py:36
  18.9 0.7 collective-permute-start.1
  19.6 1.9 %collective-permute-start.2 = (bf16[2,3,384,256]{3,2,1,0:T(8,128)(2,1)}, bf16[2,3,384,256]{3,2,1,0:T(8,128)(2,1)}, u32[]{:S(2)}, u32[]{:S(2)}) collective-permute-start(bf16[2,3,384,256]{3,2,1,0:T(8,128)(2,1)} %get-tuple-element.30), channel_id=1, source_target_pairs={{0,6},{1,7},{2,0},{3,1},{4,2},{5,3},{6,4},{7,5},{8,14},{9,15},{10,... | collective-permute-start | bytes 3538952 | tf_op jit(solution)/shard_map/ppermute | solution.py:36
  21.6 0.1 copy.20
  21.7 0.1 reshape.29
  21.7 0.2 convert_reduce_fusion
  21.9 0.1 copy.21
  22.0 0.1 broadcast_in_dim.18
  22.1 0.1 select_reduce_fusion
  22.2 0.1 all_to_all.9
  22.3 13.0 %all_to_all.14 = s32[16,1,2]{2,1,0:T(1,128)S(1)} all-to-all(s32[16,1,2]{2,1,0:T(1,128)S(1)} %bitcast.6), channel_id=1, replica_groups=mesh['db'=16,'seq'=8] {'db'}, dimensions={0} | all-to-all | bytes 256 | tf_op jit(solution)/shard_map/all_to_all | solution.py:471
  35.3 0.5 broadcast.12
  35.7 0.6 reduce.3
  36.3 0.7 reshape.30.asked
  37.0 7.1 %fetch.1 = bf16[32,64,896]{2,1,0:T(8,128)(2,1)} custom-call(s32[32]{0:T(128)} %reshape.30.asked, bf16[32,64,896]{2,1,0:T(8,128)(2,1)} %database.1), custom_call_target="tpu_custom_call" | custom-call | bytes 7340032 | tf_op jit(solution)/shard_map/fetch/pallas_call | solution.py:77
  44.1 0.0 copy-start.11
  44.1 4.7 %all-to-all-start.1 = ((bf16[32,64,896]{2,1,0:T(8,128)(2,1)}), bf16[32,64,896]{2,1,0:T(8,128)(2,1)}, u32[]{:S(2)}, u32[]{:S(2)}) async-start(bf16[32,64,896]{2,1,0:T(8,128)(2,1)} %fetch.1), calls=%async_computation.1 | async-start | bytes 7340032 | tf_op jit(solution)/shard_map/all_to_all | solution.py:479
  48.8 0.0 collective-permute-done.refs_1_
  48.8 0.0 copy-start.12
  48.8 22.1 %collective-permute-done.1.refs_2_ = bf16[2,3,384,256]{3,2,1,0:T(8,128)(2,1)S(1)} collective-permute-done((bf16[2,3,384,256]{3,2,1,0:T(8,128)(2,1)}, bf16[2,3,384,256]{3,2,1,0:T(8,128)(2,1)S(1)}, u32[]{:S(2)}, u32[]{:S(2)}) %collective-permute-start.1) | collective-permute-done | bytes 1179680 | tf_op jit(solution)/shard_map/ppermute | solution.py:36
  70.9 0.0 collective-permute-done.2.refs_3_
  70.9 0.0 copy-start
  70.9 1.3 collective-permute-start.3
  72.2 0.1 collective-permute-start.4
  72.3 0.4 collective-permute-start.5
  72.7 0.1 collective-permute-start.6
  72.8 1.9 %collective-permute-done.3.refs_4_ = bf16[2,3,384,256]{3,2,1,0:T(8,128)(2,1)S(1)} collective-permute-done((bf16[2,3,384,256]{3,2,1,0:T(8,128)(2,1)S(1)}, bf16[2,3,384,256]{3,2,1,0:T(8,128)(2,1)S(1)}, u32[]{:S(2)}, u32[]{:S(2)}) %collective-permute-start.3) | collective-permute-done | bytes 1179680 | tf_op jit(solution)/shard_map/ppermute | solution.py:36
  74.7 3.4 %collective-permute-done.4.refs_5_ = bf16[2,3,384,256]{3,2,1,0:T(8,128)(2,1)S(1)} collective-permute-done((bf16[2,3,384,256]{3,2,1,0:T(8,128)(2,1)S(1)}, bf16[2,3,384,256]{3,2,1,0:T(8,128)(2,1)S(1)}, u32[]{:S(2)}, u32[]{:S(2)}) %collective-permute-start.4) | collective-permute-done | bytes 1179680 | tf_op jit(solution)/shard_map/ppermute | solution.py:36
  78.0 1.7 collective-permute-done.5.refs_6_
  79.7 1.0 copy-done.16
  80.8 19.8 %causal.1 = (bf16[2,384,256]{2,1,0:T(8,128)(2,1)}, bf16[2,384,256]{2,1,0:T(8,128)(2,1)}, bf16[2,384,256]{2,1,0:T(8,128)(2,1)}, bf16[2,384,256]{2,1,0:T(8,128)(2,1)}) custom-call(bf16[2,3,384,256]{3,2,1,0:T(8,128)(2,1)} %get-tuple-element.31.refs_0_, bf16[2,3,384,256]{3,2,1,0:T(8,128)(2,1)} %copy-done.12, bf16[2,3,384,256]{3,2,1,0:T(8,128)(2,1)} %copy-done.13, ...), custom_call_target="tpu_custom_call" | custom-call | flops 7000000000 | bytes 8000000 | tf_op jit(solution)/shard_map/causal/pallas_call | solution.py:390
  100.6 1.8 collective-permute-start.7
  102.4 1.4 collective-permute-start.8
  103.8 0.1 collective-permute-start.9
  103.9 3.1 %collective-permute-start.14 = (bf16[64,2048]{1,0:T(8,128)(2,1)S(1)}, bf16[64,2048]{1,0:T(8,128)(2,1)S(1)}, u32[]{:S(2)}, u32[]{:S(2)}) collective-permute-start(bf16[64,2048]{1,0:T(8,128)(2,1)S(1)} %slice.10), channel_id=1, source_target_pairs={{1,0},{2,1},{3,2},{4,3},{5,4},{6,5},{7,6},{9,8},{10,9},{11,10},{12... | collective-permute-start | bytes 786440 | tf_op jit(solution)/shard_map/ppermute | solution.py:480
  107.0 0.1 collective-permute-start.10
  107.1 5.7 %collective-permute-done.7.refs_1_ = bf16[2,384,256]{2,1,0:T(8,128)(2,1)S(1)} collective-permute-done((bf16[2,384,256]{2,1,0:T(8,128)(2,1)}, bf16[2,384,256]{2,1,0:T(8,128)(2,1)S(1)}, u32[]{:S(2)}, u32[]{:S(2)}) %collective-permute-start.7) | collective-permute-done | bytes 393248 | tf_op jit(solution)/shard_map/ppermute | solution.py:36
  112.8 2.0 %collective-permute-start.11 = (bf16[2,384,256]{2,1,0:T(8,128)(2,1)S(1)}, bf16[2,384,256]{2,1,0:T(8,128)(2,1)S(1)}, u32[]{:S(2)}, u32[]{:S(2)}) collective-permute-start(bf16[2,384,256]{2,1,0:T(8,128)(2,1)S(1)} %collective-permute-done.7.refs_1_), channel_id=1, source_target_pairs={{0,1},{1,0},{2,3},{3,2},{4,5},{5,4},{6,7},{7,6},{8,9},{9,8},{10,11... | collective-permute-start | bytes 1179656 | tf_op jit(solution)/shard_map/ppermute | solution.py:36
  114.8 6.4 %collective-permute-done.8.refs_2_ = bf16[2,384,256]{2,1,0:T(8,128)(2,1)S(1)} collective-permute-done((bf16[2,384,256]{2,1,0:T(8,128)(2,1)}, bf16[2,384,256]{2,1,0:T(8,128)(2,1)S(1)}, u32[]{:S(2)}, u32[]{:S(2)}) %collective-permute-start.8) | collective-permute-done | bytes 393248 | tf_op jit(solution)/shard_map/ppermute | solution.py:36
  121.2 1.1 collective-permute-start.12
  122.3 0.1 collective-permute-start.13
  122.4 0.3 slice.9
  122.7 2.1 %collective-permute-done.14 = bf16[64,2048]{1,0:T(8,128)(2,1)S(1)} collective-permute-done((bf16[64,2048]{1,0:T(8,128)(2,1)S(1)}, bf16[64,2048]{1,0:T(8,128)(2,1)S(1)}, u32[]{:S(2)}, u32[]{:S(2)}) %collective-permute-start.14) | collective-permute-done | bytes 262176 | tf_op jit(solution)/shard_map/ppermute | solution.py:480
  124.8 1.3 pad_maximum_fusion.query
  126.2 0.7 copy-done.4
  126.9 0.2 copy-done.5
  127.1 0.2 copy-done.6
  127.3 0.7 copy-done.7
  128.0 2.8 %unpack.1 = bf16[384,2048]{1,0:T(8,128)(2,1)} custom-call(bf16[2,384,256]{2,1,0:T(8,128)(2,1)} %get-tuple-element.35.refs_0_, bf16[2,384,256]{2,1,0:T(8,128)(2,1)} %copy-done.1, bf16[2,384,256]{2,1,0:T(8,128)(2,1)} %copy-done.2, bf16[2,384,256]{2,1,0:T(8,128)(2,1)} %copy-done.3, bf16[2,384,256]{2,1,0:T(8,128)(2,1)} %copy-done.4, ...), custom_call_target="tpu_custom_call" | custom-call | bytes 3145728 | tf_op jit(solution)/shard_map/unpack/pallas_call | solution.py:424
  130.8 0.4 all-gather.2.cloned.1.call-done
  131.2 0.7 collective-permute-start.15
  131.9 12.1 %encode.1 = (f32[768,896]{1,0:T(8,128)}, bf16[768,896]{1,0:T(8,128)(2,1)}) custom-call(s32[12]{0:T(128)} %copy-done.17, bf16[32,64,896]{2,1,0:T(8,128)(2,1)} %all-to-all-done.1.arrived, bf16[16,352,896]{2,1,0:T(8,128)(2,1)} %bitcast.8), custom_call_target="tpu_custom_call" | custom-call | flops 5000000000 | bytes 12000000 | tf_op jit(solution)/shard_map/encode/pallas_call | solution.py:154
  144.0 3.5 %collective-permute-done.15.other = bf16[16,352,896]{2,1,0:T(8,128)(2,1)} collective-permute-done((bf16[16,352,896]{2,1,0:T(8,128)(2,1)}, bf16[16,352,896]{2,1,0:T(8,128)(2,1)}, u32[]{:S(2)}, u32[]{:S(2)}) %collective-permute-start.15) | collective-permute-done | bytes 10092576 | tf_op jit(solution)/shard_map/ppermute | solution.py:36
  147.5 22.9 %cross.1 = (bf16[384,2048]{1,0:T(8,128)(2,1)}, bf16[64,2048]{1,0:T(8,128)(2,1)}) custom-call(f32[768,896]{1,0:T(8,128)} %get-tuple-element.41.before, bf16[768,896]{1,0:T(8,128)(2,1)} %get-tuple-element.42.normed_in, bf16[16,352,896]{2,1,0:T(8,128)(2,1)} %bitcast.9, bf16[16,352,896]{2,1,0:T(8,128)(2,1)} %collective-permute-done.15.other, ...), custom_call_target="tpu_custom_call" | custom-call | flops 12000000000 | bytes 20000000 | tf_op jit(solution)/shard_map/cross/pallas_call | solution.py:257
  170.4 3.4 %collective-permute-start.16 = (bf16[64,2048]{1,0:T(8,128)(2,1)}, bf16[64,2048]{1,0:T(8,128)(2,1)S(1)}, u32[]{:S(2)}, u32[]{:S(2)}) collective-permute-start(bf16[64,2048]{1,0:T(8,128)(2,1)} %get-tuple-element.45), channel_id=1, source_target_pairs={{0,1},{1,2},{2,3},{3,4},{4,5},{5,6},{6,7},{8,9},{9,10},{10,11},{11... | collective-permute-start | bytes 786440 | tf_op jit(solution)/shard_map/ppermute | solution.py:492
  173.7 3.6 %collective-permute-done.16.before = bf16[64,2048]{1,0:T(8,128)(2,1)S(1)} collective-permute-done((bf16[64,2048]{1,0:T(8,128)(2,1)}, bf16[64,2048]{1,0:T(8,128)(2,1)S(1)}, u32[]{:S(2)}, u32[]{:S(2)}) %collective-permute-start.16) | collective-permute-done | bytes 262176 | tf_op jit(solution)/shard_map/ppermute | solution.py:492
  177.3 0.7 copy-done.8
  178.0 1.8 mend.1
  (34 shorter events, 0.1 us)
Async XLA Ops:
  7.2 124.1 %all-gather.2.cloned.1.call-start = ((), (), s32[]{:S(2)}) async-start(), calls=%async_computation.2 | async-start | bytes 10723328 | tf_op jit(solution)/shard_map/all_gather | solution.py:468
  9.5 12.0 %copy-start.9 = (s32[6,2]{0,1:T(2,128)S(1)}, s32[6,2]{0,1:T(2,128)}, u32[]{:S(2)}) copy-start(s32[6,2]{0,1:T(2,128)} %param.14) | copy-start | bytes 148
  9.6 12.4 %copy-start.10 = (s32[6,2]{0,1:T(2,128)S(1)}, s32[6,2]{0,1:T(2,128)}, u32[]{:S(2)}) copy-start(s32[6,2]{0,1:T(2,128)} %param.15) | copy-start | bytes 148
  14.4 34.4 %collective-permute-start = (bf16[2,3,384,256]{3,2,1,0:T(8,128)(2,1)}, bf16[2,3,384,256]{3,2,1,0:T(8,128)(2,1)S(1)}, u32[]{:S(2)}, u32[]{:S(2)}) collective-permute-start(bf16[2,3,384,256]{3,2,1,0:T(8,128)(2,1)} %get-tuple-element.28), channel_id=1, source_target_pairs={{0,4},{1,5},{2,6},{3,7},{4,0},{5,1},{6,2},{7,3},{8,12},{9,13},{10,... | collective-permute-start | bytes 3538952 | tf_op jit(solution)/shard_map/ppermute | solution.py:36
  18.9 52.0 %collective-permute-start.1 = (bf16[2,3,384,256]{3,2,1,0:T(8,128)(2,1)}, bf16[2,3,384,256]{3,2,1,0:T(8,128)(2,1)S(1)}, u32[]{:S(2)}, u32[]{:S(2)}) collective-permute-start(bf16[2,3,384,256]{3,2,1,0:T(8,128)(2,1)} %get-tuple-element.29), channel_id=1, source_target_pairs={{0,2},{1,3},{2,4},{3,5},{4,6},{5,7},{6,0},{7,1},{8,10},{9,11},{10,... | collective-permute-start | bytes 3538952 | tf_op jit(solution)/shard_map/ppermute | solution.py:36
  19.6 51.3 %collective-permute-start.2 = (bf16[2,3,384,256]{3,2,1,0:T(8,128)(2,1)}, bf16[2,3,384,256]{3,2,1,0:T(8,128)(2,1)}, u32[]{:S(2)}, u32[]{:S(2)}) collective-permute-start(bf16[2,3,384,256]{3,2,1,0:T(8,128)(2,1)} %get-tuple-element.30), channel_id=1, source_target_pairs={{0,6},{1,7},{2,0},{3,1},{4,2},{5,3},{6,4},{7,5},{8,14},{9,15},{10,... | collective-permute-start | bytes 3538952 | tf_op jit(solution)/shard_map/ppermute | solution.py:36
  22.1 22.0 %copy-start.17 = (s32[12]{0:T(128)}, s32[12]{0:T(128)S(1)}, u32[]{:S(2)}) copy-start(s32[12]{0:T(128)S(1)} %multiply_add_fusion.slot) | copy-start | bytes 148
  44.1 26.8 %copy-start.11 = (bf16[2,3,384,256]{3,2,1,0:T(8,128)(2,1)S(1)}, bf16[2,3,384,256]{3,2,1,0:T(8,128)(2,1)}, u32[]{:S(2)}) copy-start(bf16[2,3,384,256]{3,2,1,0:T(8,128)(2,1)} %get-tuple-element.31.refs_0_) | copy-start | bytes 3538948
  44.1 86.8 %all-to-all-start.1 = ((bf16[32,64,896]{2,1,0:T(8,128)(2,1)}), bf16[32,64,896]{2,1,0:T(8,128)(2,1)}, u32[]{:S(2)}, u32[]{:S(2)}) async-start(bf16[32,64,896]{2,1,0:T(8,128)(2,1)} %fetch.1), calls=%async_computation.1 | async-start | bytes 7340032 | tf_op jit(solution)/shard_map/all_to_all | solution.py:479
  48.8 32.0 %copy-start.12 = (bf16[2,3,384,256]{3,2,1,0:T(8,128)(2,1)}, bf16[2,3,384,256]{3,2,1,0:T(8,128)(2,1)S(1)}, u32[]{:S(2)}) copy-start(bf16[2,3,384,256]{3,2,1,0:T(8,128)(2,1)S(1)} %collective-permute-done.refs_1_) | copy-start | bytes 3538948
  70.9 9.8 %copy-start.13 = (bf16[2,3,384,256]{3,2,1,0:T(8,128)(2,1)}, bf16[2,3,384,256]{3,2,1,0:T(8,128)(2,1)S(1)}, u32[]{:S(2)}) copy-start(bf16[2,3,384,256]{3,2,1,0:T(8,128)(2,1)S(1)} %collective-permute-done.1.refs_2_) | copy-start | bytes 3538948
  70.9 32.9 %copy-start = (bf16[384,2048]{1,0:T(8,128)(2,1)S(1)}, bf16[384,2048]{1,0:T(8,128)(2,1)}, u32[]{:S(2)}) copy-start(bf16[384,2048]{1,0:T(8,128)(2,1)} %param.13) | copy-start | bytes 4718596
  70.9 3.7 %collective-permute-start.3 = (bf16[2,3,384,256]{3,2,1,0:T(8,128)(2,1)S(1)}, bf16[2,3,384,256]{3,2,1,0:T(8,128)(2,1)S(1)}, u32[]{:S(2)}, u32[]{:S(2)}) collective-permute-start(bf16[2,3,384,256]{3,2,1,0:T(8,128)(2,1)S(1)} %copy-done.11), channel_id=1, source_target_pairs={{0,1},{1,0},{2,3},{3,2},{4,5},{5,4},{6,7},{7,6},{8,9},{9,8},{10,11... | collective-permute-start | bytes 3538952 | tf_op jit(solution)/shard_map/ppermute | solution.py:36
  72.2 5.8 %collective-permute-start.4 = (bf16[2,3,384,256]{3,2,1,0:T(8,128)(2,1)S(1)}, bf16[2,3,384,256]{3,2,1,0:T(8,128)(2,1)S(1)}, u32[]{:S(2)}, u32[]{:S(2)}) collective-permute-start(bf16[2,3,384,256]{3,2,1,0:T(8,128)(2,1)S(1)} %collective-permute-done.refs_1_), channel_id=1, source_target_pairs={{0,1},{1,0},{2,3},{3,2},{4,5},{5,4},{6,7},{7,6},{8,9},{9,8},{10,11... | collective-permute-start | bytes 3538952 | tf_op jit(solution)/shard_map/ppermute | solution.py:36
  72.3 7.5 %collective-permute-start.5 = (bf16[2,3,384,256]{3,2,1,0:T(8,128)(2,1)S(1)}, bf16[2,3,384,256]{3,2,1,0:T(8,128)(2,1)S(1)}, u32[]{:S(2)}, u32[]{:S(2)}) collective-permute-start(bf16[2,3,384,256]{3,2,1,0:T(8,128)(2,1)S(1)} %collective-permute-done.1.refs_2_), channel_id=1, source_target_pairs={{0,1},{1,0},{2,3},{3,2},{4,5},{5,4},{6,7},{7,6},{8,9},{9,8},{10,11... | collective-permute-start | bytes 3538952 | tf_op jit(solution)/shard_map/ppermute | solution.py:36
  72.7 8.0 %collective-permute-start.6 = (bf16[2,3,384,256]{3,2,1,0:T(8,128)(2,1)}, bf16[2,3,384,256]{3,2,1,0:T(8,128)(2,1)}, u32[]{:S(2)}, u32[]{:S(2)}) collective-permute-start(bf16[2,3,384,256]{3,2,1,0:T(8,128)(2,1)} %collective-permute-done.2.refs_3_), channel_id=1, source_target_pairs={{0,1},{1,0},{2,3},{3,2},{4,5},{5,4},{6,7},{7,6},{8,9},{9,8},{10,11... | collective-permute-start | bytes 3538952 | tf_op jit(solution)/shard_map/ppermute | solution.py:36
  74.7 6.1 %copy-start.14 = (bf16[2,3,384,256]{3,2,1,0:T(8,128)(2,1)}, bf16[2,3,384,256]{3,2,1,0:T(8,128)(2,1)S(1)}, u32[]{:S(2)}) copy-start(bf16[2,3,384,256]{3,2,1,0:T(8,128)(2,1)S(1)} %collective-permute-done.3.refs_4_) | copy-start | bytes 3538948
  78.0 2.7 %copy-start.15 = (bf16[2,3,384,256]{3,2,1,0:T(8,128)(2,1)}, bf16[2,3,384,256]{3,2,1,0:T(8,128)(2,1)S(1)}, u32[]{:S(2)}) copy-start(bf16[2,3,384,256]{3,2,1,0:T(8,128)(2,1)S(1)} %collective-permute-done.4.refs_5_) | copy-start | bytes 3538948
  79.7 1.0 copy-start.16
  100.6 12.2 %collective-permute-start.7 = (bf16[2,384,256]{2,1,0:T(8,128)(2,1)}, bf16[2,384,256]{2,1,0:T(8,128)(2,1)S(1)}, u32[]{:S(2)}, u32[]{:S(2)}) collective-permute-start(bf16[2,384,256]{2,1,0:T(8,128)(2,1)} %get-tuple-element.36), channel_id=1, source_target_pairs={{0,4},{1,5},{2,6},{3,7},{4,0},{5,1},{6,2},{7,3},{8,12},{9,13},{10,... | collective-permute-start | bytes 1179656 | tf_op jit(solution)/shard_map/ppermute | solution.py:36
  102.4 18.8 %collective-permute-start.8 = (bf16[2,384,256]{2,1,0:T(8,128)(2,1)}, bf16[2,384,256]{2,1,0:T(8,128)(2,1)S(1)}, u32[]{:S(2)}, u32[]{:S(2)}) collective-permute-start(bf16[2,384,256]{2,1,0:T(8,128)(2,1)} %get-tuple-element.37), channel_id=1, source_target_pairs={{0,6},{1,7},{2,0},{3,1},{4,2},{5,3},{6,4},{7,5},{8,14},{9,15},{10,... | collective-permute-start | bytes 1179656 | tf_op jit(solution)/shard_map/ppermute | solution.py:36
  103.8 18.6 %collective-permute-start.9 = (bf16[2,384,256]{2,1,0:T(8,128)(2,1)}, bf16[2,384,256]{2,1,0:T(8,128)(2,1)S(1)}, u32[]{:S(2)}, u32[]{:S(2)}) collective-permute-start(bf16[2,384,256]{2,1,0:T(8,128)(2,1)} %get-tuple-element.38), channel_id=1, source_target_pairs={{0,2},{1,3},{2,4},{3,5},{4,6},{5,7},{6,0},{7,1},{8,10},{9,11},{10,... | collective-permute-start | bytes 1179656 | tf_op jit(solution)/shard_map/ppermute | solution.py:36
  103.9 21.0 %collective-permute-start.14 = (bf16[64,2048]{1,0:T(8,128)(2,1)S(1)}, bf16[64,2048]{1,0:T(8,128)(2,1)S(1)}, u32[]{:S(2)}, u32[]{:S(2)}) collective-permute-start(bf16[64,2048]{1,0:T(8,128)(2,1)S(1)} %slice.10), channel_id=1, source_target_pairs={{1,0},{2,1},{3,2},{4,3},{5,4},{6,5},{7,6},{9,8},{10,9},{11,10},{12... | collective-permute-start | bytes 786440 | tf_op jit(solution)/shard_map/ppermute | solution.py:480
  107.0 19.1 %collective-permute-start.10 = (bf16[2,384,256]{2,1,0:T(8,128)(2,1)}, bf16[2,384,256]{2,1,0:T(8,128)(2,1)S(1)}, u32[]{:S(2)}, u32[]{:S(2)}) collective-permute-start(bf16[2,384,256]{2,1,0:T(8,128)(2,1)} %get-tuple-element.35.refs_0_), channel_id=1, source_target_pairs={{0,1},{1,0},{2,3},{3,2},{4,5},{5,4},{6,7},{7,6},{8,9},{9,8},{10,11... | collective-permute-start | bytes 1179656 | tf_op jit(solution)/shard_map/ppermute | solution.py:36
  112.8 13.4 %copy-start.1 = (bf16[2,384,256]{2,1,0:T(8,128)(2,1)}, bf16[2,384,256]{2,1,0:T(8,128)(2,1)S(1)}, u32[]{:S(2)}) copy-start(bf16[2,384,256]{2,1,0:T(8,128)(2,1)S(1)} %collective-permute-done.7.refs_1_) | copy-start | bytes 1179652
  112.8 13.4 %collective-permute-start.11 = (bf16[2,384,256]{2,1,0:T(8,128)(2,1)S(1)}, bf16[2,384,256]{2,1,0:T(8,128)(2,1)S(1)}, u32[]{:S(2)}, u32[]{:S(2)}) collective-permute-start(bf16[2,384,256]{2,1,0:T(8,128)(2,1)S(1)} %collective-permute-done.7.refs_1_), channel_id=1, source_target_pairs={{0,1},{1,0},{2,3},{3,2},{4,5},{5,4},{6,7},{7,6},{8,9},{9,8},{10,11... | collective-permute-start | bytes 1179656 | tf_op jit(solution)/shard_map/ppermute | solution.py:36
  121.2 4.9 %copy-start.2 = (bf16[2,384,256]{2,1,0:T(8,128)(2,1)}, bf16[2,384,256]{2,1,0:T(8,128)(2,1)S(1)}, u32[]{:S(2)}) copy-start(bf16[2,384,256]{2,1,0:T(8,128)(2,1)S(1)} %collective-permute-done.8.refs_2_) | copy-start | bytes 1179652
  121.2 5.0 %collective-permute-start.12 = (bf16[2,384,256]{2,1,0:T(8,128)(2,1)S(1)}, bf16[2,384,256]{2,1,0:T(8,128)(2,1)S(1)}, u32[]{:S(2)}, u32[]{:S(2)}) collective-permute-start(bf16[2,384,256]{2,1,0:T(8,128)(2,1)S(1)} %collective-permute-done.8.refs_2_), channel_id=1, source_target_pairs={{0,1},{1,0},{2,3},{3,2},{4,5},{5,4},{6,7},{7,6},{8,9},{9,8},{10,11... | collective-permute-start | bytes 1179656 | tf_op jit(solution)/shard_map/ppermute | solution.py:36
  122.3 3.8 %copy-start.3 = (bf16[2,384,256]{2,1,0:T(8,128)(2,1)}, bf16[2,384,256]{2,1,0:T(8,128)(2,1)S(1)}, u32[]{:S(2)}) copy-start(bf16[2,384,256]{2,1,0:T(8,128)(2,1)S(1)} %collective-permute-done.9.refs_3_) | copy-start | bytes 1179652
  122.3 3.9 %collective-permute-start.13 = (bf16[2,384,256]{2,1,0:T(8,128)(2,1)S(1)}, bf16[2,384,256]{2,1,0:T(8,128)(2,1)S(1)}, u32[]{:S(2)}, u32[]{:S(2)}) collective-permute-start(bf16[2,384,256]{2,1,0:T(8,128)(2,1)S(1)} %collective-permute-done.9.refs_3_), channel_id=1, source_target_pairs={{0,1},{1,0},{2,3},{3,2},{4,5},{5,4},{6,7},{7,6},{8,9},{9,8},{10,11... | collective-permute-start | bytes 1179656 | tf_op jit(solution)/shard_map/ppermute | solution.py:36
  126.1 0.7 copy-start.4
  126.2 0.9 copy-start.5
  126.2 1.1 copy-start.6
  127.3 0.7 copy-start.7
  131.2 16.2 %collective-permute-start.15 = (bf16[16,352,896]{2,1,0:T(8,128)(2,1)}, bf16[16,352,896]{2,1,0:T(8,128)(2,1)}, u32[]{:S(2)}, u32[]{:S(2)}) collective-permute-start(bf16[16,352,896]{2,1,0:T(8,128)(2,1)} %bitcast.7), channel_id=1, source_target_pairs={{0,1},{1,0},{2,3},{3,2},{4,5},{5,4},{6,7},{7,6},{8,9},{9,8},{10,11... | collective-permute-start | bytes 30277640 | tf_op jit(solution)/shard_map/ppermute | solution.py:36
  170.4 7.0 %collective-permute-start.16 = (bf16[64,2048]{1,0:T(8,128)(2,1)}, bf16[64,2048]{1,0:T(8,128)(2,1)S(1)}, u32[]{:S(2)}, u32[]{:S(2)}) collective-permute-start(bf16[64,2048]{1,0:T(8,128)(2,1)} %get-tuple-element.45), channel_id=1, source_target_pairs={{0,1},{1,2},{2,3},{3,4},{4,5},{5,6},{6,7},{8,9},{9,10},{10,11},{11... | collective-permute-start | bytes 786440 | tf_op jit(solution)/shard_map/ppermute | solution.py:492
  177.3 0.7 copy-start.8
Sparse Core Ops, SparseCore 0:
  10.1 121.0 all-gather.1

commit v4 on v3

--- a/solution.py
+++ b/solution.py
@@ -63,7 +63,7 @@
     relay(
         [
             pltpu.make_async_copy(
-                database.at[jnp.clip(asked[i], 0, last)], held.at[i], sem.at[0, i]
+                database.at[jnp.clip(asked[i // CAP, i % CAP], 0, last)], held.at[i], sem.at[0, i]
             )
             for i in range(count)
         ],
@@ -72,7 +72,7 @@
 
 
 def fetch(asked, database):
-    slots = asked.shape[0]
+    slots = math.prod(asked.shape)
     shape = (slots, *database.shape[1:])
     return pl.pallas_call(
         fetch_kernel,
@@ -468,12 +468,12 @@
     mine = lax.all_gather(part, "db", axis=0, tiled=True).reshape(owners, -1, deep)
 
     slot, wanted = requests_of(retrieval_shard, retrieval_row)
+    self_query, self_key, self_value, wanted = together((self_query, self_key, self_value, wanted))
     asked = lax.all_to_all(wanted, "db", split_axis=0, concat_axis=0, tiled=True)
-    self_query, self_key, self_value, _ = together((self_query, self_key, self_value, wanted))
     parts = pack(chips, self_query, self_key, self_value)
     same = [parts[0]] + [hop(p, k, 0) for p, k in zip(parts[1:], HOPS[1:])]
 
-    found = fetch(asked.reshape(-1), database)
+    found = fetch(asked, database)
     *same, _ = together((*same, found))
     flipped = [hop(p, 0, 1) for p in same]
     arrived = lax.all_to_all(found, "db", split_axis=0, concat_axis=0, tiled=True)

time: 189 us -> 188 us (level)
  waiting for transfers between devices: 50.8 us -> 53.1 us
    ppermute x15, waiting for transfers between devices: 44.7 us -> 47.3 us  [hop(): return lax.ppermute(value, 'seq', pairs)]
  transfers between devices with their start and end apart: 19 -> 19, of which waited for: 10 -> 9; matrix products, arithmetic and copies ran while one was open for 2% -> 1% of each run, Pallas kernels for 25% -> 25%
where the time goes in v4:
time: 188 us; the launch traced here: 186 us
  Pallas kernels  73.6 us (39%)
  waiting for transfers between devices  53.1 us (28%)
  starting transfers between devices  26.4 us (14%)
  between operations  14.3 us (8%)
  blocking collectives  13.1 us (7%)
  local copies, waits for them, and re-layouts  4.36 us (2%)
    ppermute x15, waiting for transfers between devices, hop(): return lax.ppermute(value, 'seq', pairs)  47.3 us
    pallas_call x1, Pallas kernels, cross(): pl.pallas_call(functools.partial(cross_kernel, LOG2E / math.sqrt(d), half...  22.9 us
    pallas_call x1, Pallas kernels, self_attention(): pl.pallas_call(functools.partial(self_kernel, chips, LOG2E / math.sqrt(d)...  19.8 us
    ppermute x15, starting transfers between devices, hop(): return lax.ppermute(value, 'seq', pairs)  15.9 us
    all_to_all x1, blocking collectives, shards(): lax.all_to_all(wanted, 'db', split_axis=0, concat_axis=0, tiled=True)  13.1 us
    pallas_call x1, Pallas kernels, encode(): pl.pallas_call(encode_kernel, grid_spec=pltpu.PrefetchScalarGridSpec(num_...  12.1 us
    pallas_call x1, Pallas kernels, fetch(): pl.pallas_call(fetch_kernel, grid_spec=pltpu.PrefetchScalarGridSpec(num_s...  7.14 us
    pallas_call x1, Pallas kernels, pack(): pl.pallas_call(functools.partial(pack_kernel, chips), in_specs=[ANY] * 3,...  4.79 us
  transfers between devices with their start and end apart: 19, of which 9 were waited for; matrix products, arithmetic and copies ran while one was open for 1% of the time, Pallas kernels for 25%

profile of v4, /device:TPU:1, one launch (start us, length us, event | category | flops | bytes accessed | tf_op | source)
XLA Modules:
  0.0 186.3 jit_solution(9679123076948322828)
XLA Ops:
  7.2 0.0 all-gather.2.cloned.1.call-start
  7.2 2.3 %half.1 = bf16[352,896]{1,0:T(8,128)(2,1)} custom-call(bf16[224,896]{1,0:T(8,128)(2,1)} %bitcast.7, bf16[224,896]{1,0:T(8,128)(2,1)} %ffn_out.1, bf16[896,256]{1,0:T(8,128)(2,1)} %projection.1), custom_call_target="tpu_custom_call" | custom-call | bytes 802816 | tf_op jit(solution)/shard_map/half/pallas_call | solution.py:104
  9.5 0.0 all-gather.2.cloned.1.call-update
  9.6 0.1 copy.27
  9.7 0.1 reshape.26
  9.7 0.1 copy.28
  9.8 0.1 broadcast_in_dim.18
  9.9 0.2 convert_reduce_fusion
  10.1 0.1 select_reduce_fusion
  10.2 0.1 reshape.27
  10.3 4.8 %pack.1 = (bf16[2,3,384,256]{3,2,1,0:T(8,128)(2,1)}, bf16[2,3,384,256]{3,2,1,0:T(8,128)(2,1)}, bf16[2,3,384,256]{3,2,1,0:T(8,128)(2,1)}, bf16[2,3,384,256]{3,2,1,0:T(8,128)(2,1)}) custom-call(bf16[384,2048]{1,0:T(8,128)(2,1)} %query, bf16[384,2048]{1,0:T(8,128)(2,1)} %key, bf16[384,2048]{1,0:T(8,128)(2,1)} %value), custom_call_target="tpu_custom_call" | custom-call | bytes 9437184 | tf_op jit(solution)/shard_map/pack/pallas_call | solution.py:333
  15.1 4.5 %collective-permute-start = (bf16[2,3,384,256]{3,2,1,0:T(8,128)(2,1)}, bf16[2,3,384,256]{3,2,1,0:T(8,128)(2,1)S(1)}, u32[]{:S(2)}, u32[]{:S(2)}) collective-permute-start(bf16[2,3,384,256]{3,2,1,0:T(8,128)(2,1)} %get-tuple-element.29), channel_id=1, source_target_pairs={{0,4},{1,5},{2,6},{3,7},{4,0},{5,1},{6,2},{7,3},{8,12},{9,13},{10,... | collective-permute-start | bytes 3538952 | tf_op jit(solution)/shard_map/ppermute | solution.py:36
  19.6 0.7 collective-permute-start.1
  20.3 1.9 %collective-permute-start.2 = (bf16[2,3,384,256]{3,2,1,0:T(8,128)(2,1)}, bf16[2,3,384,256]{3,2,1,0:T(8,128)(2,1)}, u32[]{:S(2)}, u32[]{:S(2)}) collective-permute-start(bf16[2,3,384,256]{3,2,1,0:T(8,128)(2,1)} %get-tuple-element.31), channel_id=1, source_target_pairs={{0,6},{1,7},{2,0},{3,1},{4,2},{5,3},{6,4},{7,5},{8,14},{9,15},{10,... | collective-permute-start | bytes 3538952 | tf_op jit(solution)/shard_map/ppermute | solution.py:36
  22.3 13.1 %all_to_all.16 = s32[16,1,2]{2,1,0:T(1,128)} all-to-all(s32[16,1,2]{2,1,0:T(1,128)S(1)} %bitcast.9), channel_id=1, replica_groups=mesh['db'=16,'seq'=8] {'db'}, dimensions={0} | all-to-all | bytes 256 | tf_op jit(solution)/shard_map/all_to_all | solution.py:472
  35.3 7.1 %fetch.1 = bf16[32,64,896]{2,1,0:T(8,128)(2,1)} custom-call(s32[16,2]{1,0:T(8,128)} %bitcast.10, bf16[32,64,896]{2,1,0:T(8,128)(2,1)} %database.1), custom_call_target="tpu_custom_call" | custom-call | bytes 7340032 | tf_op jit(solution)/shard_map/fetch/pallas_call | solution.py:77
  42.5 0.0 copy-start.11
  42.5 4.6 %all-to-all-start.1 = ((bf16[32,64,896]{2,1,0:T(8,128)(2,1)}), bf16[32,64,896]{2,1,0:T(8,128)(2,1)}, u32[]{:S(2)}, u32[]{:S(2)}) async-start(bf16[32,64,896]{2,1,0:T(8,128)(2,1)} %fetch.1), calls=%async_computation.1 | async-start | bytes 7340032 | tf_op jit(solution)/shard_map/all_to_all | solution.py:479
  47.2 0.0 collective-permute-done.refs_1_
  47.2 0.0 copy-start.12
  47.2 24.4 %collective-permute-done.1.refs_2_ = bf16[2,3,384,256]{3,2,1,0:T(8,128)(2,1)S(1)} collective-permute-done((bf16[2,3,384,256]{3,2,1,0:T(8,128)(2,1)}, bf16[2,3,384,256]{3,2,1,0:T(8,128)(2,1)S(1)}, u32[]{:S(2)}, u32[]{:S(2)}) %collective-permute-start.1) | collective-permute-done | bytes 1179680 | tf_op jit(solution)/shard_map/ppermute | solution.py:36
  71.6 0.0 collective-permute-done.2.refs_3_
  71.6 0.0 copy-start
  71.6 1.3 collective-permute-start.3
  72.9 0.1 collective-permute-start.4
  73.0 0.4 collective-permute-start.5
  73.4 0.1 collective-permute-start.6
  73.5 1.9 %collective-permute-done.3.refs_4_ = bf16[2,3,384,256]{3,2,1,0:T(8,128)(2,1)S(1)} collective-permute-done((bf16[2,3,384,256]{3,2,1,0:T(8,128)(2,1)S(1)}, bf16[2,3,384,256]{3,2,1,0:T(8,128)(2,1)S(1)}, u32[]{:S(2)}, u32[]{:S(2)}) %collective-permute-start.3) | collective-permute-done | bytes 1179680 | tf_op jit(solution)/shard_map/ppermute | solution.py:36
  75.4 3.4 %collective-permute-done.4.refs_5_ = bf16[2,3,384,256]{3,2,1,0:T(8,128)(2,1)S(1)} collective-permute-done((bf16[2,3,384,256]{3,2,1,0:T(8,128)(2,1)S(1)}, bf16[2,3,384,256]{3,2,1,0:T(8,128)(2,1)S(1)}, u32[]{:S(2)}, u32[]{:S(2)}) %collective-permute-start.4) | collective-permute-done | bytes 1179680 | tf_op jit(solution)/shard_map/ppermute | solution.py:36
  78.7 1.7 collective-permute-done.5.refs_6_
  80.4 1.0 copy-done.16
  81.5 0.0 collective-permute-done.6.refs_7_
  81.5 19.8 %causal.1 = (bf16[2,384,256]{2,1,0:T(8,128)(2,1)}, bf16[2,384,256]{2,1,0:T(8,128)(2,1)}, bf16[2,384,256]{2,1,0:T(8,128)(2,1)}, bf16[2,384,256]{2,1,0:T(8,128)(2,1)}) custom-call(bf16[2,3,384,256]{3,2,1,0:T(8,128)(2,1)} %get-tuple-element.33.refs_0_, bf16[2,3,384,256]{3,2,1,0:T(8,128)(2,1)} %copy-done.12, bf16[2,3,384,256]{3,2,1,0:T(8,128)(2,1)} %copy-done.13, ...), custom_call_target="tpu_custom_call" | custom-call | flops 7000000000 | bytes 8000000 | tf_op jit(solution)/shard_map/causal/pallas_call | solution.py:390
  101.3 1.8 collective-permute-start.7
  103.1 1.4 collective-permute-start.8
  104.5 0.1 collective-permute-start.9
  104.6 3.1 %collective-permute-start.14 = (bf16[64,2048]{1,0:T(8,128)(2,1)S(1)}, bf16[64,2048]{1,0:T(8,128)(2,1)S(1)}, u32[]{:S(2)}, u32[]{:S(2)}) collective-permute-start(bf16[64,2048]{1,0:T(8,128)(2,1)S(1)} %slice.10), channel_id=1, source_target_pairs={{1,0},{2,1},{3,2},{4,3},{5,4},{6,5},{7,6},{9,8},{10,9},{11,10},{12... | collective-permute-start | bytes 786440 | tf_op jit(solution)/shard_map/ppermute | solution.py:480
  107.8 0.1 collective-permute-start.10
  107.9 5.6 %collective-permute-done.7.refs_1_ = bf16[2,384,256]{2,1,0:T(8,128)(2,1)S(1)} collective-permute-done((bf16[2,384,256]{2,1,0:T(8,128)(2,1)}, bf16[2,384,256]{2,1,0:T(8,128)(2,1)S(1)}, u32[]{:S(2)}, u32[]{:S(2)}) %collective-permute-start.7) | collective-permute-done | bytes 393248 | tf_op jit(solution)/shard_map/ppermute | solution.py:36
  113.5 2.0 %collective-permute-start.11 = (bf16[2,384,256]{2,1,0:T(8,128)(2,1)S(1)}, bf16[2,384,256]{2,1,0:T(8,128)(2,1)S(1)}, u32[]{:S(2)}, u32[]{:S(2)}) collective-permute-start(bf16[2,384,256]{2,1,0:T(8,128)(2,1)S(1)} %collective-permute-done.7.refs_1_), channel_id=1, source_target_pairs={{0,1},{1,0},{2,3},{3,2},{4,5},{5,4},{6,7},{7,6},{8,9},{9,8},{10,11... | collective-permute-start | bytes 1179656 | tf_op jit(solution)/shard_map/ppermute | solution.py:36
  115.5 6.5 %collective-permute-done.8.refs_2_ = bf16[2,384,256]{2,1,0:T(8,128)(2,1)S(1)} collective-permute-done((bf16[2,384,256]{2,1,0:T(8,128)(2,1)}, bf16[2,384,256]{2,1,0:T(8,128)(2,1)S(1)}, u32[]{:S(2)}, u32[]{:S(2)}) %collective-permute-start.8) | collective-permute-done | bytes 393248 | tf_op jit(solution)/shard_map/ppermute | solution.py:36
  122.0 1.1 collective-permute-start.12
  123.1 0.0 collective-permute-done.9.refs_3_
  123.1 0.1 collective-permute-start.13
  123.2 0.3 slice.9
  123.5 2.1 %collective-permute-done.14 = bf16[64,2048]{1,0:T(8,128)(2,1)S(1)} collective-permute-done((bf16[64,2048]{1,0:T(8,128)(2,1)S(1)}, bf16[64,2048]{1,0:T(8,128)(2,1)S(1)}, u32[]{:S(2)}, u32[]{:S(2)}) %collective-permute-start.14) | collective-permute-done | bytes 262176 | tf_op jit(solution)/shard_map/ppermute | solution.py:480
  125.6 1.3 pad_maximum_fusion.query
  126.9 0.0 collective-permute-done.10.refs_4_
  126.9 0.0 collective-permute-done.11.refs_5_
  126.9 0.0 collective-permute-done.12.refs_6_
  127.0 0.7 copy-done.4
  127.7 0.2 copy-done.5
  127.8 0.2 copy-done.6
  128.0 0.7 copy-done.7
  128.8 2.8 %unpack.1 = bf16[384,2048]{1,0:T(8,128)(2,1)} custom-call(bf16[2,384,256]{2,1,0:T(8,128)(2,1)} %get-tuple-element.37.refs_0_, bf16[2,384,256]{2,1,0:T(8,128)(2,1)} %copy-done.1, bf16[2,384,256]{2,1,0:T(8,128)(2,1)} %copy-done.2, bf16[2,384,256]{2,1,0:T(8,128)(2,1)} %copy-done.3, bf16[2,384,256]{2,1,0:T(8,128)(2,1)} %copy-done.4, ...), custom_call_target="tpu_custom_call" | custom-call | bytes 3145728 | tf_op jit(solution)/shard_map/unpack/pallas_call | solution.py:424
  131.6 0.0 all-to-all-done.1.arrived
  131.6 0.3 collective-permute-start.15
  131.9 12.1 %encode.1 = (f32[768,896]{1,0:T(8,128)}, bf16[768,896]{1,0:T(8,128)(2,1)}) custom-call(s32[12]{0:T(128)} %copy-done.17, bf16[32,64,896]{2,1,0:T(8,128)(2,1)} %all-to-all-done.1.arrived, bf16[16,352,896]{2,1,0:T(8,128)(2,1)} %bitcast.12), custom_call_target="tpu_custom_call" | custom-call | flops 5000000000 | bytes 12000000 | tf_op jit(solution)/shard_map/encode/pallas_call | solution.py:154
  144.0 3.8 %collective-permute-done.15.other = bf16[16,352,896]{2,1,0:T(8,128)(2,1)} collective-permute-done((bf16[16,352,896]{2,1,0:T(8,128)(2,1)}, bf16[16,352,896]{2,1,0:T(8,128)(2,1)}, u32[]{:S(2)}, u32[]{:S(2)}) %collective-permute-start.15) | collective-permute-done | bytes 10092576 | tf_op jit(solution)/shard_map/ppermute | solution.py:36
  147.8 22.9 %cross.1 = (bf16[384,2048]{1,0:T(8,128)(2,1)}, bf16[64,2048]{1,0:T(8,128)(2,1)}) custom-call(f32[768,896]{1,0:T(8,128)} %get-tuple-element.43.before, bf16[768,896]{1,0:T(8,128)(2,1)} %get-tuple-element.44.normed_in, bf16[16,352,896]{2,1,0:T(8,128)(2,1)} %bitcast.13, bf16[16,352,896]{2,1,0:T(8,128)(2,1)} %collective-permute-done.15.other, ...), custom_call_target="tpu_custom_call" | custom-call | flops 12000000000 | bytes 20000000 | tf_op jit(solution)/shard_map/cross/pallas_call | solution.py:257
  170.7 2.7 %collective-permute-start.16 = (bf16[64,2048]{1,0:T(8,128)(2,1)}, bf16[64,2048]{1,0:T(8,128)(2,1)S(1)}, u32[]{:S(2)}, u32[]{:S(2)}) collective-permute-start(bf16[64,2048]{1,0:T(8,128)(2,1)} %get-tuple-element.47), channel_id=1, source_target_pairs={{0,1},{1,2},{2,3},{3,4},{4,5},{5,6},{6,7},{8,9},{9,10},{10,11},{11... | collective-permute-start | bytes 786440 | tf_op jit(solution)/shard_map/ppermute | solution.py:492
  173.4 3.6 %collective-permute-done.16.before = bf16[64,2048]{1,0:T(8,128)(2,1)S(1)} collective-permute-done((bf16[64,2048]{1,0:T(8,128)(2,1)}, bf16[64,2048]{1,0:T(8,128)(2,1)S(1)}, u32[]{:S(2)}, u32[]{:S(2)}) %collective-permute-start.16) | collective-permute-done | bytes 262176 | tf_op jit(solution)/shard_map/ppermute | solution.py:492
  177.0 0.7 copy-done.8
  177.7 1.8 mend.1
  (31 shorter events, 0.1 us)
Async XLA Ops:
  7.2 2.4 %copy-start.9 = (s32[6,2]{0,1:T(2,128)S(1)}, s32[6,2]{0,1:T(2,128)}, u32[]{:S(2)}) copy-start(s32[6,2]{0,1:T(2,128)} %param.14) | copy-start | bytes 148
  7.2 2.6 %copy-start.10 = (s32[6,2]{0,1:T(2,128)S(1)}, s32[6,2]{0,1:T(2,128)}, u32[]{:S(2)}) copy-start(s32[6,2]{0,1:T(2,128)} %param.15) | copy-start | bytes 148
  7.2 124.4 %all-gather.2.cloned.1.call-start = ((), (), s32[]{:S(2)}) async-start(), calls=%async_computation.2 | async-start | bytes 10723328 | tf_op jit(solution)/shard_map/all_gather | solution.py:468
  10.1 5.0 %copy-start.17 = (s32[12]{0:T(128)}, s32[12]{0:T(128)S(1)}, u32[]{:S(2)}) copy-start(s32[12]{0:T(128)S(1)} %multiply_add_fusion.slot) | copy-start | bytes 148
  15.1 32.1 %collective-permute-start = (bf16[2,3,384,256]{3,2,1,0:T(8,128)(2,1)}, bf16[2,3,384,256]{3,2,1,0:T(8,128)(2,1)S(1)}, u32[]{:S(2)}, u32[]{:S(2)}) collective-permute-start(bf16[2,3,384,256]{3,2,1,0:T(8,128)(2,1)} %get-tuple-element.29), channel_id=1, source_target_pairs={{0,4},{1,5},{2,6},{3,7},{4,0},{5,1},{6,2},{7,3},{8,12},{9,13},{10,... | collective-permute-start | bytes 3538952 | tf_op jit(solution)/shard_map/ppermute | solution.py:36
  19.6 52.0 %collective-permute-start.1 = (bf16[2,3,384,256]{3,2,1,0:T(8,128)(2,1)}, bf16[2,3,384,256]{3,2,1,0:T(8,128)(2,1)S(1)}, u32[]{:S(2)}, u32[]{:S(2)}) collective-permute-start(bf16[2,3,384,256]{3,2,1,0:T(8,128)(2,1)} %get-tuple-element.30), channel_id=1, source_target_pairs={{0,2},{1,3},{2,4},{3,5},{4,6},{5,7},{6,0},{7,1},{8,10},{9,11},{10,... | collective-permute-start | bytes 3538952 | tf_op jit(solution)/shard_map/ppermute | solution.py:36
  20.3 51.3 %collective-permute-start.2 = (bf16[2,3,384,256]{3,2,1,0:T(8,128)(2,1)}, bf16[2,3,384,256]{3,2,1,0:T(8,128)(2,1)}, u32[]{:S(2)}, u32[]{:S(2)}) collective-permute-start(bf16[2,3,384,256]{3,2,1,0:T(8,128)(2,1)} %get-tuple-element.31), channel_id=1, source_target_pairs={{0,6},{1,7},{2,0},{3,1},{4,2},{5,3},{6,4},{7,5},{8,14},{9,15},{10,... | collective-permute-start | bytes 3538952 | tf_op jit(solution)/shard_map/ppermute | solution.py:36
  42.5 29.1 %copy-start.11 = (bf16[2,3,384,256]{3,2,1,0:T(8,128)(2,1)S(1)}, bf16[2,3,384,256]{3,2,1,0:T(8,128)(2,1)}, u32[]{:S(2)}) copy-start(bf16[2,3,384,256]{3,2,1,0:T(8,128)(2,1)} %get-tuple-element.33.refs_0_) | copy-start | bytes 3538948
  42.5 89.1 %all-to-all-start.1 = ((bf16[32,64,896]{2,1,0:T(8,128)(2,1)}), bf16[32,64,896]{2,1,0:T(8,128)(2,1)}, u32[]{:S(2)}, u32[]{:S(2)}) async-start(bf16[32,64,896]{2,1,0:T(8,128)(2,1)} %fetch.1), calls=%async_computation.1 | async-start | bytes 7340032 | tf_op jit(solution)/shard_map/all_to_all | solution.py:479
  47.2 34.3 %copy-start.12 = (bf16[2,3,384,256]{3,2,1,0:T(8,128)(2,1)}, bf16[2,3,384,256]{3,2,1,0:T(8,128)(2,1)S(1)}, u32[]{:S(2)}) copy-start(bf16[2,3,384,256]{3,2,1,0:T(8,128)(2,1)S(1)} %collective-permute-done.refs_1_) | copy-start | bytes 3538948
  71.6 9.9 %copy-start.13 = (bf16[2,3,384,256]{3,2,1,0:T(8,128)(2,1)}, bf16[2,3,384,256]{3,2,1,0:T(8,128)(2,1)S(1)}, u32[]{:S(2)}) copy-start(bf16[2,3,384,256]{3,2,1,0:T(8,128)(2,1)S(1)} %collective-permute-done.1.refs_2_) | copy-start | bytes 3538948
  71.6 33.0 %copy-start = (bf16[384,2048]{1,0:T(8,128)(2,1)S(1)}, bf16[384,2048]{1,0:T(8,128)(2,1)}, u32[]{:S(2)}) copy-start(bf16[384,2048]{1,0:T(8,128)(2,1)} %param.13) | copy-start | bytes 4718596
  71.6 3.7 %collective-permute-start.3 = (bf16[2,3,384,256]{3,2,1,0:T(8,128)(2,1)S(1)}, bf16[2,3,384,256]{3,2,1,0:T(8,128)(2,1)S(1)}, u32[]{:S(2)}, u32[]{:S(2)}) collective-permute-start(bf16[2,3,384,256]{3,2,1,0:T(8,128)(2,1)S(1)} %copy-done.11), channel_id=1, source_target_pairs={{0,1},{1,0},{2,3},{3,2},{4,5},{5,4},{6,7},{7,6},{8,9},{9,8},{10,11... | collective-permute-start | bytes 3538952 | tf_op jit(solution)/shard_map/ppermute | solution.py:36
  72.9 5.8 %collective-permute-start.4 = (bf16[2,3,384,256]{3,2,1,0:T(8,128)(2,1)S(1)}, bf16[2,3,384,256]{3,2,1,0:T(8,128)(2,1)S(1)}, u32[]{:S(2)}, u32[]{:S(2)}) collective-permute-start(bf16[2,3,384,256]{3,2,1,0:T(8,128)(2,1)S(1)} %collective-permute-done.refs_1_), channel_id=1, source_target_pairs={{0,1},{1,0},{2,3},{3,2},{4,5},{5,4},{6,7},{7,6},{8,9},{9,8},{10,11... | collective-permute-start | bytes 3538952 | tf_op jit(solution)/shard_map/ppermute | solution.py:36
  73.0 7.5 %collective-permute-start.5 = (bf16[2,3,384,256]{3,2,1,0:T(8,128)(2,1)S(1)}, bf16[2,3,384,256]{3,2,1,0:T(8,128)(2,1)S(1)}, u32[]{:S(2)}, u32[]{:S(2)}) collective-permute-start(bf16[2,3,384,256]{3,2,1,0:T(8,128)(2,1)S(1)} %collective-permute-done.1.refs_2_), channel_id=1, source_target_pairs={{0,1},{1,0},{2,3},{3,2},{4,5},{5,4},{6,7},{7,6},{8,9},{9,8},{10,11... | collective-permute-start | bytes 3538952 | tf_op jit(solution)/shard_map/ppermute | solution.py:36
  73.4 8.1 %collective-permute-start.6 = (bf16[2,3,384,256]{3,2,1,0:T(8,128)(2,1)}, bf16[2,3,384,256]{3,2,1,0:T(8,128)(2,1)}, u32[]{:S(2)}, u32[]{:S(2)}) collective-permute-start(bf16[2,3,384,256]{3,2,1,0:T(8,128)(2,1)} %collective-permute-done.2.refs_3_), channel_id=1, source_target_pairs={{0,1},{1,0},{2,3},{3,2},{4,5},{5,4},{6,7},{7,6},{8,9},{9,8},{10,11... | collective-permute-start | bytes 3538952 | tf_op jit(solution)/shard_map/ppermute | solution.py:36
  75.4 6.1 %copy-start.14 = (bf16[2,3,384,256]{3,2,1,0:T(8,128)(2,1)}, bf16[2,3,384,256]{3,2,1,0:T(8,128)(2,1)S(1)}, u32[]{:S(2)}) copy-start(bf16[2,3,384,256]{3,2,1,0:T(8,128)(2,1)S(1)} %collective-permute-done.3.refs_4_) | copy-start | bytes 3538948
  78.7 2.7 %copy-start.15 = (bf16[2,3,384,256]{3,2,1,0:T(8,128)(2,1)}, bf16[2,3,384,256]{3,2,1,0:T(8,128)(2,1)S(1)}, u32[]{:S(2)}) copy-start(bf16[2,3,384,256]{3,2,1,0:T(8,128)(2,1)S(1)} %collective-permute-done.4.refs_5_) | copy-start | bytes 3538948
  80.4 1.0 copy-start.16
  101.3 12.2 %collective-permute-start.7 = (bf16[2,384,256]{2,1,0:T(8,128)(2,1)}, bf16[2,384,256]{2,1,0:T(8,128)(2,1)S(1)}, u32[]{:S(2)}, u32[]{:S(2)}) collective-permute-start(bf16[2,384,256]{2,1,0:T(8,128)(2,1)} %get-tuple-element.38), channel_id=1, source_target_pairs={{0,4},{1,5},{2,6},{3,7},{4,0},{5,1},{6,2},{7,3},{8,12},{9,13},{10,... | collective-permute-start | bytes 1179656 | tf_op jit(solution)/shard_map/ppermute | solution.py:36
  103.1 18.8 %collective-permute-start.8 = (bf16[2,384,256]{2,1,0:T(8,128)(2,1)}, bf16[2,384,256]{2,1,0:T(8,128)(2,1)S(1)}, u32[]{:S(2)}, u32[]{:S(2)}) collective-permute-start(bf16[2,384,256]{2,1,0:T(8,128)(2,1)} %get-tuple-element.39), channel_id=1, source_target_pairs={{0,6},{1,7},{2,0},{3,1},{4,2},{5,3},{6,4},{7,5},{8,14},{9,15},{10,... | collective-permute-start | bytes 1179656 | tf_op jit(solution)/shard_map/ppermute | solution.py:36
  104.5 18.6 %collective-permute-start.9 = (bf16[2,384,256]{2,1,0:T(8,128)(2,1)}, bf16[2,384,256]{2,1,0:T(8,128)(2,1)S(1)}, u32[]{:S(2)}, u32[]{:S(2)}) collective-permute-start(bf16[2,384,256]{2,1,0:T(8,128)(2,1)} %get-tuple-element.40), channel_id=1, source_target_pairs={{0,2},{1,3},{2,4},{3,5},{4,6},{5,7},{6,0},{7,1},{8,10},{9,11},{10,... | collective-permute-start | bytes 1179656 | tf_op jit(solution)/shard_map/ppermute | solution.py:36
  104.6 21.0 %collective-permute-start.14 = (bf16[64,2048]{1,0:T(8,128)(2,1)S(1)}, bf16[64,2048]{1,0:T(8,128)(2,1)S(1)}, u32[]{:S(2)}, u32[]{:S(2)}) collective-permute-start(bf16[64,2048]{1,0:T(8,128)(2,1)S(1)} %slice.10), channel_id=1, source_target_pairs={{1,0},{2,1},{3,2},{4,3},{5,4},{6,5},{7,6},{9,8},{10,9},{11,10},{12... | collective-permute-start | bytes 786440 | tf_op jit(solution)/shard_map/ppermute | solution.py:480
  107.8 19.1 %collective-permute-start.10 = (bf16[2,384,256]{2,1,0:T(8,128)(2,1)}, bf16[2,384,256]{2,1,0:T(8,128)(2,1)S(1)}, u32[]{:S(2)}, u32[]{:S(2)}) collective-permute-start(bf16[2,384,256]{2,1,0:T(8,128)(2,1)} %get-tuple-element.37.refs_0_), channel_id=1, source_target_pairs={{0,1},{1,0},{2,3},{3,2},{4,5},{5,4},{6,7},{7,6},{8,9},{9,8},{10,11... | collective-permute-start | bytes 1179656 | tf_op jit(solution)/shard_map/ppermute | solution.py:36
  113.5 13.4 %copy-start.1 = (bf16[2,384,256]{2,1,0:T(8,128)(2,1)}, bf16[2,384,256]{2,1,0:T(8,128)(2,1)S(1)}, u32[]{:S(2)}) copy-start(bf16[2,384,256]{2,1,0:T(8,128)(2,1)S(1)} %collective-permute-done.7.refs_1_) | copy-start | bytes 1179652
  113.5 13.4 %collective-permute-start.11 = (bf16[2,384,256]{2,1,0:T(8,128)(2,1)S(1)}, bf16[2,384,256]{2,1,0:T(8,128)(2,1)S(1)}, u32[]{:S(2)}, u32[]{:S(2)}) collective-permute-start(bf16[2,384,256]{2,1,0:T(8,128)(2,1)S(1)} %collective-permute-done.7.refs_1_), channel_id=1, source_target_pairs={{0,1},{1,0},{2,3},{3,2},{4,5},{5,4},{6,7},{7,6},{8,9},{9,8},{10,11... | collective-permute-start | bytes 1179656 | tf_op jit(solution)/shard_map/ppermute | solution.py:36
  122.0 4.9 %copy-start.2 = (bf16[2,384,256]{2,1,0:T(8,128)(2,1)}, bf16[2,384,256]{2,1,0:T(8,128)(2,1)S(1)}, u32[]{:S(2)}) copy-start(bf16[2,384,256]{2,1,0:T(8,128)(2,1)S(1)} %collective-permute-done.8.refs_2_) | copy-start | bytes 1179652
  122.0 5.0 %collective-permute-start.12 = (bf16[2,384,256]{2,1,0:T(8,128)(2,1)S(1)}, bf16[2,384,256]{2,1,0:T(8,128)(2,1)S(1)}, u32[]{:S(2)}, u32[]{:S(2)}) collective-permute-start(bf16[2,384,256]{2,1,0:T(8,128)(2,1)S(1)} %collective-permute-done.8.refs_2_), channel_id=1, source_target_pairs={{0,1},{1,0},{2,3},{3,2},{4,5},{5,4},{6,7},{7,6},{8,9},{9,8},{10,11... | collective-permute-start | bytes 1179656 | tf_op jit(solution)/shard_map/ppermute | solution.py:36
  123.1 3.8 %copy-start.3 = (bf16[2,384,256]{2,1,0:T(8,128)(2,1)}, bf16[2,384,256]{2,1,0:T(8,128)(2,1)S(1)}, u32[]{:S(2)}) copy-start(bf16[2,384,256]{2,1,0:T(8,128)(2,1)S(1)} %collective-permute-done.9.refs_3_) | copy-start | bytes 1179652
  123.1 3.9 %collective-permute-start.13 = (bf16[2,384,256]{2,1,0:T(8,128)(2,1)S(1)}, bf16[2,384,256]{2,1,0:T(8,128)(2,1)S(1)}, u32[]{:S(2)}, u32[]{:S(2)}) collective-permute-start(bf16[2,384,256]{2,1,0:T(8,128)(2,1)S(1)} %collective-permute-done.9.refs_3_), channel_id=1, source_target_pairs={{0,1},{1,0},{2,3},{3,2},{4,5},{5,4},{6,7},{7,6},{8,9},{9,8},{10,11... | collective-permute-start | bytes 1179656 | tf_op jit(solution)/shard_map/ppermute | solution.py:36
  126.9 0.7 copy-start.4
  126.9 0.9 copy-start.5
  126.9 1.1 copy-start.6
  128.0 0.7 copy-start.7
  131.6 16.2 %collective-permute-start.15 = (bf16[16,352,896]{2,1,0:T(8,128)(2,1)}, bf16[16,352,896]{2,1,0:T(8,128)(2,1)}, u32[]{:S(2)}, u32[]{:S(2)}) collective-permute-start(bf16[16,352,896]{2,1,0:T(8,128)(2,1)} %bitcast.11), channel_id=1, source_target_pairs={{0,1},{1,0},{2,3},{3,2},{4,5},{5,4},{6,7},{7,6},{8,9},{9,8},{10,11... | collective-permute-start | bytes 30277640 | tf_op jit(solution)/shard_map/ppermute | solution.py:36
  170.7 6.3 %collective-permute-start.16 = (bf16[64,2048]{1,0:T(8,128)(2,1)}, bf16[64,2048]{1,0:T(8,128)(2,1)S(1)}, u32[]{:S(2)}, u32[]{:S(2)}) collective-permute-start(bf16[64,2048]{1,0:T(8,128)(2,1)} %get-tuple-element.47), channel_id=1, source_target_pairs={{0,1},{1,2},{2,3},{3,4},{4,5},{5,6},{6,7},{8,9},{9,10},{10,11},{11... | collective-permute-start | bytes 786440 | tf_op jit(solution)/shard_map/ppermute | solution.py:492
  177.0 0.7 copy-start.8
Sparse Core Ops, SparseCore 0:
  10.2 121.2 all-gather.1
